TPU v7x, 512 devices: a whole 4x4x16 slice. The times are simulated.
512 devices in a mesh: slab: 32 (over z, core), orb: 16 (over y, x).
Axes of the slice: x: 4, y: 4, z: 16, core: 2. Of those that a mesh axis runs over, the one named last changes fastest.
Arguments:
- diag_even: float32 [64, 2, 512, 512], P('slab', None, 'orb'), may hold values from -1.3 to 10
- odd_green: float32 [64, 2, 512, 512], P('slab', None, 'orb'), may hold values from -0.3 to 0.45
- lower: float32 [128, 2, 512, 512], P('slab', None, 'orb'), may hold values from -1.8 to 1.8
- upper: float32 [128, 2, 512, 512], P('slab', None, 'orb'), may hold values from -1.8 to 1.8
Outputs:
- final_diag: float32 [32, 2, 512, 512], P('slab', None, 'orb')
- final_lower: float32 [32, 2, 512, 512], P('slab', None, 'orb')
- final_upper: float32 [32, 2, 512, 512], P('slab', None, 'orb')
All inputs are finite; a program needn't handle non-finite values.
Results may differ from a plain program's by a relative error of at most 0.00012.
Values sent between devices are 32-bit elements; how exact they have to be, the bound alone decides.
No kernel may reach another device: no remote copies, remote signals or barrier semaphores. Data moves between devices by JAX's collectives and lax.ppermute only.
A program may use at most 64 MiB of HBM per device.

v0:
```python
import jax
import jax.numpy as jnp
from jax import lax
from jax.sharding import PartitionSpec as P


def shifted(value, axis, steps):
    count = lax.axis_size(axis)
    pairs = [(source, (source + steps) % count) for source in range(count)]
    return lax.ppermute(value, axis, pairs)


def matmul_high(first, second):
    return jnp.matmul(first, second, precision=lax.Precision.HIGHEST)


def packed(block):
    return jnp.concatenate([block[..., 0, :, :], block[..., 1, :, :]], -1)


def unpacked(block):
    half = block.shape[-1] // 2
    return jnp.stack([block[..., :half], block[..., half:]], -3)


def product_parts(left_re, left_im, right):
    half = right.shape[-1] // 2
    first = matmul_high(left_re, right)
    second = matmul_high(left_im, right)
    return jnp.concatenate(
        [first[..., :half] - second[..., half:], first[..., half:] + second[..., :half]], -1
    )


def product_packed(left, right):
    inner = right.shape[-2]
    return product_parts(left[..., :inner], left[..., inner:], right)


def combine_kept(diag_block, lower_block, upper_block, left_up, left_down, right_up, right_down):
    new_diag = (
        diag_block - product_packed(lower_block, left_up) - product_packed(upper_block, right_down)
    )
    return (
        new_diag,
        -product_packed(lower_block, left_down),
        -product_packed(upper_block, right_up),
    )


def shards(diag_even, odd_green, lower, upper):
    rows = lower.shape[2]
    orbitals = lower.shape[3]
    offset_rows = lax.axis_index("orb") * rows
    green = packed(odd_green)
    green_re = green[..., :orbitals]
    green_im = green[..., orbitals:]
    pieces = (
        lax.all_gather(packed(upper[1::2]), "orb", axis=1, tiled=True),
        lax.all_gather(packed(lower[1::2]), "orb", axis=1, tiled=True),
    )
    cols_re = green_re
    cols_im = green_im
    up_odd = product_parts(cols_re, cols_im, pieces[0])
    down_odd = product_parts(cols_re, cols_im, pieces[1])
    full_up, full_down = (
        lax.all_gather(up_odd, "orb", axis=1, tiled=True),
        lax.all_gather(down_odd, "orb", axis=1, tiled=True),
    )
    far_up, far_down = shifted((full_up[1], full_down[1]), "slab", 1)
    left_up = jnp.stack([far_up, full_up[0]])
    left_down = jnp.stack([far_down, full_down[0]])
    new_diag, new_lower, new_upper = combine_kept(
        packed(diag_even),
        packed(lower[0::2]),
        packed(upper[0::2]),
        left_up,
        left_down,
        full_up,
        full_down,
    )
    pivot = new_diag[1]
    pivot_re = pivot[:, :orbitals]
    pivot_im = pivot[:, orbitals:]
    column_iota = lax.broadcasted_iota(jnp.int32, (rows, orbitals), 1)
    row_iota = lax.broadcasted_iota(jnp.int32, (rows, orbitals), 0) + offset_rows
    on_diagonal = column_iota == row_iota
    diag_re = jnp.sum(jnp.where(on_diagonal, pivot_re, 0.0), axis=1)
    diag_im = jnp.sum(jnp.where(on_diagonal, pivot_im, 0.0), axis=1)
    modulus = diag_re * diag_re + diag_im * diag_im
    weight_re = diag_re / modulus
    weight_im = -diag_im / modulus
    whole_weights = lax.all_gather(jnp.stack([weight_re, weight_im]), "orb", axis=1, tiled=True)
    column_re = whole_weights[0][None, :]
    column_im = whole_weights[1][None, :]
    inner_re = weight_re[:, None] * pivot_re - weight_im[:, None] * pivot_im
    inner_im = weight_re[:, None] * pivot_im + weight_im[:, None] * pivot_re
    outer_re = inner_re * column_re - inner_im * column_im
    outer_im = inner_re * column_im + inner_im * column_re
    first_re = jnp.where(on_diagonal, 2.0 * weight_re[:, None], 0.0) - outer_re
    first_im = jnp.where(on_diagonal, 2.0 * weight_im[:, None], 0.0) - outer_im
    estimate = jnp.concatenate([first_re, first_im], -1)
    estimate_whole = lax.all_gather(estimate, "orb", axis=0, tiled=True)
    image = product_packed(pivot, estimate_whole)
    image_whole = lax.all_gather(image, "orb", axis=0, tiled=True)
    inverse = 2.0 * estimate - product_packed(estimate, image_whole)
    inverse_re = inverse[:, :orbitals]
    inverse_im = inverse[:, orbitals:]
    pieces = (
        lax.all_gather(new_upper[1], "orb", axis=0, tiled=True),
        lax.all_gather(new_lower[1], "orb", axis=0, tiled=True),
    )
    cols_re = inverse_re
    cols_im = inverse_im
    up_two = product_parts(cols_re, cols_im, pieces[0])
    down_two = product_parts(cols_re, cols_im, pieces[1])
    whole_up, whole_down = (
        lax.all_gather(up_two, "orb", axis=0, tiled=True),
        lax.all_gather(down_two, "orb", axis=0, tiled=True),
    )
    prior_up, prior_down = shifted((whole_up, whole_down), "slab", 1)
    final_diag, final_lower, final_upper = combine_kept(
        new_diag[0], new_lower[0], new_upper[0], prior_up, prior_down, whole_up, whole_down
    )
    return (unpacked(final_diag)[None], unpacked(final_lower)[None], unpacked(final_upper)[None])


def solution(mesh):
    return jax.shard_map(
        shards,
        mesh=mesh,
        in_specs=(
            P("slab", None, "orb", None),
            P("slab", None, "orb", None),
            P("slab", None, "orb", None),
            P("slab", None, "orb", None),
        ),
        out_specs=(
            P("slab", None, "orb", None),
            P("slab", None, "orb", None),
            P("slab", None, "orb", None),
        ),
        check_vma=False,
    )
```

profile of v0, /device:TPU:2, one launch (start us, length us, event | category | flops | bytes accessed | tf_op | source)
XLA Modules:
  0.0 745.8 jit_solution(8523353317845544824)
XLA Ops:
  7.2 1.1 fusion.57
  8.4 0.7 pad_maximum_fusion.14
  9.3 0.7 pad_maximum_fusion.16
  10.1 72.4 %all-gather.14.cloned.1.call-done = f32[2,512,1024]{2,1,0:T(8,128)} async-done(((f32[2,32,1024]{2,1,0:T(8,128)}), f32[2,512,1024]{2,1,0:T(8,128)}) %all-gather.14.cloned.1.call-update) | async-done | bytes 4194320 | tf_op jit(solution)/shard_map/all_gather | solution.py:59
  82.4 4.9 convolution_bitcast_fusion.6
  87.3 2.6 convolution_bitcast_fusion.7
  90.0 0.7 pad_maximum_fusion.15
  90.8 61.4 %all-gather.18.cloned.1.call-done = f32[2,512,1024]{2,1,0:T(8,128)} async-done(((f32[2,32,1024]{2,1,0:T(8,128)}), f32[2,512,1024]{2,1,0:T(8,128)}) %all-gather.18.cloned.1.call-update) | async-done | bytes 4194320 | tf_op jit(solution)/shard_map/all_gather | solution.py:60
  152.2 4.9 convolution_bitcast_fusion.4
  157.1 2.6 convolution_bitcast_fusion.5
  159.7 0.7 pad_maximum_fusion.17
  161.0 60.9 %all-gather.16.cloned.1.call-done = f32[2,512,1024]{2,1,0:T(8,128)} async-done(((f32[2,32,1024]{2,1,0:T(8,128)}), f32[2,512,1024]{2,1,0:T(8,128)}) %all-gather.16.cloned.1.call-update) | async-done | bytes 4194320 | tf_op jit(solution)/shard_map/all_gather | solution.py:67
  221.9 4.0 slice_bitcast_fusion.1
  226.0 65.5 %all-gather.20.cloned.1.call-done = f32[2,512,1024]{2,1,0:T(8,128)} async-done(((f32[2,32,1024]{2,1,0:T(8,128)}), f32[2,512,1024]{2,1,0:T(8,128)}) %all-gather.20.cloned.1.call-update) | async-done | bytes 4194320 | tf_op jit(solution)/shard_map/all_gather | solution.py:68
  291.5 4.9 convolution_bitcast_fusion.2
  296.4 2.6 convolution_bitcast_fusion.3
  299.0 4.2 fusion.12
  303.2 4.2 fusion.13
  307.7 21.1 %all-gather.2 = f32[16,32,2]{1,2,0:T(2,128)S(1)} all-gather(f32[1,32,2]{1,2,0:T(2,128)S(1)} %maximum_bitcast_fusion.3), channel_id=1, replica_groups=mesh['slab'=32,'orb'=16] {'orb'}, dimensions={0}, use_global_device_ids=true | all-gather | bytes 4352 | tf_op jit(solution)/shard_map/all_gather | solution.py:93
  330.0 60.3 %all-gather.22.cloned.1.call-done = f32[512,1024]{1,0:T(8,128)} async-done(((f32[32,1024]{1,0:T(8,128)}), f32[512,1024]{1,0:T(8,128)}) %all-gather.22.cloned.1.call-update) | async-done | bytes 2097168 | tf_op jit(solution)/shard_map/all_gather | solution.py:103
  390.2 3.0 fusion.49
  393.3 1.3 fusion.47
  395.3 2.5 slice_bitcast_fusion
  397.9 26.7 %collective-permute-done.1 = f32[512,1024]{1,0:T(8,128)S(1)} collective-permute-done((f32[512,1024]{1,0:T(8,128)S(1)}, f32[512,1024]{1,0:T(8,128)S(1)}, u32[]{:S(2)}, u32[]{:S(2)}) %collective-permute-start.1) | collective-permute-done | bytes 2097184 | tf_op jit(solution)/shard_map/ppermute | solution.py:10
  424.6 2.6 fusion.14
  427.2 2.6 fusion.15
  430.6 4.9 convolution_bitcast_fusion
  435.5 2.6 convolution_bitcast_fusion.1
  439.1 16.0 %all-gather.24.cloned.1.call-done = f32[512,1024]{1,0:T(8,128)} async-done(((f32[32,1024]{1,0:T(8,128)}), f32[512,1024]{1,0:T(8,128)}) %all-gather.24.cloned.1.call-update) | async-done | bytes 2097168 | tf_op jit(solution)/shard_map/all_gather | solution.py:105
  455.1 3.0 fusion.61
  458.2 1.3 fusion.62
  459.5 58.9 %all-gather.32.cloned.1.call-done = f32[1,512,1024]{2,1,0:T(8,128)} async-done(((f32[1,32,1024]{2,1,0:T(8,128)}), f32[1,512,1024]{2,1,0:T(8,128)}) %all-gather.32.cloned.1.call-update) | async-done | bytes 2097168 | tf_op jit(solution)/shard_map/all_gather | solution.py:111
  518.5 3.0 fusion.6
  521.5 1.3 fusion.4
  523.6 58.2 %all-gather.30.cloned.1.call-done = f32[1,512,1024]{2,1,0:T(8,128)} async-done(((f32[1,32,1024]{2,1,0:T(8,128)}), f32[1,512,1024]{2,1,0:T(8,128)}) %all-gather.30.cloned.1.call-update) | async-done | bytes 2097168 | tf_op jit(solution)/shard_map/all_gather | solution.py:110
  581.8 3.0 fusion.10
  584.8 1.3 fusion.8
  586.9 58.3 %all-gather.28.cloned.1.call-done = f32[512,1024]{1,0:T(8,128)} async-done(((f32[32,1024]{1,0:T(8,128)}), f32[512,1024]{1,0:T(8,128)}) %all-gather.28.cloned.1.call-update) | async-done | bytes 2097168 | tf_op jit(solution)/shard_map/all_gather | solution.py:119
  645.1 63.2 %all-gather.26.cloned.1.call-done = f32[512,1024]{1,0:T(8,128)} async-done(((f32[32,1024]{1,0:T(8,128)}), f32[512,1024]{1,0:T(8,128)}) %all-gather.26.cloned.1.call-update) | async-done | bytes 2097168 | tf_op jit(solution)/shard_map/all_gather | solution.py:118
  708.3 3.0 fusion.27
  711.4 1.3 fusion.31
  713.4 1.3 fusion.33
  714.7 1.3 fusion.29
  716.0 1.3 fusion.43
  717.3 1.3 fusion.35
  718.7 16.5 %collective-permute-done.2 = f32[512,1024]{1,0:T(8,128)S(1)} collective-permute-done((f32[512,1024]{1,0:T(8,128)}, f32[512,1024]{1,0:T(8,128)S(1)}, u32[]{:S(2)}, u32[]{:S(2)}) %collective-permute-start.2) | collective-permute-done | bytes 2097184 | tf_op jit(solution)/shard_map/ppermute | solution.py:10
  735.2 1.3 fusion.45
  736.5 1.3 fusion.37
  (98 shorter events, 8.0 us)
Async XLA Ops:
  7.2 2.0 copy-start.11
  7.2 75.3 %all-gather.14.cloned.1.call-start = ((), (), s32[]{:S(2)}) async-start(), calls=%async_computation | async-start | bytes 4456448 | tf_op jit(solution)/shard_map/all_gather | solution.py:59
  8.4 74.1 %copy-start.10 = (f32[2,2,32,512]{3,2,1,0:T(8,128)S(1)}, f32[2,2,32,512]{3,2,1,0:T(8,128)}, u32[]{:S(2)}) copy-start(f32[2,2,32,512]{3,2,1,0:T(8,128)} %param.5) | copy-start | bytes 786436
  9.1 143.0 %all-gather.18.cloned.1.call-start = ((), (), s32[]{:S(2)}) async-start(), calls=%async_computation.2 | async-start | bytes 4456448 | tf_op jit(solution)/shard_map/all_gather | solution.py:60
  10.0 211.9 %all-gather.16.cloned.1.call-start = ((), (), s32[]{:S(2)}) async-start(), calls=%async_computation.1 | async-start | bytes 4456448 | tf_op jit(solution)/shard_map/all_gather | solution.py:67
  82.4 4.9 copy-start.3
  90.7 200.8 %all-gather.20.cloned.1.call-start = ((), (), s32[]{:S(2)}) async-start(), calls=%async_computation.3 | async-start | bytes 4456448 | tf_op jit(solution)/shard_map/all_gather | solution.py:68
  152.2 4.9 copy-start.2
  160.5 65.5 %copy-start.12 = (f32[2,2,32,512]{3,2,1,0:T(8,128)S(1)}, f32[2,2,32,512]{3,2,1,0:T(8,128)}, u32[]{:S(2)}) copy-start(f32[2,2,32,512]{3,2,1,0:T(8,128)} %param.4) | copy-start | bytes 786436
  160.5 229.7 %all-gather.22.cloned.1.call-start = ((), (), s32[]{:S(2)}) async-start(), calls=%async_computation.4 | async-start | bytes 2228224 | tf_op jit(solution)/shard_map/all_gather | solution.py:103
  225.9 73.1 %collective-permute-start = (f32[512,1024]{1,0:T(8,128)}, f32[512,1024]{1,0:T(8,128)}, u32[]{:S(2)}, u32[]{:S(2)}) collective-permute-start(f32[512,1024]{1,0:T(8,128)} %get-tuple-element.11), channel_id=1, source_target_pairs={{0,16},{16,32},{32,48},{48,64},{64,80},{80,96},{96,112},{112,128},... | collective-permute-start | bytes 6291464 | tf_op jit(solution)/shard_map/ppermute | solution.py:10
  291.5 4.9 copy-start.1
  329.7 125.4 %all-gather.24.cloned.1.call-start = ((), (), s32[]{:S(2)}) async-start(), calls=%async_computation.5 | async-start | bytes 2228224 | tf_op jit(solution)/shard_map/all_gather | solution.py:105
  390.2 3.0 copy-start.9
  395.3 123.2 %all-gather.32.cloned.1.call-start = ((), (), s32[]{:S(2)}) async-start(), calls=%async_computation.9 | async-start | bytes 2228224 | tf_op jit(solution)/shard_map/all_gather | solution.py:111
  397.9 26.7 %collective-permute-start.1 = (f32[512,1024]{1,0:T(8,128)S(1)}, f32[512,1024]{1,0:T(8,128)S(1)}, u32[]{:S(2)}, u32[]{:S(2)}) collective-permute-start(f32[512,1024]{1,0:T(8,128)S(1)} %get-tuple-element.9), channel_id=1, source_target_pairs={{0,16},{16,32},{32,48},{48,64},{64,80},{80,96},{96,112},{112,128},... | collective-permute-start | bytes 6291464 | tf_op jit(solution)/shard_map/ppermute | solution.py:10
  430.5 151.3 %all-gather.30.cloned.1.call-start = ((), (), s32[]{:S(2)}) async-start(), calls=%async_computation.8 | async-start | bytes 2228224 | tf_op jit(solution)/shard_map/all_gather | solution.py:110
  430.6 4.9 copy-start
  438.9 206.3 %all-gather.28.cloned.1.call-start = ((), (), s32[]{:S(2)}) async-start(), calls=%async_computation.7 | async-start | bytes 2228224 | tf_op jit(solution)/shard_map/all_gather | solution.py:119
  455.1 3.0 copy-start.4
  518.5 3.0 copy-start.7
  523.5 184.8 %all-gather.26.cloned.1.call-start = ((), (), s32[]{:S(2)}) async-start(), calls=%async_computation.6 | async-start | bytes 2228224 | tf_op jit(solution)/shard_map/all_gather | solution.py:118
  581.8 3.0 copy-start.8
  645.1 70.9 %collective-permute-start.3 = (f32[512,1024]{1,0:T(8,128)}, f32[512,1024]{1,0:T(8,128)S(1)}, u32[]{:S(2)}, u32[]{:S(2)}) collective-permute-start(f32[512,1024]{1,0:T(8,128)} %all-gather.28.cloned.1.call-done), channel_id=1, source_target_pairs={{0,16},{16,32},{32,48},{48,64},{64,80},{80,96},{96,112},{112,128},... | collective-permute-start | bytes 6291464 | tf_op jit(solution)/shard_map/ppermute | solution.py:10
  708.3 3.0 copy-start.6
  708.3 26.9 %collective-permute-start.2 = (f32[512,1024]{1,0:T(8,128)}, f32[512,1024]{1,0:T(8,128)S(1)}, u32[]{:S(2)}, u32[]{:S(2)}) collective-permute-start(f32[512,1024]{1,0:T(8,128)} %all-gather.26.cloned.1.call-done), channel_id=1, source_target_pairs={{0,16},{16,32},{32,48},{48,64},{64,80},{80,96},{96,112},{112,128},... | collective-permute-start | bytes 6291464 | tf_op jit(solution)/shard_map/ppermute | solution.py:10
  711.3 2.0 copy-start.5
Sparse Core Ops, SparseCore 0:
  11.0 71.3 all-gather.13
  85.4 66.6 all-gather.17
  155.2 66.6 all-gather.15
  224.8 66.6 all-gather.19
  329.9 60.3 all-gather.21
  395.4 59.6 all-gather.23
  458.7 59.6 all-gather.31
  522.1 59.6 all-gather.29
  585.4 59.6 all-gather.27
  648.6 59.6 all-gather.25
where the time goes:
time: 753 us; the launch traced here: 746 us
  waiting for transfers between devices  618 us (82%)
  matrix products  72.8 us (10%)
  blocking collectives  21.1 us (3%)
  between operations  15.1 us (2%)
  local copies, waits for them, and re-layouts  9.27 us (1%)
  other arithmetic  7.81 us (1%)
    dot_general x28, matrix products, matmul_high(): return jnp.matmul(first, second, precision=lax.Precision.HIGHEST)  72.8 us
    all_gather x1, waiting for transfers between devices, shards(): lax.all_gather(packed(upper[1::2]), 'orb', axis=1, tiled=True)  72.4 us
    all_gather x1, waiting for transfers between devices, shards(): lax.all_gather(down_odd, 'orb', axis=1, tiled=True)  65.5 us
    all_gather x1, waiting for transfers between devices, shards(): lax.all_gather(up_two, 'orb', axis=0, tiled=True)  63.2 us
    all_gather x1, waiting for transfers between devices, shards(): lax.all_gather(packed(lower[1::2]), 'orb', axis=1, tiled=True)  61.4 us
    all_gather x1, waiting for transfers between devices, shards(): lax.all_gather(up_odd, 'orb', axis=1, tiled=True)  60.9 us
    all_gather x1, waiting for transfers between devices, shards(): estimate_whole = lax.all_gather(estimate, 'orb', axis=0, tiled=True)  60.3 us
    all_gather x1, waiting for transfers between devices, shards(): lax.all_gather(new_lower[1], 'orb', axis=0, tiled=True)  58.9 us
  transfers between devices with their start and end apart: 14, of which 12 were waited for; matrix products, arithmetic and copies ran while one was open for 9% of the time, Pallas kernels for 0%

commit v1 on v0

v1 whole, which is shorter than its diff:
```python
import jax
import jax.numpy as jnp
from jax import lax
from jax.sharding import PartitionSpec as P

SIDE = 4


def shifted(value, axis, steps):
    count = lax.axis_size(axis)
    pairs = [(source, (source + steps) % count) for source in range(count)]
    return lax.ppermute(value, axis, pairs)


def orb_shift(value, dy, dx):
    pairs = []
    for y in range(SIDE):
        for x in range(SIDE):
            pairs.append((y * SIDE + x, ((y + dy) % SIDE) * SIDE + (x + dx) % SIDE))
    return lax.ppermute(value, "orb", pairs)


def gathered_by_permutes(value):
    index = lax.axis_index("orb")
    place_y = index // SIDE
    place_x = index % SIDE
    along_x = [value] + [orb_shift(value, 0, step) for step in range(1, SIDE)]
    line = jnp.stack(along_x[::-1] + along_x[::-1])
    line = lax.dynamic_slice_in_dim(line, SIDE - 1 - place_x, SIDE, 0)
    along_y = [line] + [orb_shift(line, step, 0) for step in range(1, SIDE)]
    plane = jnp.stack(along_y[::-1] + along_y[::-1])
    plane = lax.dynamic_slice_in_dim(plane, SIDE - 1 - place_y, SIDE, 0)
    return plane.reshape(SIDE * SIDE * value.shape[0], value.shape[1])


def packed(block):
    return jnp.concatenate([block[..., 0, :, :], block[..., 1, :, :]], -1)


def unpacked(block):
    half = block.shape[-1] // 2
    return jnp.stack([block[..., :half], block[..., half:]], -3)


def product(left, right):
    rows = left.shape[1]
    half = right.shape[-1] // 2
    both = jnp.matmul(left.reshape(2 * rows, left.shape[2]), right, precision=lax.Precision.HIGH)
    real = both[:rows, :half] - both[rows:, half:]
    imag = both[:rows, half:] + both[rows:, :half]
    return jnp.stack([real, imag])


def scaled(value, weight_re, weight_im):
    return jnp.stack(
        [value[0] * weight_re - value[1] * weight_im, value[0] * weight_im + value[1] * weight_re]
    )


def shards(diag_even, odd_green, lower, upper):
    rows = lower.shape[2]
    orbitals = lower.shape[3]
    wide = 2 * orbitals
    next_lower = shifted(lower[0], "slab", -1)
    mine = jnp.concatenate([packed(odd_green), packed(lower[1::2]), packed(upper[1::2])])
    whole = lax.all_gather(mine, "orb", axis=1, tiled=True)
    left_rows = (
        jnp.concatenate([upper[0], lower[2]], 1),
        jnp.concatenate([upper[2], next_lower], 1),
    )
    parts = []
    for odd in range(2):
        middle = product(left_rows[odd], whole[odd])
        parts.append((product(middle, whole[2 + odd]), product(middle, whole[4 + odd])))
    (first_down, first_up), (second_down, second_up) = parts
    kept_diag = diag_even[0] - first_down[:, :rows]
    kept_upper = -first_up[:, :rows]
    pivot_diag = diag_even[1] - first_up[:, rows:] - second_down[:, :rows]
    pivot_lower = -first_down[:, rows:]
    pivot_upper = -second_up[:, :rows]
    next_part = -second_up[:, rows:]
    next_kept_lower = -second_down[:, rows:]

    mine_two = jnp.concatenate([packed(pivot_diag), packed(pivot_lower), packed(pivot_upper)], -1)
    whole_two = gathered_by_permutes(mine_two)
    pivot = whole_two[:, :wide]
    on_diagonal = jnp.eye(orbitals, dtype=bool)
    diag_re = jnp.sum(jnp.where(on_diagonal, pivot[:, :orbitals], 0.0), axis=0)
    diag_im = jnp.sum(jnp.where(on_diagonal, pivot[:, orbitals:], 0.0), axis=0)
    modulus = diag_re * diag_re + diag_im * diag_im
    weight_re = (diag_re / modulus)[None, :]
    weight_im = (-diag_im / modulus)[None, :]

    def times_first(value):
        value = scaled(value, weight_re, weight_im)
        return 2.0 * value - scaled(product(value, pivot), weight_re, weight_im)

    chain = jnp.concatenate([kept_upper, next_kept_lower], 1)
    estimate = times_first(chain)
    solved = 2.0 * estimate - times_first(product(estimate, pivot))
    with_lower = product(solved, whole_two[:, wide : 2 * wide])
    with_upper = product(solved, whole_two[:, 2 * wide :])
    sent = jnp.stack([next_part - with_upper[:, rows:], -with_lower[:, rows:]])
    came = shifted(sent, "slab", 1)
    final_diag = kept_diag - with_lower[:, :rows] + came[0]
    final_upper = -with_upper[:, :rows]
    return final_diag[None], came[1][None], final_upper[None]


def solution(mesh):
    spec = P("slab", None, "orb", None)
    return jax.shard_map(
        shards, mesh=mesh, in_specs=(spec,) * 4, out_specs=(spec,) * 3, check_vma=False
    )
```

time: 753 us -> 269 us (0.36)
  the two profiles are of different devices: /device:TPU:2 before, /device:TPU:4 now
where the time goes in v1:
time: 269 us; the launch traced here: 268 us
  waiting for transfers between devices  186 us (69%)
  starting transfers between devices  27.4 us (10%)
  matrix products  18.1 us (7%)
  local copies, waits for them, and re-layouts  17.6 us (7%)
  between operations  14.8 us (6%)
  other arithmetic  4 us (1%)
    all_gather x1, waiting for transfers between devices, shards(): whole = lax.all_gather(mine, 'orb', axis=1, tiled=True)  98.3 us
    ppermute x6, waiting for transfers between devices, orb_shift(): return lax.ppermute(value, 'orb', pairs)  77.6 us
    ppermute x6, starting transfers between devices, orb_shift(): return lax.ppermute(value, 'orb', pairs)  18.4 us
    dot_general x11, matrix products, product(): jnp.matmul(left.reshape(2 * rows, left.shape[2]), right, precision=lax.Pr...  18.1 us
    unnamed x47, local copies, waits for them, and re-layouts  11.6 us
    ppermute x2, waiting for transfers between devices, shifted(): return lax.ppermute(value, axis, pairs)  10.2 us
    ppermute x2, starting transfers between devices, shifted(): return lax.ppermute(value, axis, pairs)  8.98 us
  transfers between devices with their start and end apart: 9, of which 8 were waited for; matrix products, arithmetic and copies ran while one was open for 2% of the time, Pallas kernels for 0%

profile of v1, /device:TPU:4, one launch (start us, length us, event | category | flops | bytes accessed | tf_op | source)
XLA Modules:
  0.0 268.0 jit_solution(12133151997825452704)
XLA Ops:
  7.2 1.0 slice.282
  8.3 1.0 slice.285
  9.3 1.0 slice_bitcast_fusion.14
  10.3 1.0 maximum_maximum_fusion
  11.3 8.9 %collective-permute-start = (f32[2,32,512]{2,1,0:T(8,128)S(1)}, f32[2,32,512]{2,1,0:T(8,128)S(1)}, u32[]{:S(2)}, u32[]{:S(2)}) collective-permute-start(f32[2,32,512]{2,1,0:T(8,128)S(1)} %get-tuple-element.26), channel_id=1, source_target_pairs={{0,496},{16,0},{32,16},{48,32},{64,48},{80,64},{96,80},{112,96},{1... | collective-permute-start | bytes 393224 | tf_op jit(solution)/shard_map/ppermute | solution.py:12
  20.3 2.5 collective-permute-done
  22.8 98.3 %all-gather.2.cloned.1.call-done = f32[6,512,1024]{2,1,0:T(8,128)} async-done(((f32[6,32,1024]{2,1,0:T(8,128)}), f32[6,512,1024]{2,1,0:T(8,128)}) %all-gather.2.cloned.1.call-update) | async-done | bytes 12582928 | tf_op jit(solution)/shard_map/all_gather | solution.py:66
  121.2 2.3 fusion.6
  123.5 2.3 fusion.9
  125.9 2.3 fusion.7
  128.3 2.3 fusion.8
  130.7 2.4 fusion.5
  133.2 2.3 fusion.4
  135.6 0.8 fusion.32
  136.5 2.5 collective-permute-start.1
  139.0 3.4 %collective-permute-start.3 = (f32[32,3072]{1,0:T(8,128)S(1)}, f32[32,3072]{1,0:T(8,128)S(1)}, u32[]{:S(2)}, u32[]{:S(2)}) collective-permute-start(f32[32,3072]{1,0:T(8,128)S(1)} %fusion.59), channel_id=1, source_target_pairs={{0,1},{1,2},{2,3},{3,0},{4,5},{5,6},{6,7},{7,4},{8,9},{9,10},{10,1... | collective-permute-start | bytes 1179656 | tf_op jit(solution)/shard_map/ppermute | solution.py:20
  142.4 3.1 %collective-permute-start.2 = (f32[32,3072]{1,0:T(8,128)S(1)}, f32[32,3072]{1,0:T(8,128)S(1)}, u32[]{:S(2)}, u32[]{:S(2)}) collective-permute-start(f32[32,3072]{1,0:T(8,128)S(1)} %fusion.59), channel_id=1, source_target_pairs={{0,2},{1,3},{2,0},{3,1},{4,6},{5,7},{6,4},{7,5},{8,10},{9,11},{10,... | collective-permute-start | bytes 1179656 | tf_op jit(solution)/shard_map/ppermute | solution.py:20
  145.5 5.0 %collective-permute-done.1 = f32[32,3072]{1,0:T(8,128)} collective-permute-done((f32[32,3072]{1,0:T(8,128)S(1)}, f32[32,3072]{1,0:T(8,128)}, u32[]{:S(2)}, u32[]{:S(2)}) %collective-permute-start.1) | collective-permute-done | bytes 393248 | tf_op jit(solution)/shard_map/ppermute | solution.py:20
  150.5 1.0 bitcast_dynamic-update-slice_fusion.14
  151.5 9.3 %collective-permute-done.2 = f32[32,3072]{1,0:T(8,128)S(1)} collective-permute-done((f32[32,3072]{1,0:T(8,128)S(1)}, f32[32,3072]{1,0:T(8,128)S(1)}, u32[]{:S(2)}, u32[]{:S(2)}) %collective-permute-start.2) | collective-permute-done | bytes 393248 | tf_op jit(solution)/shard_map/ppermute | solution.py:20
  160.9 1.0 bitcast_dynamic-update-slice_fusion.15
  162.1 1.3 constant_dynamic-slice_fusion.1
  163.4 3.7 %collective-permute-start.4 = (f32[4,32,3072]{2,1,0:T(8,128)}, f32[4,32,3072]{2,1,0:T(8,128)}, u32[]{:S(2)}, u32[]{:S(2)}) collective-permute-start(f32[4,32,3072]{2,1,0:T(8,128)} %constant_dynamic-slice_fusion.1), channel_id=1, source_target_pairs={{0,12},{1,13},{2,14},{3,15},{4,0},{5,1},{6,2},{7,3},{8,4},{9,5},{1... | collective-permute-start | bytes 4718600 | tf_op jit(solution)/shard_map/ppermute | solution.py:20
  167.0 2.7 %collective-permute-start.5 = (f32[4,32,3072]{2,1,0:T(8,128)}, f32[4,32,3072]{2,1,0:T(8,128)}, u32[]{:S(2)}, u32[]{:S(2)}) collective-permute-start(f32[4,32,3072]{2,1,0:T(8,128)} %constant_dynamic-slice_fusion.1), channel_id=1, source_target_pairs={{0,8},{1,9},{2,10},{3,11},{4,12},{5,13},{6,14},{7,15},{8,0},{9,1},... | collective-permute-start | bytes 4718600 | tf_op jit(solution)/shard_map/ppermute | solution.py:20
  169.8 3.0 %collective-permute-start.6 = (f32[4,32,3072]{2,1,0:T(8,128)}, f32[4,32,3072]{2,1,0:T(8,128)}, u32[]{:S(2)}, u32[]{:S(2)}) collective-permute-start(f32[4,32,3072]{2,1,0:T(8,128)} %constant_dynamic-slice_fusion.1), channel_id=1, source_target_pairs={{0,4},{1,5},{2,6},{3,7},{4,8},{5,9},{6,10},{7,11},{8,12},{9,13},{1... | collective-permute-start | bytes 4718600 | tf_op jit(solution)/shard_map/ppermute | solution.py:20
  172.8 30.1 %collective-permute-done.4 = f32[4,32,3072]{2,1,0:T(8,128)} collective-permute-done((f32[4,32,3072]{2,1,0:T(8,128)}, f32[4,32,3072]{2,1,0:T(8,128)}, u32[]{:S(2)}, u32[]{:S(2)}) %collective-permute-start.4) | collective-permute-done | bytes 1572896 | tf_op jit(solution)/shard_map/ppermute | solution.py:20
  202.9 1.5 bitcast_dynamic-update-slice_fusion.6
  204.4 3.7 %collective-permute-done.5 = f32[4,32,3072]{2,1,0:T(8,128)} collective-permute-done((f32[4,32,3072]{2,1,0:T(8,128)}, f32[4,32,3072]{2,1,0:T(8,128)}, u32[]{:S(2)}, u32[]{:S(2)}) %collective-permute-start.5) | collective-permute-done | bytes 1572896 | tf_op jit(solution)/shard_map/ppermute | solution.py:20
  208.1 1.5 bitcast_dynamic-update-slice_fusion.4
  209.7 29.5 %collective-permute-done.6 = f32[4,32,3072]{2,1,0:T(8,128)} collective-permute-done((f32[4,32,3072]{2,1,0:T(8,128)}, f32[4,32,3072]{2,1,0:T(8,128)}, u32[]{:S(2)}, u32[]{:S(2)}) %collective-permute-start.6) | collective-permute-done | bytes 1572896 | tf_op jit(solution)/shard_map/ppermute | solution.py:20
  239.1 1.5 bitcast_dynamic-update-slice_fusion.2
  240.7 0.1 bitcast_dynamic-update-slice_fusion
  240.8 1.5 bitcast_dynamic-update-slice_fusion.7
  242.3 1.5 bitcast_dynamic-update-slice_fusion.5
  243.9 1.5 bitcast_dynamic-update-slice_fusion.3
  245.4 0.1 bitcast_dynamic-update-slice_fusion.1
  245.5 0.7 constant_dynamic-slice_fusion
  246.3 0.1 fusion.17
  246.6 0.8 fusion.14
  247.5 0.8 fusion.12
  248.5 0.8 fusion.10
  249.4 0.1 fusion.18
  249.5 0.8 fusion
  250.4 0.8 fusion.2
  251.3 0.7 fusion.36
  252.1 7.7 %collective-permute-done.7 = f32[2,2,32,512]{3,2,1,0:T(8,128)S(1)} collective-permute-done((f32[2,2,32,512]{3,2,1,0:T(8,128)S(1)}, f32[2,2,32,512]{3,2,1,0:T(8,128)S(1)}, u32[]{:S(2)}, u32[]{:S(2)}) %collective-permute-start.7) | collective-permute-done | bytes 262176 | tf_op jit(solution)/shard_map/ppermute | solution.py:12
  259.8 0.7 fusion.25
  260.5 0.7 slice.448
  (73 shorter events, 1.3 us)
Async XLA Ops:
  7.2 4.1 %copy-start.8 = (f32[4,2,32,512]{3,2,1,0:T(8,128)S(1)}, f32[4,2,32,512]{3,2,1,0:T(8,128)}, u32[]{:S(2)}) copy-start(f32[4,2,32,512]{3,2,1,0:T(8,128)} %param.6) | copy-start | bytes 1572868
  7.2 13.1 %copy-start.9 = (f32[4,2,32,512]{3,2,1,0:T(8,128)S(1)}, f32[4,2,32,512]{3,2,1,0:T(8,128)}, u32[]{:S(2)}) copy-start(f32[4,2,32,512]{3,2,1,0:T(8,128)} %param.7) | copy-start | bytes 1572868
  7.2 114.0 %all-gather.2.cloned.1.call-start = ((), (), s32[]{:S(2)}) async-start(), calls=%async_computation | async-start | bytes 13369344 | tf_op jit(solution)/shard_map/all_gather | solution.py:66
  11.3 11.5 %collective-permute-start = (f32[2,32,512]{2,1,0:T(8,128)S(1)}, f32[2,32,512]{2,1,0:T(8,128)S(1)}, u32[]{:S(2)}, u32[]{:S(2)}) collective-permute-start(f32[2,32,512]{2,1,0:T(8,128)S(1)} %get-tuple-element.26), channel_id=1, source_target_pairs={{0,496},{16,0},{32,16},{48,32},{64,48},{80,64},{96,80},{112,96},{1... | collective-permute-start | bytes 393224 | tf_op jit(solution)/shard_map/ppermute | solution.py:12
  130.7 5.7 %copy-start = (f32[1,64,512]{2,1,0:T(8,128)}, f32[1,64,512]{2,1,0:T(8,128)S(1)}, u32[]{:S(2)}) copy-start(f32[1,64,512]{2,1,0:T(8,128)S(1)} %get-tuple-element.17) | copy-start | bytes 393220
  130.7 5.7 %copy-start.2 = (f32[1,64,512]{2,1,0:T(8,128)}, f32[1,64,512]{2,1,0:T(8,128)S(1)}, u32[]{:S(2)}) copy-start(f32[1,64,512]{2,1,0:T(8,128)S(1)} %get-tuple-element.18) | copy-start | bytes 393220
  130.7 4.8 %copy-start.12 = (f32[2,2,32,512]{3,2,1,0:T(8,128)S(1)}, f32[2,2,32,512]{3,2,1,0:T(8,128)}, u32[]{:S(2)}) copy-start(f32[2,2,32,512]{3,2,1,0:T(8,128)} %param.4) | copy-start | bytes 786436
  135.5 0.9 copy-start.4
  135.5 3.4 %copy-start.6 = (f32[1,64,512]{2,1,0:T(8,128)}, f32[1,64,512]{2,1,0:T(8,128)S(1)}, u32[]{:S(2)}) copy-start(f32[1,64,512]{2,1,0:T(8,128)S(1)} %get-tuple-element.16) | copy-start | bytes 393220
  136.5 14.0 %collective-permute-start.1 = (f32[32,3072]{1,0:T(8,128)S(1)}, f32[32,3072]{1,0:T(8,128)}, u32[]{:S(2)}, u32[]{:S(2)}) collective-permute-start(f32[32,3072]{1,0:T(8,128)S(1)} %fusion.59), channel_id=1, source_target_pairs={{0,3},{1,0},{2,1},{3,2},{4,7},{5,4},{6,5},{7,6},{8,11},{9,8},{10,9... | collective-permute-start | bytes 1179656 | tf_op jit(solution)/shard_map/ppermute | solution.py:20
  139.0 21.9 %collective-permute-start.3 = (f32[32,3072]{1,0:T(8,128)S(1)}, f32[32,3072]{1,0:T(8,128)S(1)}, u32[]{:S(2)}, u32[]{:S(2)}) collective-permute-start(f32[32,3072]{1,0:T(8,128)S(1)} %fusion.59), channel_id=1, source_target_pairs={{0,1},{1,2},{2,3},{3,0},{4,5},{5,6},{6,7},{7,4},{8,9},{9,10},{10,1... | collective-permute-start | bytes 1179656 | tf_op jit(solution)/shard_map/ppermute | solution.py:20
  142.4 18.4 %collective-permute-start.2 = (f32[32,3072]{1,0:T(8,128)S(1)}, f32[32,3072]{1,0:T(8,128)S(1)}, u32[]{:S(2)}, u32[]{:S(2)}) collective-permute-start(f32[32,3072]{1,0:T(8,128)S(1)} %fusion.59), channel_id=1, source_target_pairs={{0,2},{1,3},{2,0},{3,1},{4,6},{5,7},{6,4},{7,5},{8,10},{9,11},{10,... | collective-permute-start | bytes 1179656 | tf_op jit(solution)/shard_map/ppermute | solution.py:20
  163.4 39.5 %collective-permute-start.4 = (f32[4,32,3072]{2,1,0:T(8,128)}, f32[4,32,3072]{2,1,0:T(8,128)}, u32[]{:S(2)}, u32[]{:S(2)}) collective-permute-start(f32[4,32,3072]{2,1,0:T(8,128)} %constant_dynamic-slice_fusion.1), channel_id=1, source_target_pairs={{0,12},{1,13},{2,14},{3,15},{4,0},{5,1},{6,2},{7,3},{8,4},{9,5},{1... | collective-permute-start | bytes 4718600 | tf_op jit(solution)/shard_map/ppermute | solution.py:20
  167.0 41.1 %collective-permute-start.5 = (f32[4,32,3072]{2,1,0:T(8,128)}, f32[4,32,3072]{2,1,0:T(8,128)}, u32[]{:S(2)}, u32[]{:S(2)}) collective-permute-start(f32[4,32,3072]{2,1,0:T(8,128)} %constant_dynamic-slice_fusion.1), channel_id=1, source_target_pairs={{0,8},{1,9},{2,10},{3,11},{4,12},{5,13},{6,14},{7,15},{8,0},{9,1},... | collective-permute-start | bytes 4718600 | tf_op jit(solution)/shard_map/ppermute | solution.py:20
  169.8 69.4 %collective-permute-start.6 = (f32[4,32,3072]{2,1,0:T(8,128)}, f32[4,32,3072]{2,1,0:T(8,128)}, u32[]{:S(2)}, u32[]{:S(2)}) collective-permute-start(f32[4,32,3072]{2,1,0:T(8,128)} %constant_dynamic-slice_fusion.1), channel_id=1, source_target_pairs={{0,4},{1,5},{2,6},{3,7},{4,8},{5,9},{6,10},{7,11},{8,12},{9,13},{1... | collective-permute-start | bytes 4718600 | tf_op jit(solution)/shard_map/ppermute | solution.py:20
  245.5 0.9 copy-start.10
  245.5 1.0 copy-start.11
  249.5 1.8 copy-start.5
  249.5 1.8 copy-start.7
  250.3 9.4 %copy-start.1 = (f32[1,64,512]{2,1,0:T(8,128)S(1)}, f32[1,64,512]{2,1,0:T(8,128)}, u32[]{:S(2)}) copy-start(f32[1,64,512]{2,1,0:T(8,128)} %copy-done) | copy-start | bytes 393220
  250.3 9.4 %copy-start.3 = (f32[1,64,512]{2,1,0:T(8,128)S(1)}, f32[1,64,512]{2,1,0:T(8,128)}, u32[]{:S(2)}) copy-start(f32[1,64,512]{2,1,0:T(8,128)} %copy-done.2) | copy-start | bytes 393220
  250.3 9.4 %copy-start.13 = (f32[2,2,32,512]{3,2,1,0:T(8,128)S(1)}, f32[2,2,32,512]{3,2,1,0:T(8,128)}, u32[]{:S(2)}) copy-start(f32[2,2,32,512]{3,2,1,0:T(8,128)} %param.4) | copy-start | bytes 786436
  252.0 7.7 %collective-permute-start.7 = (f32[2,2,32,512]{3,2,1,0:T(8,128)S(1)}, f32[2,2,32,512]{3,2,1,0:T(8,128)S(1)}, u32[]{:S(2)}, u32[]{:S(2)}) collective-permute-start(f32[2,2,32,512]{3,2,1,0:T(8,128)S(1)} %pad_maximum_fusion.8), channel_id=1, source_target_pairs={{0,16},{16,32},{32,48},{48,64},{64,80},{80,96},{96,112},{112,128},... | collective-permute-start | bytes 786440 | tf_op jit(solution)/shard_map/ppermute | solution.py:12
Sparse Core Ops, SparseCore 0:
  11.4 109.6 all-gather.1

commit v2 on v1

v2 whole, which is shorter than its diff:
```python
import jax
import jax.numpy as jnp
from jax import lax
from jax.experimental import pallas as pl
from jax.experimental.pallas import tpu as pltpu
from jax.sharding import PartitionSpec as P

SIDE = 4
VMEM_LIMIT = 28 * 1024 * 1024


def permuted(value, slabs, target):
    pairs = []
    for slab in range(slabs):
        for line in range(SIDE):
            for kind in range(SIDE):
                there = target(slab, line, kind)
                if there is None:
                    continue
                to_slab, to_orb = there
                pairs.append((slab * SIDE * SIDE + orb(slab, line, kind), to_slab % slabs * SIDE * SIDE + to_orb))
    return lax.ppermute(value, ("slab", "orb"), pairs)


def orb(slab, line, kind):
    line, kind = line % SIDE, kind % SIDE
    return SIDE * kind + line if slab % 2 == 0 else SIDE * line + kind


def along_kind(step):
    return lambda slab, line, kind: (slab, orb(slab, line, kind + step))


def along_line(step):
    return lambda slab, line, kind: (slab, orb(slab, line + step, kind))


def crossed(slab, line, kind):
    return slab, orb(slab, line, kind ^ 2)


def outwards(slab, line, kind):
    return (slab, orb(slab, line, kind ^ 1)) if kind in (1, 2) else None


def inner(slab, line, kind):
    return (slab, orb(slab, line, 3 - kind)) if kind in (1, 2) else None


def slab_below(slab, line, kind):
    return slab - 1, orb(slab, line, kind)


def to_owner(step):
    def target(slab, line, kind):
        return slab + kind // 2, orb(slab, line, step + kind - line)

    return target


def place():
    core = lax.rem(lax.axis_index("slab"), 2)
    index = lax.axis_index("orb")
    y = lax.div(index, SIDE)
    x = lax.rem(index, SIDE)
    return core, jnp.where(core == 0, x, y), jnp.where(core == 0, y, x)


def block_row(core, line, step, block, rows):
    there = lax.rem(line - step + 4, 4)
    index = jnp.where(core == 0, SIDE * block + there, SIDE * there + block)
    return pl.multiple_of(index * rows, rows)


def halves(value):
    high = value.astype(jnp.bfloat16)
    low = (value - high.astype(jnp.float32)).astype(jnp.bfloat16)
    return high, low


def dot(first, second):
    return jnp.dot(first, second, preferred_element_type=jnp.float32)


def product(left_re, left_im, right_high, right_low):
    rows, width = left_re.shape
    high, low = halves(jnp.concatenate([left_re, left_im], 0))
    both = dot(high, right_high) + (dot(high, right_low) + dot(low, right_high))
    return (
        both[:rows, :width] - both[rows:, width:],
        both[:rows, width:] + both[rows:, :width],
    )


def store_block(high_ref, low_ref, row, rows, block_re, block_im):
    width = block_re.shape[1]
    for part, value in enumerate((block_re, block_im)):
        high, low = halves(value)
        columns = slice(part * width, (part + 1) * width)
        high_ref[pl.ds(row, rows), columns] = high
        low_ref[pl.ds(row, rows), columns] = low


def first_kernel(*refs):
    chunks = refs[0:4]
    lefts = refs[4:8]
    both_ref, term_ref, cross_ref = refs[8:11]
    green_high, green_low, part_high, part_low, left = refs[11:]
    core, line, kind = place()
    rows = lefts[0].shape[2]
    for step in range(4):
        for block in range(4):
            row = block_row(core, line, step, lax.rem(kind - block + 4, 4), rows)
            ref = chunks[step].at[block]
            store_block(green_high, green_low, row, rows, ref[0, 0], ref[0, 1])
            store_block(part_high, part_low, row, rows, ref[1, 0], ref[1, 1])
    for step in range(4):
        own = pl.multiple_of(lax.rem(kind - step + 4, 4) * rows, rows)
        for side in range(2):
            for part in range(2):
                left[part, pl.ds(side * 4 * rows + own, rows), :] = lefts[step][side, part]
    middle_re, middle_im = product(left[0], left[1], green_high[...], green_low[...])
    out_re, out_im = product(middle_re, middle_im, part_high[...], part_low[...])
    count = 4 * rows
    even = lax.rem(kind, 2) == 0
    outer = (kind == 0) | (kind == 3)
    for part, value in enumerate((out_re, out_im)):
        below = -value[:count]
        above = -value[count:]
        panel = jnp.where(even, above, below)
        other = jnp.where(even, below, above)
        for block in range(4):
            piece = slice(block * rows, (block + 1) * rows)
            both_ref[0, block, part] = panel[piece]
            term_ref[block, part] = other[piece]
        for step in range(4):
            block = lax.rem(kind - step + 4, 4)
            term_ref[block, part] += jnp.where(kind == 1, lefts[step][2, part], 0.0)
        for block in range(4):
            term = term_ref[block, part]
            both_ref[1, block, part] = term
            cross_ref[block, part] = jnp.where(outer, both_ref[0, block, part], term)


def second_kernel(*refs):
    left_ref, keep_ref = refs[0:2]
    pivots = refs[2:6]
    panels = refs[6:10]
    out_ref = refs[10]
    pivot_high, pivot_low, panel_high, panel_low = refs[11:]
    core, line, kind = place()
    rows = left_ref.shape[2]
    width = left_ref.shape[3]
    column_iota = lax.broadcasted_iota(jnp.int32, (rows, width), 1)
    row_iota = lax.broadcasted_iota(jnp.int32, (rows, width), 0)
    diag_re = jnp.zeros((1, width), jnp.float32)
    diag_im = jnp.zeros((1, width), jnp.float32)
    for step in range(4):
        for block in range(4):
            row = block_row(core, line, step, block, rows)
            block_re = pivots[step][block, 0]
            block_im = pivots[step][block, 1]
            on_diagonal = column_iota == row_iota + row
            diag_re += jnp.sum(jnp.where(on_diagonal, block_re, 0.0), axis=0, keepdims=True)
            diag_im += jnp.sum(jnp.where(on_diagonal, block_im, 0.0), axis=0, keepdims=True)
            store_block(pivot_high, pivot_low, row, rows, block_re, block_im)
            store_block(panel_high, panel_low, row, rows, panels[step][block, 0], panels[step][block, 1])
    modulus = diag_re * diag_re + diag_im * diag_im
    weight_re = diag_re / modulus
    weight_im = -diag_im / modulus

    def scaled(re, im):
        return re * weight_re - im * weight_im, re * weight_im + im * weight_re

    def times_pivot(re, im):
        return product(re, im, pivot_high[...], pivot_low[...])

    def times_first(re, im):
        re, im = scaled(re, im)
        take_re, take_im = scaled(*times_pivot(re, im))
        return 2.0 * re - take_re, 2.0 * im - take_im

    left_re = jnp.concatenate([left_ref[block, 0] for block in range(4)], 0)
    left_im = jnp.concatenate([left_ref[block, 1] for block in range(4)], 0)
    guess_re, guess_im = times_first(left_re, left_im)
    take_re, take_im = times_first(*times_pivot(guess_re, guess_im))
    solved_re = 2.0 * guess_re - take_re
    solved_im = 2.0 * guess_im - take_im
    outs = product(solved_re, solved_im, panel_high[...], panel_low[...])
    for part, value in enumerate(outs):
        for block in range(4):
            kept = jnp.where((kind == 0) | (kind == 3), keep_ref[block, part], 0.0)
            slot = lax.rem(block + line - kind + 4, 4)
            out_ref[slot, part] = kept - value[block * rows : (block + 1) * rows]


def vmem(count):
    return [pl.BlockSpec(memory_space=pltpu.VMEM)] * count


def shards(diag_even, odd_green, lower, upper):
    rows = lower.shape[2]
    width = lower.shape[3]
    slabs = lax.axis_size("slab")
    core, line, kind = place()
    next_lower = permuted(lower[0], slabs, slab_below)

    def wanted(step):
        code = lax.rem(kind + step, 4)
        return lax.div(code, 2), lax.rem(code, 2)

    def rights(step):
        odd, part = wanted(step)
        green = lax.dynamic_index_in_dim(odd_green, odd, 0, False)
        down = lax.dynamic_index_in_dim(lower, 2 * odd + 1, 0, False)
        up = lax.dynamic_index_in_dim(upper, 2 * odd + 1, 0, False)
        return jnp.stack([green, jnp.where(part == 0, down, up)])

    def lefts(step):
        odd, part = wanted(step)
        below = lax.dynamic_index_in_dim(upper, 2 * odd, 0, False)
        above = jnp.where(odd == 0, lower[2], next_lower)
        return jnp.stack([below, above, diag_even[1]])

    whole = jnp.stack([rights(0)] + [permuted(rights(step), slabs, along_kind(step)) for step in range(1, 4)])
    rings = [permuted(whole, slabs, along_line(step)) for step in range(1, 4)]
    left_rows = [lefts(0)] + [permuted(lefts(step), slabs, along_kind(step)) for step in range(1, 4)]
    four = jax.ShapeDtypeStruct((4, 2, rows, width), jnp.float32)
    wide = pltpu.VMEM((width, 2 * width), jnp.bfloat16)
    both, term, cross = pl.pallas_call(
        first_kernel,
        out_shape=[jax.ShapeDtypeStruct((2, 4, 2, rows, width), jnp.float32), four, four],
        in_specs=vmem(8),
        out_specs=vmem(3),
        scratch_shapes=[wide] * 4 + [pltpu.VMEM((2, 8 * rows, width), jnp.float32)],
        compiler_params=pltpu.CompilerParams(vmem_limit_bytes=VMEM_LIMIT),
        name="first_level",
    )(whole, *rings, *left_rows)

    outer = (kind == 0) | (kind == 3)
    cross_there = permuted(cross, slabs, crossed)
    both_there = permuted(both, slabs, outwards)
    term_there = permuted(term, slabs, inner)
    panel = jnp.where(outer, both[0], cross_there)
    panel_rings = [permuted(panel, slabs, along_line(step)) for step in range(1, 4)]
    pivot = jnp.where(outer, cross_there + both_there[1], term + term_there)
    pivot_rings = [permuted(pivot, slabs, along_line(step)) for step in range(1, 4)]
    left = jnp.where(outer, both_there[0], both[0])
    out = pl.pallas_call(
        second_kernel,
        out_shape=four,
        in_specs=vmem(10),
        out_specs=vmem(1)[0],
        scratch_shapes=[wide] * 4,
        compiler_params=pltpu.CompilerParams(vmem_limit_bytes=VMEM_LIMIT),
        name="second_level",
    )(left, term, pivot, *pivot_rings, panel, *panel_rings)
    ends = [permuted(out[step], slabs, to_owner(step)) for step in range(4)]

    def ended(code):
        place_of = lax.rem(line + kind - code + 4, 4)
        result = ends[0]
        for step in range(1, 4):
            result = jnp.where(place_of == step, ends[step], result)
        return result

    final_diag = diag_even[0] + ended(0) + ended(3)
    return final_diag[None], ended(2)[None], ended(1)[None]


def solution(mesh):
    spec = P("slab", None, "orb", None)
    return jax.shard_map(
        shards, mesh=mesh, in_specs=(spec,) * 4, out_specs=(spec,) * 3, check_vma=False
    )
```

time: 269 us -> 152 us (0.57)
  the two profiles are of different devices: /device:TPU:4 before, /device:TPU:152 now
where the time goes in v2:
time: 152 us; the launch traced here: 151 us
  starting transfers between devices  82 us (54%)
  waiting for transfers between devices  53.9 us (35%)
  Pallas kernels  9.06 us (6%)
  other arithmetic  2.94 us (2%)
  local copies, waits for them, and re-layouts  2.04 us (1%)
    ppermute x23, starting transfers between devices, permuted(): return lax.ppermute(value, ('slab', 'orb'), pairs)  82 us
    ppermute x23, waiting for transfers between devices, permuted(): return lax.ppermute(value, ('slab', 'orb'), pairs)  53.9 us
    pallas_call x1, Pallas kernels, shards(): pl.pallas_call(second_kernel, out_shape=four, in_specs=vmem(10), out_spec...  4.88 us
    pallas_call x1, Pallas kernels, shards(): pl.pallas_call(first_kernel, out_shape=[jax.ShapeDtypeStruct((2, 4, 2, ro...  4.18 us
  transfers between devices with their start and end apart: 23, of which 11 were waited for; matrix products, arithmetic and copies ran while one was open for 0% of the time, Pallas kernels for 0%

profile of v2, /device:TPU:152, one launch (start us, length us, event | category | flops | bytes accessed | tf_op | source)
XLA Modules:
  0.0 151.2 jit_solution(139817605417344516)
XLA Ops:
  0.8 0.8 copy-done.2
  1.6 1.0 copy-done
  2.6 0.2 copy-done.1
  2.8 0.2 constant_dynamic-slice_fusion
  3.0 2.1 %collective-permute-start = (f32[2,2,32,512]{3,2,1,0:T(8,128)S(1)}, f32[2,2,32,512]{3,2,1,0:T(8,128)S(1)}, u32[]{:S(2)}, u32[]{:S(2)}) collective-permute-start(f32[2,2,32,512]{3,2,1,0:T(8,128)S(1)} %pad_maximum_fusion.5), channel_id=1, source_target_pairs={{0,4},{4,8},{8,12},{12,0},{1,5},{5,9},{9,13},{13,1},{2,6},{6,10},{... | collective-permute-start | bytes 786440 | tf_op jit(solution)/shard_map/ppermute | solution.py:22
  5.1 4.5 %collective-permute-start.1 = (f32[2,2,32,512]{3,2,1,0:T(8,128)S(1)}, f32[2,2,32,512]{3,2,1,0:T(8,128)S(1)}, u32[]{:S(2)}, u32[]{:S(2)}) collective-permute-start(f32[2,2,32,512]{3,2,1,0:T(8,128)S(1)} %pad_maximum_fusion.6), channel_id=1, source_target_pairs={{0,8},{4,12},{8,0},{12,4},{1,9},{5,13},{9,1},{13,5},{2,10},{6,14},... | collective-permute-start | bytes 786440 | tf_op jit(solution)/shard_map/ppermute | solution.py:22
  9.7 1.9 %collective-permute-start.2 = (f32[2,2,32,512]{3,2,1,0:T(8,128)S(1)}, f32[2,2,32,512]{3,2,1,0:T(8,128)S(1)}, u32[]{:S(2)}, u32[]{:S(2)}) collective-permute-start(f32[2,2,32,512]{3,2,1,0:T(8,128)S(1)} %pad_maximum_fusion.7), channel_id=1, source_target_pairs={{0,12},{4,0},{8,4},{12,8},{1,13},{5,1},{9,5},{13,9},{2,14},{6,2},{... | collective-permute-start | bytes 786440 | tf_op jit(solution)/shard_map/ppermute | solution.py:22
  11.6 1.6 %collective-permute-start.6 = (f32[2,32,512]{2,1,0:T(8,128)S(1)}, f32[2,32,512]{2,1,0:T(8,128)S(1)}, u32[]{:S(2)}, u32[]{:S(2)}) collective-permute-start(f32[2,32,512]{2,1,0:T(8,128)S(1)} %get-tuple-element.34), channel_id=1, source_target_pairs={{0,496},{4,500},{8,504},{12,508},{1,497},{5,501},{9,505},{13,509},... | collective-permute-start | bytes 393224 | tf_op jit(solution)/shard_map/ppermute | solution.py:22
  13.2 0.0 collective-permute-done
  13.2 1.7 %collective-permute-done.1 = f32[2,2,32,512]{3,2,1,0:T(8,128)S(1)} collective-permute-done((f32[2,2,32,512]{3,2,1,0:T(8,128)S(1)}, f32[2,2,32,512]{3,2,1,0:T(8,128)S(1)}, u32[]{:S(2)}, u32[]{:S(2)}) %collective-permute-start.1) | collective-permute-done | bytes 262176 | tf_op jit(solution)/shard_map/ppermute | solution.py:22
  14.9 4.2 %collective-permute-done.2 = f32[2,2,32,512]{3,2,1,0:T(8,128)S(1)} collective-permute-done((f32[2,2,32,512]{3,2,1,0:T(8,128)S(1)}, f32[2,2,32,512]{3,2,1,0:T(8,128)S(1)}, u32[]{:S(2)}, u32[]{:S(2)}) %collective-permute-start.2) | collective-permute-done | bytes 262176 | tf_op jit(solution)/shard_map/ppermute | solution.py:22
  19.2 0.1 pad_maximum_fusion.refs_0_
  19.3 0.0 slice-start
  19.3 3.5 %collective-permute-start.3 = (f32[4,2,2,32,512]{4,3,2,1,0:T(8,128)S(1)}, f32[4,2,2,32,512]{4,3,2,1,0:T(8,128)S(1)}, u32[]{:S(2)}, u32[]{:S(2)}) collective-permute-start(f32[4,2,2,32,512]{4,3,2,1,0:T(8,128)S(1)} %pad_maximum_fusion.refs_0_), channel_id=1, source_target_pairs={{0,1},{4,5},{8,9},{12,13},{1,2},{5,6},{9,10},{13,14},{2,3},{6,7},{... | collective-permute-start | bytes 3145736 | tf_op jit(solution)/shard_map/ppermute | solution.py:22
  22.8 4.6 %collective-permute-start.4 = (f32[4,2,2,32,512]{4,3,2,1,0:T(8,128)S(1)}, f32[4,2,2,32,512]{4,3,2,1,0:T(8,128)S(1)}, u32[]{:S(2)}, u32[]{:S(2)}) collective-permute-start(f32[4,2,2,32,512]{4,3,2,1,0:T(8,128)S(1)} %pad_maximum_fusion.refs_0_), channel_id=1, source_target_pairs={{0,2},{4,6},{8,10},{12,14},{1,3},{5,7},{9,11},{13,15},{2,0},{6,4},... | collective-permute-start | bytes 3145736 | tf_op jit(solution)/shard_map/ppermute | solution.py:22
  27.5 3.3 %collective-permute-start.5 = (f32[4,2,2,32,512]{4,3,2,1,0:T(8,128)S(1)}, f32[4,2,2,32,512]{4,3,2,1,0:T(8,128)S(1)}, u32[]{:S(2)}, u32[]{:S(2)}) collective-permute-start(f32[4,2,2,32,512]{4,3,2,1,0:T(8,128)S(1)} %pad_maximum_fusion.refs_0_), channel_id=1, source_target_pairs={{0,3},{4,7},{8,11},{12,15},{1,0},{5,4},{9,8},{13,12},{2,1},{6,5},{... | collective-permute-start | bytes 3145736 | tf_op jit(solution)/shard_map/ppermute | solution.py:22
  30.8 0.1 fusion.6
  30.9 0.2 pad_maximum_fusion.1
  31.1 2.6 %collective-permute-start.7 = (f32[3,2,32,512]{3,2,1,0:T(8,128)S(1)}, f32[3,2,32,512]{3,2,1,0:T(8,128)S(1)}, u32[]{:S(2)}, u32[]{:S(2)}) collective-permute-start(f32[3,2,32,512]{3,2,1,0:T(8,128)S(1)} %get-tuple-element.41), channel_id=1, source_target_pairs={{0,4},{4,8},{8,12},{12,0},{1,5},{5,9},{9,13},{13,1},{2,6},{6,10},{... | collective-permute-start | bytes 1179656 | tf_op jit(solution)/shard_map/ppermute | solution.py:22
  33.7 3.0 %collective-permute-start.8 = (f32[3,2,32,512]{3,2,1,0:T(8,128)S(1)}, f32[3,2,32,512]{3,2,1,0:T(8,128)S(1)}, u32[]{:S(2)}, u32[]{:S(2)}) collective-permute-start(f32[3,2,32,512]{3,2,1,0:T(8,128)S(1)} %get-tuple-element.42), channel_id=1, source_target_pairs={{0,8},{4,12},{8,0},{12,4},{1,9},{5,13},{9,1},{13,5},{2,10},{6,14},... | collective-permute-start | bytes 1179656 | tf_op jit(solution)/shard_map/ppermute | solution.py:22
  36.6 8.4 %collective-permute-done.7.refs_5_ = f32[3,2,32,512]{3,2,1,0:T(8,128)S(1)} collective-permute-done((f32[3,2,32,512]{3,2,1,0:T(8,128)S(1)}, f32[3,2,32,512]{3,2,1,0:T(8,128)S(1)}, u32[]{:S(2)}, u32[]{:S(2)}) %collective-permute-start.7) | collective-permute-done | bytes 393248 | tf_op jit(solution)/shard_map/ppermute | solution.py:22
  45.0 11.0 %collective-permute-start.9 = (f32[3,2,32,512]{3,2,1,0:T(8,128)S(1)}, f32[3,2,32,512]{3,2,1,0:T(8,128)S(1)}, u32[]{:S(2)}, u32[]{:S(2)}) collective-permute-start(f32[3,2,32,512]{3,2,1,0:T(8,128)S(1)} %get-tuple-element.40), channel_id=1, source_target_pairs={{0,12},{4,0},{8,4},{12,8},{1,13},{5,1},{9,5},{13,9},{2,14},{6,2},{... | collective-permute-start | bytes 1179656 | tf_op jit(solution)/shard_map/ppermute | solution.py:22
  56.1 5.3 %collective-permute-done.9.refs_7_ = f32[3,2,32,512]{3,2,1,0:T(8,128)S(1)} collective-permute-done((f32[3,2,32,512]{3,2,1,0:T(8,128)S(1)}, f32[3,2,32,512]{3,2,1,0:T(8,128)S(1)}, u32[]{:S(2)}, u32[]{:S(2)}) %collective-permute-start.9) | collective-permute-done | bytes 393248 | tf_op jit(solution)/shard_map/ppermute | solution.py:22
  61.3 4.2 %first_level.1 = (f32[2,4,2,32,512]{4,3,2,1,0:T(8,128)S(1)}, f32[4,2,32,512]{3,2,1,0:T(8,128)S(1)}, f32[4,2,32,512]{3,2,1,0:T(8,128)S(1)}) custom-call(f32[4,2,2,32,512]{4,3,2,1,0:T(8,128)S(1)} %pad_maximum_fusion.refs_0_, f32[4,2,2,32,512]{4,3,2,1,0:T(8,128)S(1)} %collective-permute-done.3.refs_1_, ...), custom_call_target="tpu_custom_call" | custom-call | tf_op jit(solution)/shard_map/first_level/pallas_call | solution.py:230
  65.5 1.3 collective-permute-start.10
  66.8 4.5 %collective-permute-start.11 = (f32[4,2,32,512]{3,2,1,0:T(8,128)S(1)}, f32[4,2,32,512]{3,2,1,0:T(8,128)}, u32[]{:S(2)}, u32[]{:S(2)}) collective-permute-start(f32[4,2,32,512]{3,2,1,0:T(8,128)S(1)} %get-tuple-element.8), channel_id=1, source_target_pairs={{0,8},{4,12},{8,0},{12,4},{1,9},{5,13},{9,1},{13,5},{2,10},{6,14},... | collective-permute-start | bytes 1572872 | tf_op jit(solution)/shard_map/ppermute | solution.py:22
  71.3 1.5 collective-permute-start.12
  72.8 15.0 %collective-permute-done.11 = f32[4,2,32,512]{3,2,1,0:T(8,128)} collective-permute-done((f32[4,2,32,512]{3,2,1,0:T(8,128)S(1)}, f32[4,2,32,512]{3,2,1,0:T(8,128)}, u32[]{:S(2)}, u32[]{:S(2)}) %collective-permute-start.11) | collective-permute-done | bytes 524320 | tf_op jit(solution)/shard_map/ppermute | solution.py:22
  87.8 1.6 %bitcast_select_fusion = (f32[4,2,32,512]{3,2,1,0:T(8,128)S(1)}, f32[4,2,32,512]{3,2,1,0:T(8,128)S(1)}, f32[4,2,32,512]{3,2,1,0:T(8,128)S(1)}) fusion(f32[4,2,32,512]{3,2,1,0:T(8,128)} %collective-permute-done.11, f32[2,4,2,32,512]{4,3,2,1,0:T(8,128)S(1)} %get-tuple-element.6, pred[]{:T(512)S(6)} %or.3, ...), kind=kLoop, calls=%fused_computation.10 | loop fusion | flops 655360 | bytes 4718593 | tf_op jit(solution)/shard_map/jit(_where)/select_n | solution.py:244
  89.4 3.3 %collective-permute-start.13 = (f32[4,2,32,512]{3,2,1,0:T(8,128)S(1)}, f32[4,2,32,512]{3,2,1,0:T(8,128)S(1)}, u32[]{:S(2)}, u32[]{:S(2)}) collective-permute-start(f32[4,2,32,512]{3,2,1,0:T(8,128)S(1)} %get-tuple-element.11.refs_2_), channel_id=1, source_target_pairs={{0,1},{4,5},{8,9},{12,13},{1,2},{5,6},{9,10},{13,14},{2,3},{6,7},{... | collective-permute-start | bytes 1572872 | tf_op jit(solution)/shard_map/ppermute | solution.py:22
  92.7 4.3 %collective-permute-start.14 = (f32[4,2,32,512]{3,2,1,0:T(8,128)S(1)}, f32[4,2,32,512]{3,2,1,0:T(8,128)S(1)}, u32[]{:S(2)}, u32[]{:S(2)}) collective-permute-start(f32[4,2,32,512]{3,2,1,0:T(8,128)S(1)} %get-tuple-element.11.refs_2_), channel_id=1, source_target_pairs={{0,2},{4,6},{8,10},{12,14},{1,3},{5,7},{9,11},{13,15},{2,0},{6,4},... | collective-permute-start | bytes 1572872 | tf_op jit(solution)/shard_map/ppermute | solution.py:22
  97.1 2.7 %collective-permute-start.15 = (f32[4,2,32,512]{3,2,1,0:T(8,128)S(1)}, f32[4,2,32,512]{3,2,1,0:T(8,128)S(1)}, u32[]{:S(2)}, u32[]{:S(2)}) collective-permute-start(f32[4,2,32,512]{3,2,1,0:T(8,128)S(1)} %get-tuple-element.11.refs_2_), channel_id=1, source_target_pairs={{0,3},{4,7},{8,11},{12,15},{1,0},{5,4},{9,8},{13,12},{2,1},{6,5},{... | collective-permute-start | bytes 1572872 | tf_op jit(solution)/shard_map/ppermute | solution.py:22
  99.8 3.1 %collective-permute-start.16 = (f32[4,2,32,512]{3,2,1,0:T(8,128)S(1)}, f32[4,2,32,512]{3,2,1,0:T(8,128)S(1)}, u32[]{:S(2)}, u32[]{:S(2)}) collective-permute-start(f32[4,2,32,512]{3,2,1,0:T(8,128)S(1)} %get-tuple-element.9.refs_6_), channel_id=1, source_target_pairs={{0,1},{4,5},{8,9},{12,13},{1,2},{5,6},{9,10},{13,14},{2,3},{6,7},{... | collective-permute-start | bytes 1572872 | tf_op jit(solution)/shard_map/ppermute | solution.py:22
  102.9 3.0 %collective-permute-start.17 = (f32[4,2,32,512]{3,2,1,0:T(8,128)S(1)}, f32[4,2,32,512]{3,2,1,0:T(8,128)S(1)}, u32[]{:S(2)}, u32[]{:S(2)}) collective-permute-start(f32[4,2,32,512]{3,2,1,0:T(8,128)S(1)} %get-tuple-element.9.refs_6_), channel_id=1, source_target_pairs={{0,2},{4,6},{8,10},{12,14},{1,3},{5,7},{9,11},{13,15},{2,0},{6,4},... | collective-permute-start | bytes 1572872 | tf_op jit(solution)/shard_map/ppermute | solution.py:22
  106.0 3.7 %collective-permute-start.18 = (f32[4,2,32,512]{3,2,1,0:T(8,128)S(1)}, f32[4,2,32,512]{3,2,1,0:T(8,128)S(1)}, u32[]{:S(2)}, u32[]{:S(2)}) collective-permute-start(f32[4,2,32,512]{3,2,1,0:T(8,128)S(1)} %get-tuple-element.9.refs_6_), channel_id=1, source_target_pairs={{0,3},{4,7},{8,11},{12,15},{1,0},{5,4},{9,8},{13,12},{2,1},{6,5},{... | collective-permute-start | bytes 1572872 | tf_op jit(solution)/shard_map/ppermute | solution.py:22
  109.7 0.4 collective-permute-done.15.refs_5_
  110.1 3.4 %collective-permute-done.16.refs_7_ = f32[4,2,32,512]{3,2,1,0:T(8,128)S(1)} collective-permute-done((f32[4,2,32,512]{3,2,1,0:T(8,128)S(1)}, f32[4,2,32,512]{3,2,1,0:T(8,128)S(1)}, u32[]{:S(2)}, u32[]{:S(2)}) %collective-permute-start.16) | collective-permute-done | bytes 524320 | tf_op jit(solution)/shard_map/ppermute | solution.py:22
  113.5 5.6 %collective-permute-done.17.refs_8_ = f32[4,2,32,512]{3,2,1,0:T(8,128)S(1)} collective-permute-done((f32[4,2,32,512]{3,2,1,0:T(8,128)S(1)}, f32[4,2,32,512]{3,2,1,0:T(8,128)S(1)}, u32[]{:S(2)}, u32[]{:S(2)}) %collective-permute-start.17) | collective-permute-done | bytes 524320 | tf_op jit(solution)/shard_map/ppermute | solution.py:22
  119.1 2.3 %collective-permute-done.18.refs_9_ = f32[4,2,32,512]{3,2,1,0:T(8,128)S(1)} collective-permute-done((f32[4,2,32,512]{3,2,1,0:T(8,128)S(1)}, f32[4,2,32,512]{3,2,1,0:T(8,128)S(1)}, u32[]{:S(2)}, u32[]{:S(2)}) %collective-permute-start.18) | collective-permute-done | bytes 524320 | tf_op jit(solution)/shard_map/ppermute | solution.py:22
  121.4 4.9 %second_level.1 = f32[4,2,32,512]{3,2,1,0:T(8,128)S(1)} custom-call(f32[4,2,32,512]{3,2,1,0:T(8,128)S(1)} %get-tuple-element.10.refs_0_, f32[4,2,32,512]{3,2,1,0:T(8,128)S(1)} %get-tuple-element.7.refs_1_, f32[4,2,32,512]{3,2,1,0:T(8,128)S(1)} %get-tuple-element.11.refs_2_, f32[4,2,32,512]{3,2,1,0:T(8,128)S(1)} %collective-permute-done.13.refs_3_, ...), custom_call_target="tpu_custom_call" | custom-call | tf_op jit(solution)/shard_map/second_level/pallas_call | solution.py:249
  126.3 0.0 copy-start.3
  126.4 2.1 %collective-permute-start.19 = (f32[2,32,512]{2,1,0:T(8,128)S(1)}, f32[2,32,512]{2,1,0:T(8,128)S(1)}, u32[]{:S(2)}, u32[]{:S(2)}) collective-permute-start(f32[2,32,512]{2,1,0:T(8,128)S(1)} %get-tuple-element.26), channel_id=1, source_target_pairs={{0,12},{4,0},{8,20},{12,24},{1,9},{5,13},{9,17},{13,21},{2,6},{6,1... | collective-permute-start | bytes 393224 | tf_op jit(solution)/shard_map/ppermute | solution.py:22
  128.4 1.9 %collective-permute-start.20 = (f32[2,32,512]{2,1,0:T(8,128)S(1)}, f32[2,32,512]{2,1,0:T(8,128)S(1)}, u32[]{:S(2)}, u32[]{:S(2)}) collective-permute-start(f32[2,32,512]{2,1,0:T(8,128)S(1)} %get-tuple-element.25), channel_id=1, source_target_pairs={{0,8},{4,12},{8,16},{12,20},{1,5},{5,9},{9,29},{13,17},{2,2},{6,6}... | collective-permute-start | bytes 393224 | tf_op jit(solution)/shard_map/ppermute | solution.py:22
  130.4 10.4 %collective-permute-start.21 = (f32[2,32,512]{2,1,0:T(8,128)S(1)}, f32[2,32,512]{2,1,0:T(8,128)S(1)}, u32[]{:S(2)}, u32[]{:S(2)}) collective-permute-start(f32[2,32,512]{2,1,0:T(8,128)S(1)} %get-tuple-element.24), channel_id=1, source_target_pairs={{0,4},{4,8},{8,28},{12,16},{1,1},{5,5},{9,25},{13,29},{2,14},{6,2}... | collective-permute-start | bytes 393224 | tf_op jit(solution)/shard_map/ppermute | solution.py:22
  140.8 1.9 %collective-permute-start.22 = (f32[2,32,512]{2,1,0:T(8,128)S(1)}, f32[2,32,512]{2,1,0:T(8,128)S(1)}, u32[]{:S(2)}, u32[]{:S(2)}) collective-permute-start(f32[2,32,512]{2,1,0:T(8,128)S(1)} %get-tuple-element.23), channel_id=1, source_target_pairs={{0,0},{4,4},{8,24},{12,28},{1,13},{5,1},{9,21},{13,25},{2,10},{6,1... | collective-permute-start | bytes 393224 | tf_op jit(solution)/shard_map/ppermute | solution.py:22
  142.8 0.5 collective-permute-done.21
  143.3 7.1 %collective-permute-done.22 = f32[2,32,512]{2,1,0:T(8,128)S(1)} collective-permute-done((f32[2,32,512]{2,1,0:T(8,128)S(1)}, f32[2,32,512]{2,1,0:T(8,128)S(1)}, u32[]{:S(2)}, u32[]{:S(2)}) %collective-permute-start.22) | collective-permute-done | bytes 131104 | tf_op jit(solution)/shard_map/ppermute | solution.py:22
  150.4 0.8 select_bitcast_fusion
  (22 shorter events, 0.2 us)
Async XLA Ops:
  0.6 1.0 copy-start.2
  1.6 1.0 copy-start
  1.6 1.2 copy-start.1
  3.0 10.2 %collective-permute-start = (f32[2,2,32,512]{3,2,1,0:T(8,128)S(1)}, f32[2,2,32,512]{3,2,1,0:T(8,128)S(1)}, u32[]{:S(2)}, u32[]{:S(2)}) collective-permute-start(f32[2,2,32,512]{3,2,1,0:T(8,128)S(1)} %pad_maximum_fusion.5), channel_id=1, source_target_pairs={{0,4},{4,8},{8,12},{12,0},{1,5},{5,9},{9,13},{13,1},{2,6},{6,10},{... | collective-permute-start | bytes 786440 | tf_op jit(solution)/shard_map/ppermute | solution.py:22
  5.1 9.8 %collective-permute-start.1 = (f32[2,2,32,512]{3,2,1,0:T(8,128)S(1)}, f32[2,2,32,512]{3,2,1,0:T(8,128)S(1)}, u32[]{:S(2)}, u32[]{:S(2)}) collective-permute-start(f32[2,2,32,512]{3,2,1,0:T(8,128)S(1)} %pad_maximum_fusion.6), channel_id=1, source_target_pairs={{0,8},{4,12},{8,0},{12,4},{1,9},{5,13},{9,1},{13,5},{2,10},{6,14},... | collective-permute-start | bytes 786440 | tf_op jit(solution)/shard_map/ppermute | solution.py:22
  9.7 9.5 %collective-permute-start.2 = (f32[2,2,32,512]{3,2,1,0:T(8,128)S(1)}, f32[2,2,32,512]{3,2,1,0:T(8,128)S(1)}, u32[]{:S(2)}, u32[]{:S(2)}) collective-permute-start(f32[2,2,32,512]{3,2,1,0:T(8,128)S(1)} %pad_maximum_fusion.7), channel_id=1, source_target_pairs={{0,12},{4,0},{8,4},{12,8},{1,13},{5,1},{9,5},{13,9},{2,14},{6,2},{... | collective-permute-start | bytes 786440 | tf_op jit(solution)/shard_map/ppermute | solution.py:22
  11.6 19.2 %collective-permute-start.6 = (f32[2,32,512]{2,1,0:T(8,128)S(1)}, f32[2,32,512]{2,1,0:T(8,128)S(1)}, u32[]{:S(2)}, u32[]{:S(2)}) collective-permute-start(f32[2,32,512]{2,1,0:T(8,128)S(1)} %get-tuple-element.34), channel_id=1, source_target_pairs={{0,496},{4,500},{8,504},{12,508},{1,497},{5,501},{9,505},{13,509},... | collective-permute-start | bytes 393224 | tf_op jit(solution)/shard_map/ppermute | solution.py:22
  19.3 11.6 %slice-start = ((f32[2,2,32,512]{3,2,1,0:T(8,128)}), f32[1,2,32,512]{3,2,1,0:T(8,128)S(1)}, s32[]{:S(2)}) async-start(f32[2,2,32,512]{3,2,1,0:T(8,128)} %param.4), calls=%async_computation | async-start | bytes 262144 | tf_op jit(solution)/shard_map/slice | solution.py:223
  19.3 42.1 %collective-permute-start.3 = (f32[4,2,2,32,512]{4,3,2,1,0:T(8,128)S(1)}, f32[4,2,2,32,512]{4,3,2,1,0:T(8,128)S(1)}, u32[]{:S(2)}, u32[]{:S(2)}) collective-permute-start(f32[4,2,2,32,512]{4,3,2,1,0:T(8,128)S(1)} %pad_maximum_fusion.refs_0_), channel_id=1, source_target_pairs={{0,1},{4,5},{8,9},{12,13},{1,2},{5,6},{9,10},{13,14},{2,3},{6,7},{... | collective-permute-start | bytes 3145736 | tf_op jit(solution)/shard_map/ppermute | solution.py:22
  22.8 38.5 %collective-permute-start.4 = (f32[4,2,2,32,512]{4,3,2,1,0:T(8,128)S(1)}, f32[4,2,2,32,512]{4,3,2,1,0:T(8,128)S(1)}, u32[]{:S(2)}, u32[]{:S(2)}) collective-permute-start(f32[4,2,2,32,512]{4,3,2,1,0:T(8,128)S(1)} %pad_maximum_fusion.refs_0_), channel_id=1, source_target_pairs={{0,2},{4,6},{8,10},{12,14},{1,3},{5,7},{9,11},{13,15},{2,0},{6,4},... | collective-permute-start | bytes 3145736 | tf_op jit(solution)/shard_map/ppermute | solution.py:22
  27.5 33.9 %collective-permute-start.5 = (f32[4,2,2,32,512]{4,3,2,1,0:T(8,128)S(1)}, f32[4,2,2,32,512]{4,3,2,1,0:T(8,128)S(1)}, u32[]{:S(2)}, u32[]{:S(2)}) collective-permute-start(f32[4,2,2,32,512]{4,3,2,1,0:T(8,128)S(1)} %pad_maximum_fusion.refs_0_), channel_id=1, source_target_pairs={{0,3},{4,7},{8,11},{12,15},{1,0},{5,4},{9,8},{13,12},{2,1},{6,5},{... | collective-permute-start | bytes 3145736 | tf_op jit(solution)/shard_map/ppermute | solution.py:22
  31.1 13.9 %collective-permute-start.7 = (f32[3,2,32,512]{3,2,1,0:T(8,128)S(1)}, f32[3,2,32,512]{3,2,1,0:T(8,128)S(1)}, u32[]{:S(2)}, u32[]{:S(2)}) collective-permute-start(f32[3,2,32,512]{3,2,1,0:T(8,128)S(1)} %get-tuple-element.41), channel_id=1, source_target_pairs={{0,4},{4,8},{8,12},{12,0},{1,5},{5,9},{9,13},{13,1},{2,6},{6,10},{... | collective-permute-start | bytes 1179656 | tf_op jit(solution)/shard_map/ppermute | solution.py:22
  33.7 22.4 %collective-permute-start.8 = (f32[3,2,32,512]{3,2,1,0:T(8,128)S(1)}, f32[3,2,32,512]{3,2,1,0:T(8,128)S(1)}, u32[]{:S(2)}, u32[]{:S(2)}) collective-permute-start(f32[3,2,32,512]{3,2,1,0:T(8,128)S(1)} %get-tuple-element.42), channel_id=1, source_target_pairs={{0,8},{4,12},{8,0},{12,4},{1,9},{5,13},{9,1},{13,5},{2,10},{6,14},... | collective-permute-start | bytes 1179656 | tf_op jit(solution)/shard_map/ppermute | solution.py:22
  45.0 16.3 %collective-permute-start.9 = (f32[3,2,32,512]{3,2,1,0:T(8,128)S(1)}, f32[3,2,32,512]{3,2,1,0:T(8,128)S(1)}, u32[]{:S(2)}, u32[]{:S(2)}) collective-permute-start(f32[3,2,32,512]{3,2,1,0:T(8,128)S(1)} %get-tuple-element.40), channel_id=1, source_target_pairs={{0,12},{4,0},{8,4},{12,8},{1,13},{5,1},{9,5},{13,9},{2,14},{6,2},{... | collective-permute-start | bytes 1179656 | tf_op jit(solution)/shard_map/ppermute | solution.py:22
  65.5 22.3 %collective-permute-start.10 = (f32[2,4,2,32,512]{4,3,2,1,0:T(8,128)S(1)}, f32[2,4,2,32,512]{4,3,2,1,0:T(8,128)S(1)}, u32[]{:S(2)}, u32[]{:S(2)}) collective-permute-start(f32[2,4,2,32,512]{4,3,2,1,0:T(8,128)S(1)} %get-tuple-element.6), channel_id=1, source_target_pairs={{4,0},{8,12},{5,1},{9,13},{6,2},{10,14},{7,3},{11,15},{17,16},{18,... | collective-permute-start | bytes 3145736 | tf_op jit(solution)/shard_map/ppermute | solution.py:22
  66.8 21.0 %collective-permute-start.11 = (f32[4,2,32,512]{3,2,1,0:T(8,128)S(1)}, f32[4,2,32,512]{3,2,1,0:T(8,128)}, u32[]{:S(2)}, u32[]{:S(2)}) collective-permute-start(f32[4,2,32,512]{3,2,1,0:T(8,128)S(1)} %get-tuple-element.8), channel_id=1, source_target_pairs={{0,8},{4,12},{8,0},{12,4},{1,9},{5,13},{9,1},{13,5},{2,10},{6,14},... | collective-permute-start | bytes 1572872 | tf_op jit(solution)/shard_map/ppermute | solution.py:22
  71.3 16.5 %collective-permute-start.12 = (f32[4,2,32,512]{3,2,1,0:T(8,128)S(1)}, f32[4,2,32,512]{3,2,1,0:T(8,128)}, u32[]{:S(2)}, u32[]{:S(2)}) collective-permute-start(f32[4,2,32,512]{3,2,1,0:T(8,128)S(1)} %get-tuple-element.7.refs_1_), channel_id=1, source_target_pairs={{4,8},{8,4},{5,9},{9,5},{6,10},{10,6},{7,11},{11,7},{17,18},{18,17... | collective-permute-start | bytes 1572872 | tf_op jit(solution)/shard_map/ppermute | solution.py:22
  89.4 16.5 %collective-permute-start.13 = (f32[4,2,32,512]{3,2,1,0:T(8,128)S(1)}, f32[4,2,32,512]{3,2,1,0:T(8,128)S(1)}, u32[]{:S(2)}, u32[]{:S(2)}) collective-permute-start(f32[4,2,32,512]{3,2,1,0:T(8,128)S(1)} %get-tuple-element.11.refs_2_), channel_id=1, source_target_pairs={{0,1},{4,5},{8,9},{12,13},{1,2},{5,6},{9,10},{13,14},{2,3},{6,7},{... | collective-permute-start | bytes 1572872 | tf_op jit(solution)/shard_map/ppermute | solution.py:22
  92.7 17.0 %collective-permute-start.14 = (f32[4,2,32,512]{3,2,1,0:T(8,128)S(1)}, f32[4,2,32,512]{3,2,1,0:T(8,128)S(1)}, u32[]{:S(2)}, u32[]{:S(2)}) collective-permute-start(f32[4,2,32,512]{3,2,1,0:T(8,128)S(1)} %get-tuple-element.11.refs_2_), channel_id=1, source_target_pairs={{0,2},{4,6},{8,10},{12,14},{1,3},{5,7},{9,11},{13,15},{2,0},{6,4},... | collective-permute-start | bytes 1572872 | tf_op jit(solution)/shard_map/ppermute | solution.py:22
  97.1 13.1 %collective-permute-start.15 = (f32[4,2,32,512]{3,2,1,0:T(8,128)S(1)}, f32[4,2,32,512]{3,2,1,0:T(8,128)S(1)}, u32[]{:S(2)}, u32[]{:S(2)}) collective-permute-start(f32[4,2,32,512]{3,2,1,0:T(8,128)S(1)} %get-tuple-element.11.refs_2_), channel_id=1, source_target_pairs={{0,3},{4,7},{8,11},{12,15},{1,0},{5,4},{9,8},{13,12},{2,1},{6,5},{... | collective-permute-start | bytes 1572872 | tf_op jit(solution)/shard_map/ppermute | solution.py:22
  99.8 13.7 %collective-permute-start.16 = (f32[4,2,32,512]{3,2,1,0:T(8,128)S(1)}, f32[4,2,32,512]{3,2,1,0:T(8,128)S(1)}, u32[]{:S(2)}, u32[]{:S(2)}) collective-permute-start(f32[4,2,32,512]{3,2,1,0:T(8,128)S(1)} %get-tuple-element.9.refs_6_), channel_id=1, source_target_pairs={{0,1},{4,5},{8,9},{12,13},{1,2},{5,6},{9,10},{13,14},{2,3},{6,7},{... | collective-permute-start | bytes 1572872 | tf_op jit(solution)/shard_map/ppermute | solution.py:22
  102.9 16.2 %collective-permute-start.17 = (f32[4,2,32,512]{3,2,1,0:T(8,128)S(1)}, f32[4,2,32,512]{3,2,1,0:T(8,128)S(1)}, u32[]{:S(2)}, u32[]{:S(2)}) collective-permute-start(f32[4,2,32,512]{3,2,1,0:T(8,128)S(1)} %get-tuple-element.9.refs_6_), channel_id=1, source_target_pairs={{0,2},{4,6},{8,10},{12,14},{1,3},{5,7},{9,11},{13,15},{2,0},{6,4},... | collective-permute-start | bytes 1572872 | tf_op jit(solution)/shard_map/ppermute | solution.py:22
  106.0 15.4 %collective-permute-start.18 = (f32[4,2,32,512]{3,2,1,0:T(8,128)S(1)}, f32[4,2,32,512]{3,2,1,0:T(8,128)S(1)}, u32[]{:S(2)}, u32[]{:S(2)}) collective-permute-start(f32[4,2,32,512]{3,2,1,0:T(8,128)S(1)} %get-tuple-element.9.refs_6_), channel_id=1, source_target_pairs={{0,3},{4,7},{8,11},{12,15},{1,0},{5,4},{9,8},{13,12},{2,1},{6,5},{... | collective-permute-start | bytes 1572872 | tf_op jit(solution)/shard_map/ppermute | solution.py:22
  126.3 24.1 %copy-start.3 = (f32[2,2,32,512]{3,2,1,0:T(8,128)S(1)}, f32[2,2,32,512]{3,2,1,0:T(8,128)}, u32[]{:S(2)}) copy-start(f32[2,2,32,512]{3,2,1,0:T(8,128)} %param.4) | copy-start | bytes 786436
  126.4 16.4 %collective-permute-start.19 = (f32[2,32,512]{2,1,0:T(8,128)S(1)}, f32[2,32,512]{2,1,0:T(8,128)S(1)}, u32[]{:S(2)}, u32[]{:S(2)}) collective-permute-start(f32[2,32,512]{2,1,0:T(8,128)S(1)} %get-tuple-element.26), channel_id=1, source_target_pairs={{0,12},{4,0},{8,20},{12,24},{1,9},{5,13},{9,17},{13,21},{2,6},{6,1... | collective-permute-start | bytes 393224 | tf_op jit(solution)/shard_map/ppermute | solution.py:22
  128.4 14.4 %collective-permute-start.20 = (f32[2,32,512]{2,1,0:T(8,128)S(1)}, f32[2,32,512]{2,1,0:T(8,128)S(1)}, u32[]{:S(2)}, u32[]{:S(2)}) collective-permute-start(f32[2,32,512]{2,1,0:T(8,128)S(1)} %get-tuple-element.25), channel_id=1, source_target_pairs={{0,8},{4,12},{8,16},{12,20},{1,5},{5,9},{9,29},{13,17},{2,2},{6,6}... | collective-permute-start | bytes 393224 | tf_op jit(solution)/shard_map/ppermute | solution.py:22
  130.4 12.9 %collective-permute-start.21 = (f32[2,32,512]{2,1,0:T(8,128)S(1)}, f32[2,32,512]{2,1,0:T(8,128)S(1)}, u32[]{:S(2)}, u32[]{:S(2)}) collective-permute-start(f32[2,32,512]{2,1,0:T(8,128)S(1)} %get-tuple-element.24), channel_id=1, source_target_pairs={{0,4},{4,8},{8,28},{12,16},{1,1},{5,5},{9,25},{13,29},{2,14},{6,2}... | collective-permute-start | bytes 393224 | tf_op jit(solution)/shard_map/ppermute | solution.py:22
  140.8 9.6 %collective-permute-start.22 = (f32[2,32,512]{2,1,0:T(8,128)S(1)}, f32[2,32,512]{2,1,0:T(8,128)S(1)}, u32[]{:S(2)}, u32[]{:S(2)}) collective-permute-start(f32[2,32,512]{2,1,0:T(8,128)S(1)} %get-tuple-element.23), channel_id=1, source_target_pairs={{0,0},{4,4},{8,24},{12,28},{1,13},{5,1},{9,21},{13,25},{2,10},{6,1... | collective-permute-start | bytes 393224 | tf_op jit(solution)/shard_map/ppermute | solution.py:22

commit v3 on v2

v3 whole, which is shorter than its diff:
```python
import jax
import jax.numpy as jnp
from jax import lax
from jax.experimental import pallas as pl
from jax.experimental.pallas import tpu as pltpu
from jax.sharding import PartitionSpec as P

SIDE = 4
VMEM_LIMIT = 20 * 1024 * 1024


def permuted(value, slabs, target):
    pairs = []
    for slab in range(slabs):
        for line in range(SIDE):
            for spot in range(SIDE):
                there = target(slab, line, spot)
                if there is None:
                    continue
                to_slab, to_orb = there
                pairs.append((slab * SIDE * SIDE + orb(slab, line, spot), to_slab % slabs * SIDE * SIDE + to_orb))
    return lax.ppermute(value, ("slab", "orb"), pairs)


def orb(slab, line, spot):
    line, spot = line % SIDE, spot % SIDE
    return SIDE * spot + line if slab % 2 == 0 else SIDE * line + spot


def along_spot(step):
    return lambda slab, line, spot: (slab, orb(slab, line, spot + step))


def along_line(step):
    return lambda slab, line, spot: (slab, orb(slab, line + step, spot))


def crossed(slab, line, spot):
    return slab, orb(slab, line, 3 - spot)


def outwards(slab, line, spot):
    return (slab, orb(slab, line, spot - 1)) if spot % 2 else None


def inner(slab, line, spot):
    return (slab, orb(slab, line, spot + 2)) if spot % 2 else None


def slab_below(slab, line, spot):
    return slab - 1, orb(slab, line, spot)


def to_owner(step):
    def target(slab, line, spot):
        return slab + spot // 2, orb(slab, line, step + spot - line)

    return target


def place():
    core = lax.rem(lax.axis_index("slab"), 2)
    index = lax.axis_index("orb")
    y = lax.div(index, SIDE)
    x = lax.rem(index, SIDE)
    return core, jnp.where(core == 0, x, y), jnp.where(core == 0, y, x)


def block_row(core, line, step, block, rows):
    there = lax.rem(line - step + 4, 4)
    index = jnp.where(core == 0, SIDE * block + there, SIDE * there + block)
    return pl.multiple_of(index * rows, rows)


def halves(value):
    high = value.astype(jnp.bfloat16)
    low = (value - high.astype(jnp.float32)).astype(jnp.bfloat16)
    return high, low


def dot(first, second):
    return jnp.dot(first, second, preferred_element_type=jnp.float32)


def product(left_re, left_im, right_high, right_low):
    rows, width = left_re.shape
    high, low = halves(jnp.concatenate([left_re, left_im], 0))
    both = dot(high, right_high) + (dot(high, right_low) + dot(low, right_high))
    return (
        both[:rows, :width] - both[rows:, width:],
        both[:rows, width:] + both[rows:, :width],
    )


def store_block(high_ref, low_ref, row, rows, block_re, block_im):
    width = block_re.shape[1]
    for part, value in enumerate((block_re, block_im)):
        high, low = halves(value)
        columns = slice(part * width, (part + 1) * width)
        high_ref[pl.ds(row, rows), columns] = high
        low_ref[pl.ds(row, rows), columns] = low


def first_kernel(*refs):
    messages = refs[0:4]
    rings = refs[4:7]
    front_ref, term_ref, cross_ref = refs[7:10]
    green_high, green_low, part_high, part_low, left = refs[10:]
    core, line, spot = place()
    rows = messages[0].shape[2]
    for step in range(4):
        for block in range(4):
            row = block_row(core, line, step, lax.rem(spot - block + 4, 4), rows)
            ref = messages[block] if step == 0 else rings[step - 1].at[block]
            store_block(green_high, green_low, row, rows, ref[0, 0], ref[0, 1])
            store_block(part_high, part_low, row, rows, ref[1, 0], ref[1, 1])
    for step in range(4):
        own = pl.multiple_of(lax.rem(spot - step + 4, 4) * rows, rows)
        for part in range(2):
            left[part, pl.ds(own, rows), :] = messages[step][2, part]
            left[part, pl.ds(4 * rows + own, rows), :] = messages[step][3, part]
    middle_re, middle_im = product(left[0], left[1], green_high[...], green_low[...])
    out_re, out_im = product(middle_re, middle_im, part_high[...], part_low[...])
    count = 4 * rows
    with_lower = (spot == 0) | (spot == 3)
    outer = lax.rem(spot, 2) == 0
    for part, value in enumerate((out_re, out_im)):
        below = -value[:count]
        above = -value[count:]
        panel = jnp.where(with_lower, above, below)
        other = jnp.where(with_lower, below, above)
        for block in range(4):
            piece = slice(block * rows, (block + 1) * rows)
            front_ref[block, part] = panel[piece]
            term_ref[block, part] = other[piece]
        for step in range(2):
            block = lax.rem(spot - step + 4, 4)
            term_ref[block, part] += jnp.where(outer, 0.0, messages[step][4, part])
        for block in range(4):
            cross_ref[block, part] = jnp.where(outer, front_ref[block, part], term_ref[block, part])


def second_kernel(*refs):
    front_ref, front_there_ref, keep_ref = refs[0:3]
    chunks = refs[3:7]
    out_ref = refs[7]
    pivot_high, pivot_low, panel_high, panel_low = refs[8:]
    core, line, spot = place()
    rows = front_ref.shape[2]
    width = front_ref.shape[3]
    outer = lax.rem(spot, 2) == 0
    column_iota = lax.broadcasted_iota(jnp.int32, (rows, width), 1)
    row_iota = lax.broadcasted_iota(jnp.int32, (rows, width), 0)
    diag_re = jnp.zeros((1, width), jnp.float32)
    diag_im = jnp.zeros((1, width), jnp.float32)
    for step in range(4):
        for block in range(4):
            row = block_row(core, line, step, block, rows)
            block_re = chunks[step][0, block, 0]
            block_im = chunks[step][0, block, 1]
            on_diagonal = column_iota == row_iota + row
            diag_re += jnp.sum(jnp.where(on_diagonal, block_re, 0.0), axis=0, keepdims=True)
            diag_im += jnp.sum(jnp.where(on_diagonal, block_im, 0.0), axis=0, keepdims=True)
            store_block(pivot_high, pivot_low, row, rows, block_re, block_im)
            store_block(panel_high, panel_low, row, rows, chunks[step][1, block, 0], chunks[step][1, block, 1])
    modulus = diag_re * diag_re + diag_im * diag_im
    weight_re = diag_re / modulus
    weight_im = -diag_im / modulus

    def scaled(re, im):
        return re * weight_re - im * weight_im, re * weight_im + im * weight_re

    def times_pivot(re, im):
        return product(re, im, pivot_high[...], pivot_low[...])

    def times_first(re, im):
        re, im = scaled(re, im)
        take_re, take_im = scaled(*times_pivot(re, im))
        return 2.0 * re - take_re, 2.0 * im - take_im

    left_re, left_im = (
        jnp.concatenate([jnp.where(outer, front_there_ref[block, part], front_ref[block, part]) for block in range(4)], 0)
        for part in range(2)
    )
    guess_re, guess_im = times_first(left_re, left_im)
    take_re, take_im = times_first(*times_pivot(guess_re, guess_im))
    solved_re = 2.0 * guess_re - take_re
    solved_im = 2.0 * guess_im - take_im
    outs = product(solved_re, solved_im, panel_high[...], panel_low[...])
    for part, value in enumerate(outs):
        for block in range(4):
            kept = jnp.where(outer, keep_ref[block, part], 0.0)
            slot = lax.rem(block + line - spot + 4, 4)
            out_ref[slot, part] = kept - value[block * rows : (block + 1) * rows]


def vmem(count):
    return [pl.BlockSpec(memory_space=pltpu.VMEM)] * count


def shards(diag_even, odd_green, lower, upper):
    rows = lower.shape[2]
    width = lower.shape[3]
    slabs = lax.axis_size("slab")
    core, line, spot = place()
    next_lower = permuted(lower[0], slabs, slab_below)

    def message(step):
        there = lax.rem(spot + step, 4)
        odd = lax.div(there, 2)
        green = lax.dynamic_index_in_dim(odd_green, odd, 0, False)
        down = lax.dynamic_index_in_dim(lower, 2 * odd + 1, 0, False)
        up = lax.dynamic_index_in_dim(upper, 2 * odd + 1, 0, False)
        below = lax.dynamic_index_in_dim(upper, 2 * odd, 0, False)
        with_lower = (there == 0) | (there == 3)
        above = jnp.where(odd == 0, lower[2], next_lower)
        blocks = [green, jnp.where(with_lower, down, up), below, above]
        return jnp.stack(blocks + [diag_even[1]] if step < 2 else blocks)

    def around(value, move, own):
        far, near, back = [permuted(value(step), slabs, move(step)) for step in (2, 1, 3)]
        return [own, near, far, back]

    messages = around(message, along_spot, message(0))
    whole = jnp.stack([piece[:2] for piece in messages])
    rings = around(lambda step: whole, along_line, whole)[1:]
    four = jax.ShapeDtypeStruct((4, 2, rows, width), jnp.float32)
    wide = pltpu.VMEM((width, 2 * width), jnp.bfloat16)
    front, term, cross = pl.pallas_call(
        first_kernel,
        out_shape=[four] * 3,
        in_specs=vmem(7),
        out_specs=vmem(3),
        scratch_shapes=[wide] * 4 + [pltpu.VMEM((2, 8 * rows, width), jnp.float32)],
        compiler_params=pltpu.CompilerParams(vmem_limit_bytes=VMEM_LIMIT),
        name="first_level",
    )(*messages, *rings)

    outer = lax.rem(spot, 2) == 0
    term_there = permuted(term, slabs, inner)
    term_out = permuted(term, slabs, outwards)
    cross_there = permuted(cross, slabs, crossed)
    panel = jnp.where(outer, front, cross_there)
    pivot = jnp.where(outer, cross_there + term_out, term + term_there)
    chunk = jnp.stack([pivot, panel])
    chunks = around(lambda step: chunk, along_line, chunk)
    after, _ = lax.optimization_barrier((front, term_there))
    front_there = permuted(after, slabs, outwards)
    out = pl.pallas_call(
        second_kernel,
        out_shape=four,
        in_specs=vmem(7),
        out_specs=vmem(1)[0],
        scratch_shapes=[wide] * 4,
        compiler_params=pltpu.CompilerParams(vmem_limit_bytes=VMEM_LIMIT),
        name="second_level",
    )(front, front_there, term, *chunks)
    ends = [permuted(out[step], slabs, to_owner(step)) for step in range(4)]

    def ended(code):
        place_of = lax.rem(line + spot - code + 4, 4)
        result = ends[0]
        for step in range(1, 4):
            result = jnp.where(place_of == step, ends[step], result)
        return result

    final_diag = diag_even[0] + ended(0) + ended(2)
    return final_diag[None], ended(3)[None], ended(1)[None]


def solution(mesh):
    spec = P("slab", None, "orb", None)
    return jax.shard_map(
        shards, mesh=mesh, in_specs=(spec,) * 4, out_specs=(spec,) * 3, check_vma=False
    )
```

time: 152 us -> 181 us (1.19)
  the two profiles are of different devices: /device:TPU:152 before, /device:TPU:4 now
where the time goes in v3:
time: 181 us
  waiting for transfers between devices  106 us (59%)
  starting transfers between devices  59.5 us (33%)
  Pallas kernels  8.97 us (5%)
  local copies, waits for them, and re-layouts  3.98 us (2%)
    ppermute x18, waiting for transfers between devices, permuted(): return lax.ppermute(value, ('slab', 'orb'), pairs)  106 us
    ppermute x18, starting transfers between devices, permuted(): return lax.ppermute(value, ('slab', 'orb'), pairs)  59.5 us
    pallas_call x1, Pallas kernels, shards(): pl.pallas_call(second_kernel, out_shape=four, in_specs=vmem(7), out_specs...  4.87 us
    pallas_call x1, Pallas kernels, shards(): pl.pallas_call(first_kernel, out_shape=[four] * 3, in_specs=vmem(7), out_...  4.1 us
  transfers between devices with their start and end apart: 18, of which 14 were waited for; matrix products, arithmetic and copies ran while one was open for 0% of the time, Pallas kernels for 0%

profile of v3, /device:TPU:4, one launch (start us, length us, event | category | flops | bytes accessed | tf_op | source)
XLA Modules:
  0.0 180.7 jit_solution(17044937637880474226)
XLA Ops:
  0.8 0.0 copy-start
  0.8 0.0 copy-start.1
  0.8 1.3 constant_dynamic-slice_fusion.1
  2.1 0.0 copy-done
  2.1 0.2 copy-done.1
  2.2 0.1 dynamic-slice_select_fusion
  2.4 0.8 copy-done.3
  3.2 8.9 %collective-permute-start = (f32[2,32,512]{2,1,0:T(8,128)S(1)}, f32[2,32,512]{2,1,0:T(8,128)S(1)}, u32[]{:S(2)}, u32[]{:S(2)}) collective-permute-start(f32[2,32,512]{2,1,0:T(8,128)S(1)} %get-tuple-element.33), channel_id=1, source_target_pairs={{0,496},{4,500},{8,504},{12,508},{1,497},{5,501},{9,505},{13,509},... | collective-permute-start | bytes 393224 | tf_op jit(solution)/shard_map/ppermute | solution.py:22
  12.2 0.7 dynamic-slice_dynamic-update-slice_fusion
  12.9 1.8 %collective-permute-done = f32[2,32,512]{2,1,0:T(8,128)S(1)} collective-permute-done((f32[2,32,512]{2,1,0:T(8,128)S(1)}, f32[2,32,512]{2,1,0:T(8,128)S(1)}, u32[]{:S(2)}, u32[]{:S(2)}) %collective-permute-start) | collective-permute-done | bytes 131104 | tf_op jit(solution)/shard_map/ppermute | solution.py:22
  14.8 5.1 %collective-permute-start.3 = (f32[4,2,32,512]{3,2,1,0:T(8,128)S(1)}, f32[4,2,32,512]{3,2,1,0:T(8,128)S(1)}, u32[]{:S(2)}, u32[]{:S(2)}) collective-permute-start(f32[4,2,32,512]{3,2,1,0:T(8,128)S(1)} %pad_maximum_fusion.3), channel_id=1, source_target_pairs={{0,12},{4,0},{8,4},{12,8},{1,13},{5,1},{9,5},{13,9},{2,14},{6,2},{... | collective-permute-start | bytes 1572872 | tf_op jit(solution)/shard_map/ppermute | solution.py:22
  19.9 2.5 %collective-permute-start.2 = (f32[4,2,32,512]{3,2,1,0:T(8,128)S(1)}, f32[4,2,32,512]{3,2,1,0:T(8,128)S(1)}, u32[]{:S(2)}, u32[]{:S(2)}) collective-permute-start(f32[4,2,32,512]{3,2,1,0:T(8,128)S(1)} %pad_maximum_fusion.2), channel_id=1, source_target_pairs={{0,8},{4,12},{8,0},{12,4},{1,9},{5,13},{9,1},{13,5},{2,10},{6,14},... | collective-permute-start | bytes 1572872 | tf_op jit(solution)/shard_map/ppermute | solution.py:22
  22.4 0.0 copy-start.2
  22.5 0.9 copy-done.2
  23.4 2.9 %collective-permute-start.1 = (f32[5,2,32,512]{3,2,1,0:T(8,128)S(1)}, f32[5,2,32,512]{3,2,1,0:T(8,128)S(1)}, u32[]{:S(2)}, u32[]{:S(2)}) collective-permute-start(f32[5,2,32,512]{3,2,1,0:T(8,128)S(1)} %get-tuple-element.43), channel_id=1, source_target_pairs={{0,4},{4,8},{8,12},{12,0},{1,5},{5,9},{9,13},{13,1},{2,6},{6,10},{... | collective-permute-start | bytes 1966088 | tf_op jit(solution)/shard_map/ppermute | solution.py:22
  26.3 5.8 %collective-permute-done.3.refs_3_ = f32[4,2,32,512]{3,2,1,0:T(8,128)S(1)} collective-permute-done((f32[4,2,32,512]{3,2,1,0:T(8,128)S(1)}, f32[4,2,32,512]{3,2,1,0:T(8,128)S(1)}, u32[]{:S(2)}, u32[]{:S(2)}) %collective-permute-start.3) | collective-permute-done | bytes 524320 | tf_op jit(solution)/shard_map/ppermute | solution.py:22
  32.2 0.4 collective-permute-done.2.refs_2_
  32.6 11.3 %collective-permute-done.1.refs_1_ = f32[5,2,32,512]{3,2,1,0:T(8,128)S(1)} collective-permute-done((f32[5,2,32,512]{3,2,1,0:T(8,128)S(1)}, f32[5,2,32,512]{3,2,1,0:T(8,128)S(1)}, u32[]{:S(2)}, u32[]{:S(2)}) %collective-permute-start.1) | collective-permute-done | bytes 655392 | tf_op jit(solution)/shard_map/ppermute | solution.py:22
  43.9 0.1 pad_maximum_fusion
  44.0 3.0 %collective-permute-start.4 = (f32[4,2,2,32,512]{4,3,2,1,0:T(8,128)S(1)}, f32[4,2,2,32,512]{4,3,2,1,0:T(8,128)S(1)}, u32[]{:S(2)}, u32[]{:S(2)}) collective-permute-start(f32[4,2,2,32,512]{4,3,2,1,0:T(8,128)S(1)} %pad_maximum_fusion), channel_id=1, source_target_pairs={{0,1},{4,5},{8,9},{12,13},{1,2},{5,6},{9,10},{13,14},{2,3},{6,7},{... | collective-permute-start | bytes 3145736 | tf_op jit(solution)/shard_map/ppermute | solution.py:22
  47.1 2.7 %collective-permute-start.5 = (f32[4,2,2,32,512]{4,3,2,1,0:T(8,128)S(1)}, f32[4,2,2,32,512]{4,3,2,1,0:T(8,128)S(1)}, u32[]{:S(2)}, u32[]{:S(2)}) collective-permute-start(f32[4,2,2,32,512]{4,3,2,1,0:T(8,128)S(1)} %pad_maximum_fusion), channel_id=1, source_target_pairs={{0,2},{4,6},{8,10},{12,14},{1,3},{5,7},{9,11},{13,15},{2,0},{6,4},... | collective-permute-start | bytes 3145736 | tf_op jit(solution)/shard_map/ppermute | solution.py:22
  49.8 2.6 %collective-permute-start.6 = (f32[4,2,2,32,512]{4,3,2,1,0:T(8,128)S(1)}, f32[4,2,2,32,512]{4,3,2,1,0:T(8,128)S(1)}, u32[]{:S(2)}, u32[]{:S(2)}) collective-permute-start(f32[4,2,2,32,512]{4,3,2,1,0:T(8,128)S(1)} %pad_maximum_fusion), channel_id=1, source_target_pairs={{0,3},{4,7},{8,11},{12,15},{1,0},{5,4},{9,8},{13,12},{2,1},{6,5},{... | collective-permute-start | bytes 3145736 | tf_op jit(solution)/shard_map/ppermute | solution.py:22
  52.4 8.4 %collective-permute-done.4.refs_4_ = f32[4,2,2,32,512]{4,3,2,1,0:T(8,128)S(1)} collective-permute-done((f32[4,2,2,32,512]{4,3,2,1,0:T(8,128)S(1)}, f32[4,2,2,32,512]{4,3,2,1,0:T(8,128)S(1)}, u32[]{:S(2)}, u32[]{:S(2)}) %collective-permute-start.4) | collective-permute-done | bytes 1048608 | tf_op jit(solution)/shard_map/ppermute | solution.py:22
  60.7 11.2 %collective-permute-done.5.refs_5_ = f32[4,2,2,32,512]{4,3,2,1,0:T(8,128)S(1)} collective-permute-done((f32[4,2,2,32,512]{4,3,2,1,0:T(8,128)S(1)}, f32[4,2,2,32,512]{4,3,2,1,0:T(8,128)S(1)}, u32[]{:S(2)}, u32[]{:S(2)}) %collective-permute-start.5) | collective-permute-done | bytes 1048608 | tf_op jit(solution)/shard_map/ppermute | solution.py:22
  72.0 9.5 %collective-permute-done.6.refs_6_ = f32[4,2,2,32,512]{4,3,2,1,0:T(8,128)S(1)} collective-permute-done((f32[4,2,2,32,512]{4,3,2,1,0:T(8,128)S(1)}, f32[4,2,2,32,512]{4,3,2,1,0:T(8,128)S(1)}, u32[]{:S(2)}, u32[]{:S(2)}) %collective-permute-start.6) | collective-permute-done | bytes 1048608 | tf_op jit(solution)/shard_map/ppermute | solution.py:22
  81.5 4.1 %first_level.1 = (f32[4,2,32,512]{3,2,1,0:T(8,128)S(1)}, f32[4,2,32,512]{3,2,1,0:T(8,128)S(1)}, f32[4,2,32,512]{3,2,1,0:T(8,128)S(1)}) custom-call(f32[5,2,32,512]{3,2,1,0:T(8,128)S(1)} %get-tuple-element.44.refs_0_, f32[5,2,32,512]{3,2,1,0:T(8,128)S(1)} %collective-permute-done.1.refs_1_, f32[4,2,32,512]{3,2,1,0:T(8,128)S(1)} %collective-permute-done.2.refs_2_, ...), custom_call_target="tpu_custom_call" | custom-call | tf_op jit(solution)/shard_map/first_level/pallas_call | solution.py:229
  85.6 1.3 collective-permute-start.10
  86.9 0.7 collective-permute-start.7
  87.6 8.5 %collective-permute-start.9 = (f32[4,2,32,512]{3,2,1,0:T(8,128)S(1)}, f32[4,2,32,512]{3,2,1,0:T(8,128)S(1)}, u32[]{:S(2)}, u32[]{:S(2)}) collective-permute-start(f32[4,2,32,512]{3,2,1,0:T(8,128)S(1)} %get-tuple-element.10), channel_id=1, source_target_pairs={{0,12},{4,8},{8,4},{12,0},{1,13},{5,9},{9,5},{13,1},{2,14},{6,10},... | collective-permute-start | bytes 1572872 | tf_op jit(solution)/shard_map/ppermute | solution.py:22
  96.1 4.5 %collective-permute-done.10 = f32[4,2,32,512]{3,2,1,0:T(8,128)S(1)} collective-permute-done((f32[4,2,32,512]{3,2,1,0:T(8,128)S(1)}, f32[4,2,32,512]{3,2,1,0:T(8,128)S(1)}, u32[]{:S(2)}, u32[]{:S(2)}) %collective-permute-start.10) | collective-permute-done | bytes 524320 | tf_op jit(solution)/shard_map/ppermute | solution.py:22
  100.5 22.0 %collective-permute-done.9 = f32[4,2,32,512]{3,2,1,0:T(8,128)S(1)} collective-permute-done((f32[4,2,32,512]{3,2,1,0:T(8,128)S(1)}, f32[4,2,32,512]{3,2,1,0:T(8,128)S(1)}, u32[]{:S(2)}, u32[]{:S(2)}) %collective-permute-start.9) | collective-permute-done | bytes 524320 | tf_op jit(solution)/shard_map/ppermute | solution.py:22
  122.6 0.3 select_bitcast_fusion.1
  122.9 0.1 pad_maximum_fusion.1.refs_3_
  123.0 2.5 %collective-permute-start.11 = (f32[2,4,2,32,512]{4,3,2,1,0:T(8,128)S(1)}, f32[2,4,2,32,512]{4,3,2,1,0:T(8,128)S(1)}, u32[]{:S(2)}, u32[]{:S(2)}) collective-permute-start(f32[2,4,2,32,512]{4,3,2,1,0:T(8,128)S(1)} %pad_maximum_fusion.1.refs_3_), channel_id=1, source_target_pairs={{0,1},{4,5},{8,9},{12,13},{1,2},{5,6},{9,10},{13,14},{2,3},{6,7},{... | collective-permute-start | bytes 3145736 | tf_op jit(solution)/shard_map/ppermute | solution.py:22
  125.5 1.9 %collective-permute-start.12 = (f32[2,4,2,32,512]{4,3,2,1,0:T(8,128)S(1)}, f32[2,4,2,32,512]{4,3,2,1,0:T(8,128)S(1)}, u32[]{:S(2)}, u32[]{:S(2)}) collective-permute-start(f32[2,4,2,32,512]{4,3,2,1,0:T(8,128)S(1)} %pad_maximum_fusion.1.refs_3_), channel_id=1, source_target_pairs={{0,2},{4,6},{8,10},{12,14},{1,3},{5,7},{9,11},{13,15},{2,0},{6,4},... | collective-permute-start | bytes 3145736 | tf_op jit(solution)/shard_map/ppermute | solution.py:22
  127.4 4.2 %collective-permute-start.13 = (f32[2,4,2,32,512]{4,3,2,1,0:T(8,128)S(1)}, f32[2,4,2,32,512]{4,3,2,1,0:T(8,128)S(1)}, u32[]{:S(2)}, u32[]{:S(2)}) collective-permute-start(f32[2,4,2,32,512]{4,3,2,1,0:T(8,128)S(1)} %pad_maximum_fusion.1.refs_3_), channel_id=1, source_target_pairs={{0,3},{4,7},{8,11},{12,15},{1,0},{5,4},{9,8},{13,12},{2,1},{6,5},{... | collective-permute-start | bytes 3145736 | tf_op jit(solution)/shard_map/ppermute | solution.py:22
  131.7 1.3 collective-permute-start.8
  132.9 9.8 %collective-permute-done.8.refs_1_ = f32[4,2,32,512]{3,2,1,0:T(8,128)S(1)} collective-permute-done((f32[4,2,32,512]{3,2,1,0:T(8,128)S(1)}, f32[4,2,32,512]{3,2,1,0:T(8,128)S(1)}, u32[]{:S(2)}, u32[]{:S(2)}) %collective-permute-start.8) | collective-permute-done | bytes 524320 | tf_op jit(solution)/shard_map/ppermute | solution.py:22
  142.7 10.5 %collective-permute-done.11.refs_4_ = f32[2,4,2,32,512]{4,3,2,1,0:T(8,128)S(1)} collective-permute-done((f32[2,4,2,32,512]{4,3,2,1,0:T(8,128)S(1)}, f32[2,4,2,32,512]{4,3,2,1,0:T(8,128)S(1)}, u32[]{:S(2)}, u32[]{:S(2)}) %collective-permute-start.11) | collective-permute-done | bytes 1048608 | tf_op jit(solution)/shard_map/ppermute | solution.py:22
  153.2 1.7 collective-permute-done.13.refs_6_
  154.9 4.9 %second_level.1 = f32[4,2,32,512]{3,2,1,0:T(8,128)S(1)} custom-call(f32[4,2,32,512]{3,2,1,0:T(8,128)S(1)} %get-tuple-element.9.refs_0_, f32[4,2,32,512]{3,2,1,0:T(8,128)S(1)} %collective-permute-done.8.refs_1_, f32[4,2,32,512]{3,2,1,0:T(8,128)S(1)} %get-tuple-element.8.refs_2_, f32[2,4,2,32,512]{4,3,2,1,0:T(8,128)S(1)} %pad_maximum_fusion.1.refs_3_, ...), custom_call_target="tpu_custom_call" | custom-call | tf_op jit(solution)/shard_map/second_level/pallas_call | solution.py:249
  159.9 2.9 %collective-permute-start.14 = (f32[2,32,512]{2,1,0:T(8,128)S(1)}, f32[2,32,512]{2,1,0:T(8,128)S(1)}, u32[]{:S(2)}, u32[]{:S(2)}) collective-permute-start(f32[2,32,512]{2,1,0:T(8,128)S(1)} %get-tuple-element.30), channel_id=1, source_target_pairs={{0,12},{4,0},{8,20},{12,24},{1,9},{5,13},{9,17},{13,21},{2,6},{6,1... | collective-permute-start | bytes 393224 | tf_op jit(solution)/shard_map/ppermute | solution.py:22
  162.8 0.7 collective-permute-start.15
  163.4 5.9 %collective-permute-start.16 = (f32[2,32,512]{2,1,0:T(8,128)S(1)}, f32[2,32,512]{2,1,0:T(8,128)S(1)}, u32[]{:S(2)}, u32[]{:S(2)}) collective-permute-start(f32[2,32,512]{2,1,0:T(8,128)S(1)} %get-tuple-element.28), channel_id=1, source_target_pairs={{0,4},{4,8},{8,28},{12,16},{1,1},{5,5},{9,25},{13,29},{2,14},{6,2}... | collective-permute-start | bytes 393224 | tf_op jit(solution)/shard_map/ppermute | solution.py:22
  169.3 1.9 %collective-permute-start.17 = (f32[2,32,512]{2,1,0:T(8,128)S(1)}, f32[2,32,512]{2,1,0:T(8,128)S(1)}, u32[]{:S(2)}, u32[]{:S(2)}) collective-permute-start(f32[2,32,512]{2,1,0:T(8,128)S(1)} %get-tuple-element.27), channel_id=1, source_target_pairs={{0,0},{4,4},{8,24},{12,28},{1,13},{5,1},{9,21},{13,25},{2,10},{6,1... | collective-permute-start | bytes 393224 | tf_op jit(solution)/shard_map/ppermute | solution.py:22
  171.3 0.5 collective-permute-done.16
  171.8 8.1 %collective-permute-done.17 = f32[2,32,512]{2,1,0:T(8,128)S(1)} collective-permute-done((f32[2,32,512]{2,1,0:T(8,128)S(1)}, f32[2,32,512]{2,1,0:T(8,128)S(1)}, u32[]{:S(2)}, u32[]{:S(2)}) %collective-permute-start.17) | collective-permute-done | bytes 131104 | tf_op jit(solution)/shard_map/ppermute | solution.py:22
  179.9 0.8 select_bitcast_fusion.2
  (17 shorter events, 0.3 us)
Async XLA Ops:
  0.8 1.3 copy-start
  0.8 1.4 copy-start.1
  2.4 0.8 copy-start.3
  3.2 11.5 %collective-permute-start = (f32[2,32,512]{2,1,0:T(8,128)S(1)}, f32[2,32,512]{2,1,0:T(8,128)S(1)}, u32[]{:S(2)}, u32[]{:S(2)}) collective-permute-start(f32[2,32,512]{2,1,0:T(8,128)S(1)} %get-tuple-element.33), channel_id=1, source_target_pairs={{0,496},{4,500},{8,504},{12,508},{1,497},{5,501},{9,505},{13,509},... | collective-permute-start | bytes 393224 | tf_op jit(solution)/shard_map/ppermute | solution.py:22
  14.8 7.7 %copy-start.4 = (f32[5,2,32,512]{3,2,1,0:T(8,128)S(1)}, f32[5,2,32,512]{3,2,1,0:T(8,128)}, u32[]{:S(2)}) copy-start(f32[5,2,32,512]{3,2,1,0:T(8,128)} %get-tuple-element.36) | copy-start | bytes 1966084
  14.8 17.4 %collective-permute-start.3 = (f32[4,2,32,512]{3,2,1,0:T(8,128)S(1)}, f32[4,2,32,512]{3,2,1,0:T(8,128)S(1)}, u32[]{:S(2)}, u32[]{:S(2)}) collective-permute-start(f32[4,2,32,512]{3,2,1,0:T(8,128)S(1)} %pad_maximum_fusion.3), channel_id=1, source_target_pairs={{0,12},{4,0},{8,4},{12,8},{1,13},{5,1},{9,5},{13,9},{2,14},{6,2},{... | collective-permute-start | bytes 1572872 | tf_op jit(solution)/shard_map/ppermute | solution.py:22
  19.9 12.7 %collective-permute-start.2 = (f32[4,2,32,512]{3,2,1,0:T(8,128)S(1)}, f32[4,2,32,512]{3,2,1,0:T(8,128)S(1)}, u32[]{:S(2)}, u32[]{:S(2)}) collective-permute-start(f32[4,2,32,512]{3,2,1,0:T(8,128)S(1)} %pad_maximum_fusion.2), channel_id=1, source_target_pairs={{0,8},{4,12},{8,0},{12,4},{1,9},{5,13},{9,1},{13,5},{2,10},{6,14},... | collective-permute-start | bytes 1572872 | tf_op jit(solution)/shard_map/ppermute | solution.py:22
  22.4 1.0 copy-start.2
  23.4 20.5 %collective-permute-start.1 = (f32[5,2,32,512]{3,2,1,0:T(8,128)S(1)}, f32[5,2,32,512]{3,2,1,0:T(8,128)S(1)}, u32[]{:S(2)}, u32[]{:S(2)}) collective-permute-start(f32[5,2,32,512]{3,2,1,0:T(8,128)S(1)} %get-tuple-element.43), channel_id=1, source_target_pairs={{0,4},{4,8},{8,12},{12,0},{1,5},{5,9},{9,13},{13,1},{2,6},{6,10},{... | collective-permute-start | bytes 1966088 | tf_op jit(solution)/shard_map/ppermute | solution.py:22
  44.0 16.7 %collective-permute-start.4 = (f32[4,2,2,32,512]{4,3,2,1,0:T(8,128)S(1)}, f32[4,2,2,32,512]{4,3,2,1,0:T(8,128)S(1)}, u32[]{:S(2)}, u32[]{:S(2)}) collective-permute-start(f32[4,2,2,32,512]{4,3,2,1,0:T(8,128)S(1)} %pad_maximum_fusion), channel_id=1, source_target_pairs={{0,1},{4,5},{8,9},{12,13},{1,2},{5,6},{9,10},{13,14},{2,3},{6,7},{... | collective-permute-start | bytes 3145736 | tf_op jit(solution)/shard_map/ppermute | solution.py:22
  47.1 24.9 %collective-permute-start.5 = (f32[4,2,2,32,512]{4,3,2,1,0:T(8,128)S(1)}, f32[4,2,2,32,512]{4,3,2,1,0:T(8,128)S(1)}, u32[]{:S(2)}, u32[]{:S(2)}) collective-permute-start(f32[4,2,2,32,512]{4,3,2,1,0:T(8,128)S(1)} %pad_maximum_fusion), channel_id=1, source_target_pairs={{0,2},{4,6},{8,10},{12,14},{1,3},{5,7},{9,11},{13,15},{2,0},{6,4},... | collective-permute-start | bytes 3145736 | tf_op jit(solution)/shard_map/ppermute | solution.py:22
  49.8 31.7 %collective-permute-start.6 = (f32[4,2,2,32,512]{4,3,2,1,0:T(8,128)S(1)}, f32[4,2,2,32,512]{4,3,2,1,0:T(8,128)S(1)}, u32[]{:S(2)}, u32[]{:S(2)}) collective-permute-start(f32[4,2,2,32,512]{4,3,2,1,0:T(8,128)S(1)} %pad_maximum_fusion), channel_id=1, source_target_pairs={{0,3},{4,7},{8,11},{12,15},{1,0},{5,4},{9,8},{13,12},{2,1},{6,5},{... | collective-permute-start | bytes 3145736 | tf_op jit(solution)/shard_map/ppermute | solution.py:22
  85.6 14.9 %collective-permute-start.10 = (f32[4,2,32,512]{3,2,1,0:T(8,128)S(1)}, f32[4,2,32,512]{3,2,1,0:T(8,128)S(1)}, u32[]{:S(2)}, u32[]{:S(2)}) collective-permute-start(f32[4,2,32,512]{3,2,1,0:T(8,128)S(1)} %get-tuple-element.8.refs_2_), channel_id=1, source_target_pairs={{4,0},{12,8},{5,1},{13,9},{6,2},{14,10},{7,3},{15,11},{17,16},{19,... | collective-permute-start | bytes 1572872 | tf_op jit(solution)/shard_map/ppermute | solution.py:22
  86.9 13.6 %collective-permute-start.7 = (f32[4,2,32,512]{3,2,1,0:T(8,128)S(1)}, f32[4,2,32,512]{3,2,1,0:T(8,128)S(1)}, u32[]{:S(2)}, u32[]{:S(2)}) collective-permute-start(f32[4,2,32,512]{3,2,1,0:T(8,128)S(1)} %get-tuple-element.8.refs_2_), channel_id=1, source_target_pairs={{4,12},{12,4},{5,13},{13,5},{6,14},{14,6},{7,15},{15,7},{17,19},{1... | collective-permute-start | bytes 1572872 | tf_op jit(solution)/shard_map/ppermute | solution.py:22
  87.6 35.0 %collective-permute-start.9 = (f32[4,2,32,512]{3,2,1,0:T(8,128)S(1)}, f32[4,2,32,512]{3,2,1,0:T(8,128)S(1)}, u32[]{:S(2)}, u32[]{:S(2)}) collective-permute-start(f32[4,2,32,512]{3,2,1,0:T(8,128)S(1)} %get-tuple-element.10), channel_id=1, source_target_pairs={{0,12},{4,8},{8,4},{12,0},{1,13},{5,9},{9,5},{13,1},{2,14},{6,10},... | collective-permute-start | bytes 1572872 | tf_op jit(solution)/shard_map/ppermute | solution.py:22
  123.0 30.2 %collective-permute-start.11 = (f32[2,4,2,32,512]{4,3,2,1,0:T(8,128)S(1)}, f32[2,4,2,32,512]{4,3,2,1,0:T(8,128)S(1)}, u32[]{:S(2)}, u32[]{:S(2)}) collective-permute-start(f32[2,4,2,32,512]{4,3,2,1,0:T(8,128)S(1)} %pad_maximum_fusion.1.refs_3_), channel_id=1, source_target_pairs={{0,1},{4,5},{8,9},{12,13},{1,2},{5,6},{9,10},{13,14},{2,3},{6,7},{... | collective-permute-start | bytes 3145736 | tf_op jit(solution)/shard_map/ppermute | solution.py:22
  125.5 27.7 %collective-permute-start.12 = (f32[2,4,2,32,512]{4,3,2,1,0:T(8,128)S(1)}, f32[2,4,2,32,512]{4,3,2,1,0:T(8,128)S(1)}, u32[]{:S(2)}, u32[]{:S(2)}) collective-permute-start(f32[2,4,2,32,512]{4,3,2,1,0:T(8,128)S(1)} %pad_maximum_fusion.1.refs_3_), channel_id=1, source_target_pairs={{0,2},{4,6},{8,10},{12,14},{1,3},{5,7},{9,11},{13,15},{2,0},{6,4},... | collective-permute-start | bytes 3145736 | tf_op jit(solution)/shard_map/ppermute | solution.py:22
  127.4 27.5 %collective-permute-start.13 = (f32[2,4,2,32,512]{4,3,2,1,0:T(8,128)S(1)}, f32[2,4,2,32,512]{4,3,2,1,0:T(8,128)S(1)}, u32[]{:S(2)}, u32[]{:S(2)}) collective-permute-start(f32[2,4,2,32,512]{4,3,2,1,0:T(8,128)S(1)} %pad_maximum_fusion.1.refs_3_), channel_id=1, source_target_pairs={{0,3},{4,7},{8,11},{12,15},{1,0},{5,4},{9,8},{13,12},{2,1},{6,5},{... | collective-permute-start | bytes 3145736 | tf_op jit(solution)/shard_map/ppermute | solution.py:22
  131.7 11.1 %collective-permute-start.8 = (f32[4,2,32,512]{3,2,1,0:T(8,128)S(1)}, f32[4,2,32,512]{3,2,1,0:T(8,128)S(1)}, u32[]{:S(2)}, u32[]{:S(2)}) collective-permute-start(f32[4,2,32,512]{3,2,1,0:T(8,128)S(1)} %get-tuple-element.9.refs_0_), channel_id=1, source_target_pairs={{4,0},{12,8},{5,1},{13,9},{6,2},{14,10},{7,3},{15,11},{17,16},{19,... | collective-permute-start | bytes 1572872 | tf_op jit(solution)/shard_map/ppermute | solution.py:22
  159.9 11.5 %collective-permute-start.14 = (f32[2,32,512]{2,1,0:T(8,128)S(1)}, f32[2,32,512]{2,1,0:T(8,128)S(1)}, u32[]{:S(2)}, u32[]{:S(2)}) collective-permute-start(f32[2,32,512]{2,1,0:T(8,128)S(1)} %get-tuple-element.30), channel_id=1, source_target_pairs={{0,12},{4,0},{8,20},{12,24},{1,9},{5,13},{9,17},{13,21},{2,6},{6,1... | collective-permute-start | bytes 393224 | tf_op jit(solution)/shard_map/ppermute | solution.py:22
  162.8 8.6 %collective-permute-start.15 = (f32[2,32,512]{2,1,0:T(8,128)S(1)}, f32[2,32,512]{2,1,0:T(8,128)S(1)}, u32[]{:S(2)}, u32[]{:S(2)}) collective-permute-start(f32[2,32,512]{2,1,0:T(8,128)S(1)} %get-tuple-element.29), channel_id=1, source_target_pairs={{0,8},{4,12},{8,16},{12,20},{1,5},{5,9},{9,29},{13,17},{2,2},{6,6}... | collective-permute-start | bytes 393224 | tf_op jit(solution)/shard_map/ppermute | solution.py:22
  163.4 8.4 %collective-permute-start.16 = (f32[2,32,512]{2,1,0:T(8,128)S(1)}, f32[2,32,512]{2,1,0:T(8,128)S(1)}, u32[]{:S(2)}, u32[]{:S(2)}) collective-permute-start(f32[2,32,512]{2,1,0:T(8,128)S(1)} %get-tuple-element.28), channel_id=1, source_target_pairs={{0,4},{4,8},{8,28},{12,16},{1,1},{5,5},{9,25},{13,29},{2,14},{6,2}... | collective-permute-start | bytes 393224 | tf_op jit(solution)/shard_map/ppermute | solution.py:22
  169.3 10.6 %collective-permute-start.17 = (f32[2,32,512]{2,1,0:T(8,128)S(1)}, f32[2,32,512]{2,1,0:T(8,128)S(1)}, u32[]{:S(2)}, u32[]{:S(2)}) collective-permute-start(f32[2,32,512]{2,1,0:T(8,128)S(1)} %get-tuple-element.27), channel_id=1, source_target_pairs={{0,0},{4,4},{8,24},{12,28},{1,13},{5,1},{9,21},{13,25},{2,10},{6,1... | collective-permute-start | bytes 393224 | tf_op jit(solution)/shard_map/ppermute | solution.py:22

commit v4 on v3

--- a/solution.py
+++ b/solution.py
@@ -103,17 +103,19 @@
 
 def first_kernel(*refs):
     messages = refs[0:4]
-    rings = refs[4:7]
-    front_ref, term_ref, cross_ref = refs[7:10]
-    green_high, green_low, part_high, part_low, left = refs[10:]
+    greens = refs[4:7]
+    parts = refs[7:10]
+    front_ref, term_ref, cross_ref = refs[10:13]
+    green_high, green_low, part_high, part_low, left = refs[13:]
     core, line, spot = place()
     rows = messages[0].shape[2]
     for step in range(4):
         for block in range(4):
             row = block_row(core, line, step, lax.rem(spot - block + 4, 4), rows)
-            ref = messages[block] if step == 0 else rings[step - 1].at[block]
-            store_block(green_high, green_low, row, rows, ref[0, 0], ref[0, 1])
-            store_block(part_high, part_low, row, rows, ref[1, 0], ref[1, 1])
+            green = messages[block].at[0] if step == 0 else greens[step - 1].at[block]
+            factor = messages[block].at[1] if step == 0 else parts[step - 1].at[block]
+            store_block(green_high, green_low, row, rows, green[0], green[1])
+            store_block(part_high, part_low, row, rows, factor[0], factor[1])
     for step in range(4):
         own = pl.multiple_of(lax.rem(spot - step + 4, 4) * rows, rows)
         for part in range(2):
@@ -133,7 +135,7 @@
             piece = slice(block * rows, (block + 1) * rows)
             front_ref[block, part] = panel[piece]
             term_ref[block, part] = other[piece]
-        for step in range(2):
+        for step in (0, 3):
             block = lax.rem(spot - step + 4, 4)
             term_ref[block, part] += jnp.where(outer, 0.0, messages[step][4, part])
         for block in range(4):
@@ -142,9 +144,10 @@
 
 def second_kernel(*refs):
     front_ref, front_there_ref, keep_ref = refs[0:3]
-    chunks = refs[3:7]
-    out_ref = refs[7]
-    pivot_high, pivot_low, panel_high, panel_low = refs[8:]
+    pivots = refs[3:7]
+    panels = refs[7:11]
+    out_ref = refs[11]
+    pivot_high, pivot_low, panel_high, panel_low = refs[12:]
     core, line, spot = place()
     rows = front_ref.shape[2]
     width = front_ref.shape[3]
@@ -156,13 +159,13 @@
     for step in range(4):
         for block in range(4):
             row = block_row(core, line, step, block, rows)
-            block_re = chunks[step][0, block, 0]
-            block_im = chunks[step][0, block, 1]
+            block_re = pivots[step][block, 0]
+            block_im = pivots[step][block, 1]
             on_diagonal = column_iota == row_iota + row
             diag_re += jnp.sum(jnp.where(on_diagonal, block_re, 0.0), axis=0, keepdims=True)
             diag_im += jnp.sum(jnp.where(on_diagonal, block_im, 0.0), axis=0, keepdims=True)
             store_block(pivot_high, pivot_low, row, rows, block_re, block_im)
-            store_block(panel_high, panel_low, row, rows, chunks[step][1, block, 0], chunks[step][1, block, 1])
+            store_block(panel_high, panel_low, row, rows, panels[step][block, 0], panels[step][block, 1])
     modulus = diag_re * diag_re + diag_im * diag_im
     weight_re = diag_re / modulus
     weight_im = -diag_im / modulus
@@ -215,26 +218,30 @@
         with_lower = (there == 0) | (there == 3)
         above = jnp.where(odd == 0, lower[2], next_lower)
         blocks = [green, jnp.where(with_lower, down, up), below, above]
-        return jnp.stack(blocks + [diag_even[1]] if step < 2 else blocks)
-
-    def around(value, move, own):
-        far, near, back = [permuted(value(step), slabs, move(step)) for step in (2, 1, 3)]
-        return [own, near, far, back]
-
-    messages = around(message, along_spot, message(0))
-    whole = jnp.stack([piece[:2] for piece in messages])
-    rings = around(lambda step: whole, along_line, whole)[1:]
+        return jnp.stack(blocks + [diag_even[1]] if step in (0, 3) else blocks)
+
+    def ringed(first, second):
+        first_one = permuted(first, slabs, along_line(1))
+        second_three = permuted(second, slabs, along_line(-1))
+        first_two = permuted(first_one, slabs, along_line(1))
+        second_two = permuted(second_three, slabs, along_line(-1))
+        second_one = permuted(second, slabs, along_line(1))
+        first_three = permuted(first, slabs, along_line(-1))
+        return [first_one, first_two, first_three], [second_one, second_two, second_three]
+
+    messages = [message(0)] + [permuted(message(step), slabs, along_spot(step)) for step in range(1, 4)]
+    greens, parts = ringed(*(jnp.stack([piece[side] for piece in messages]) for side in range(2)))
     four = jax.ShapeDtypeStruct((4, 2, rows, width), jnp.float32)
     wide = pltpu.VMEM((width, 2 * width), jnp.bfloat16)
     front, term, cross = pl.pallas_call(
         first_kernel,
         out_shape=[four] * 3,
-        in_specs=vmem(7),
+        in_specs=vmem(10),
         out_specs=vmem(3),
         scratch_shapes=[wide] * 4 + [pltpu.VMEM((2, 8 * rows, width), jnp.float32)],
         compiler_params=pltpu.CompilerParams(vmem_limit_bytes=VMEM_LIMIT),
         name="first_level",
-    )(*messages, *rings)
+    )(*messages, *greens, *parts)
 
     outer = lax.rem(spot, 2) == 0
     term_there = permuted(term, slabs, inner)
@@ -242,19 +249,18 @@
     cross_there = permuted(cross, slabs, crossed)
     panel = jnp.where(outer, front, cross_there)
     pivot = jnp.where(outer, cross_there + term_out, term + term_there)
-    chunk = jnp.stack([pivot, panel])
-    chunks = around(lambda step: chunk, along_line, chunk)
+    pivots, panels = ringed(pivot, panel)
     after, _ = lax.optimization_barrier((front, term_there))
     front_there = permuted(after, slabs, outwards)
     out = pl.pallas_call(
         second_kernel,
         out_shape=four,
-        in_specs=vmem(7),
+        in_specs=vmem(11),
         out_specs=vmem(1)[0],
         scratch_shapes=[wide] * 4,
         compiler_params=pltpu.CompilerParams(vmem_limit_bytes=VMEM_LIMIT),
         name="second_level",
-    )(front, front_there, term, *chunks)
+    )(front, front_there, term, pivot, *pivots, panel, *panels)
     ends = [permuted(out[step], slabs, to_owner(step)) for step in range(4)]
 
     def ended(code):

time: 181 us -> 156 us (0.86)
  waiting for transfers between devices: 106 us -> 56 us
  starting transfers between devices: 59.5 us -> 85 us
    ppermute x18 -> x24, waiting for transfers between devices: 106 us -> 56 us  [permuted(): return lax.ppermute(value, ('slab', 'orb'), pairs)]
    ppermute x18 -> x24, starting transfers between devices: 59.5 us -> 85 us  [permuted(): return lax.ppermute(value, ('slab', 'orb'), pairs)]
  transfers between devices with their start and end apart: 18 -> 24, of which waited for: 14 -> 15; matrix products, arithmetic and copies ran while one was open for 0% -> 0% of each run, Pallas kernels for 0% -> 0%
where the time goes in v4:
time: 156 us; the launch traced here: 155 us
  starting transfers between devices  85 us (54%)
  waiting for transfers between devices  56 us (36%)
  Pallas kernels  8.99 us (6%)
  local copies, waits for them, and re-layouts  2.51 us (2%)
    ppermute x24, starting transfers between devices, permuted(): return lax.ppermute(value, ('slab', 'orb'), pairs)  85 us
    ppermute x24, waiting for transfers between devices, permuted(): return lax.ppermute(value, ('slab', 'orb'), pairs)  56 us
    pallas_call x1, Pallas kernels, shards(): pl.pallas_call(second_kernel, out_shape=four, in_specs=vmem(11), out_spec...  4.88 us
    pallas_call x1, Pallas kernels, shards(): pl.pallas_call(first_kernel, out_shape=[four] * 3, in_specs=vmem(10), out...  4.11 us
  transfers between devices with their start and end apart: 24, of which 15 were waited for; matrix products, arithmetic and copies ran while one was open for 0% of the time, Pallas kernels for 0%

profile of v4, /device:TPU:4, one launch (start us, length us, event | category | flops | bytes accessed | tf_op | source)
XLA Modules:
  0.0 155.2 jit_solution(17207746462753023363)
XLA Ops:
  0.8 1.3 dynamic-slice_dynamic-update-slice_fusion.1
  2.1 0.0 copy-done
  2.1 0.2 copy-done.1
  2.3 0.1 select_dynamic-update-slice_fusion
  2.4 8.9 %collective-permute-start = (f32[2,32,512]{2,1,0:T(8,128)S(1)}, f32[2,32,512]{2,1,0:T(8,128)S(1)}, u32[]{:S(2)}, u32[]{:S(2)}) collective-permute-start(f32[2,32,512]{2,1,0:T(8,128)S(1)} %get-tuple-element.43), channel_id=1, source_target_pairs={{0,496},{4,500},{8,504},{12,508},{1,497},{5,501},{9,505},{13,509},... | collective-permute-start | bytes 393224 | tf_op jit(solution)/shard_map/ppermute | solution.py:22
  11.4 2.5 %collective-permute-done = f32[2,32,512]{2,1,0:T(8,128)S(1)} collective-permute-done((f32[2,32,512]{2,1,0:T(8,128)S(1)}, f32[2,32,512]{2,1,0:T(8,128)S(1)}, u32[]{:S(2)}, u32[]{:S(2)}) %collective-permute-start) | collective-permute-done | bytes 131104 | tf_op jit(solution)/shard_map/ppermute | solution.py:22
  13.9 5.1 %collective-permute-start.2 = (f32[4,2,32,512]{3,2,1,0:T(8,128)S(1)}, f32[4,2,32,512]{3,2,1,0:T(8,128)S(1)}, u32[]{:S(2)}, u32[]{:S(2)}) collective-permute-start(f32[4,2,32,512]{3,2,1,0:T(8,128)S(1)} %pad_maximum_fusion.1), channel_id=1, source_target_pairs={{0,8},{4,12},{8,0},{12,4},{1,9},{5,13},{9,1},{13,5},{2,10},{6,14},... | collective-permute-start | bytes 1572872 | tf_op jit(solution)/shard_map/ppermute | solution.py:22
  19.1 2.7 %collective-permute-start.1 = (f32[4,2,32,512]{3,2,1,0:T(8,128)S(1)}, f32[4,2,32,512]{3,2,1,0:T(8,128)S(1)}, u32[]{:S(2)}, u32[]{:S(2)}) collective-permute-start(f32[4,2,32,512]{3,2,1,0:T(8,128)S(1)} %pad_maximum_fusion), channel_id=1, source_target_pairs={{0,4},{4,8},{8,12},{12,0},{1,5},{5,9},{9,13},{13,1},{2,6},{6,10},{... | collective-permute-start | bytes 1572872 | tf_op jit(solution)/shard_map/ppermute | solution.py:22
  21.9 0.9 copy-done.2
  22.8 4.5 %collective-permute-start.3 = (f32[5,2,32,512]{3,2,1,0:T(8,128)S(1)}, f32[5,2,32,512]{3,2,1,0:T(8,128)S(1)}, u32[]{:S(2)}, u32[]{:S(2)}) collective-permute-start(f32[5,2,32,512]{3,2,1,0:T(8,128)S(1)} %get-tuple-element.44), channel_id=1, source_target_pairs={{0,12},{4,0},{8,4},{12,8},{1,13},{5,1},{9,5},{13,9},{2,14},{6,2},{... | collective-permute-start | bytes 1966088 | tf_op jit(solution)/shard_map/ppermute | solution.py:22
  27.3 4.8 %collective-permute-done.1.refs_1_ = f32[4,2,32,512]{3,2,1,0:T(8,128)S(1)} collective-permute-done((f32[4,2,32,512]{3,2,1,0:T(8,128)S(1)}, f32[4,2,32,512]{3,2,1,0:T(8,128)S(1)}, u32[]{:S(2)}, u32[]{:S(2)}) %collective-permute-start.1) | collective-permute-done | bytes 524320 | tf_op jit(solution)/shard_map/ppermute | solution.py:22
  32.1 7.6 %collective-permute-done.3.refs_3_ = f32[5,2,32,512]{3,2,1,0:T(8,128)S(1)} collective-permute-done((f32[5,2,32,512]{3,2,1,0:T(8,128)S(1)}, f32[5,2,32,512]{3,2,1,0:T(8,128)S(1)}, u32[]{:S(2)}, u32[]{:S(2)}) %collective-permute-start.3) | collective-permute-done | bytes 655392 | tf_op jit(solution)/shard_map/ppermute | solution.py:22
  39.8 2.4 %collective-permute-start.8 = (f32[4,2,32,512]{3,2,1,0:T(8,128)S(1)}, f32[4,2,32,512]{3,2,1,0:T(8,128)S(1)}, u32[]{:S(2)}, u32[]{:S(2)}) collective-permute-start(f32[4,2,32,512]{3,2,1,0:T(8,128)S(1)} %pad_maximum_fusion.3), channel_id=1, source_target_pairs={{0,3},{4,7},{8,11},{12,15},{1,0},{5,4},{9,8},{13,12},{2,1},{6,5},{... | collective-permute-start | bytes 1572872 | tf_op jit(solution)/shard_map/ppermute | solution.py:22
  42.2 3.5 %collective-permute-start.4 = (f32[4,2,32,512]{3,2,1,0:T(8,128)S(1)}, f32[4,2,32,512]{3,2,1,0:T(8,128)S(1)}, u32[]{:S(2)}, u32[]{:S(2)}) collective-permute-start(f32[4,2,32,512]{3,2,1,0:T(8,128)S(1)} %pad_maximum_fusion.2), channel_id=1, source_target_pairs={{0,1},{4,5},{8,9},{12,13},{1,2},{5,6},{9,10},{13,14},{2,3},{6,7},{... | collective-permute-start | bytes 1572872 | tf_op jit(solution)/shard_map/ppermute | solution.py:22
  45.7 2.6 %collective-permute-start.7 = (f32[4,2,32,512]{3,2,1,0:T(8,128)S(1)}, f32[4,2,32,512]{3,2,1,0:T(8,128)S(1)}, u32[]{:S(2)}, u32[]{:S(2)}) collective-permute-start(f32[4,2,32,512]{3,2,1,0:T(8,128)S(1)} %pad_maximum_fusion.3), channel_id=1, source_target_pairs={{0,1},{4,5},{8,9},{12,13},{1,2},{5,6},{9,10},{13,14},{2,3},{6,7},{... | collective-permute-start | bytes 1572872 | tf_op jit(solution)/shard_map/ppermute | solution.py:22
  48.3 3.3 %collective-permute-start.6 = (f32[4,2,32,512]{3,2,1,0:T(8,128)S(1)}, f32[4,2,32,512]{3,2,1,0:T(8,128)S(1)}, u32[]{:S(2)}, u32[]{:S(2)}) collective-permute-start(f32[4,2,32,512]{3,2,1,0:T(8,128)S(1)} %pad_maximum_fusion.2), channel_id=1, source_target_pairs={{0,3},{4,7},{8,11},{12,15},{1,0},{5,4},{9,8},{13,12},{2,1},{6,5},{... | collective-permute-start | bytes 1572872 | tf_op jit(solution)/shard_map/ppermute | solution.py:22
  51.6 2.4 %collective-permute-start.9 = (f32[4,2,32,512]{3,2,1,0:T(8,128)S(1)}, f32[4,2,32,512]{3,2,1,0:T(8,128)S(1)}, u32[]{:S(2)}, u32[]{:S(2)}) collective-permute-start(f32[4,2,32,512]{3,2,1,0:T(8,128)S(1)} %collective-permute-done.8.refs_9_), channel_id=1, source_target_pairs={{0,3},{4,7},{8,11},{12,15},{1,0},{5,4},{9,8},{13,12},{2,1},{6,5},{... | collective-permute-start | bytes 1572872 | tf_op jit(solution)/shard_map/ppermute | solution.py:22
  54.0 3.5 %collective-permute-start.5 = (f32[4,2,32,512]{3,2,1,0:T(8,128)S(1)}, f32[4,2,32,512]{3,2,1,0:T(8,128)S(1)}, u32[]{:S(2)}, u32[]{:S(2)}) collective-permute-start(f32[4,2,32,512]{3,2,1,0:T(8,128)S(1)} %collective-permute-done.4.refs_4_), channel_id=1, source_target_pairs={{0,1},{4,5},{8,9},{12,13},{1,2},{5,6},{9,10},{13,14},{2,3},{6,7},{... | collective-permute-start | bytes 1572872 | tf_op jit(solution)/shard_map/ppermute | solution.py:22
  57.4 1.5 collective-permute-done.7.refs_7_
  58.9 0.4 collective-permute-done.6.refs_6_
  59.4 5.6 %collective-permute-done.9.refs_8_ = f32[4,2,32,512]{3,2,1,0:T(8,128)S(1)} collective-permute-done((f32[4,2,32,512]{3,2,1,0:T(8,128)S(1)}, f32[4,2,32,512]{3,2,1,0:T(8,128)S(1)}, u32[]{:S(2)}, u32[]{:S(2)}) %collective-permute-start.9) | collective-permute-done | bytes 524320 | tf_op jit(solution)/shard_map/ppermute | solution.py:22
  65.0 0.1 collective-permute-done.5.refs_5_
  65.0 4.1 %first_level.1 = (f32[4,2,32,512]{3,2,1,0:T(8,128)S(1)}, f32[4,2,32,512]{3,2,1,0:T(8,128)S(1)}, f32[4,2,32,512]{3,2,1,0:T(8,128)S(1)}) custom-call(f32[5,2,32,512]{3,2,1,0:T(8,128)S(1)} %get-tuple-element.45.refs_0_, f32[4,2,32,512]{3,2,1,0:T(8,128)S(1)} %collective-permute-done.1.refs_1_, f32[4,2,32,512]{3,2,1,0:T(8,128)S(1)} %collective-permute-done.2.refs_2_, ...), custom_call_target="tpu_custom_call" | custom-call | tf_op jit(solution)/shard_map/first_level/pallas_call | solution.py:236
  69.2 0.7 collective-permute-start.10
  69.9 8.9 %collective-permute-start.12 = (f32[4,2,32,512]{3,2,1,0:T(8,128)S(1)}, f32[4,2,32,512]{3,2,1,0:T(8,128)S(1)}, u32[]{:S(2)}, u32[]{:S(2)}) collective-permute-start(f32[4,2,32,512]{3,2,1,0:T(8,128)S(1)} %get-tuple-element.10), channel_id=1, source_target_pairs={{0,12},{4,8},{8,4},{12,0},{1,13},{5,9},{9,5},{13,1},{2,14},{6,10},... | collective-permute-start | bytes 1572872 | tf_op jit(solution)/shard_map/ppermute | solution.py:22
  78.8 1.3 collective-permute-start.13
  80.1 14.0 %collective-permute-done.12 = f32[4,2,32,512]{3,2,1,0:T(8,128)S(1)} collective-permute-done((f32[4,2,32,512]{3,2,1,0:T(8,128)S(1)}, f32[4,2,32,512]{3,2,1,0:T(8,128)S(1)}, u32[]{:S(2)}, u32[]{:S(2)}) %collective-permute-start.12) | collective-permute-done | bytes 524320 | tf_op jit(solution)/shard_map/ppermute | solution.py:22
  94.1 2.6 %collective-permute-done.13 = f32[4,2,32,512]{3,2,1,0:T(8,128)S(1)} collective-permute-done((f32[4,2,32,512]{3,2,1,0:T(8,128)S(1)}, f32[4,2,32,512]{3,2,1,0:T(8,128)S(1)}, u32[]{:S(2)}, u32[]{:S(2)}) %collective-permute-start.13) | collective-permute-done | bytes 524320 | tf_op jit(solution)/shard_map/ppermute | solution.py:22
  96.7 0.3 broadcast_select_fusion
  97.0 10.4 %collective-permute-start.14 = (f32[4,2,32,512]{3,2,1,0:T(8,128)S(1)}, f32[4,2,32,512]{3,2,1,0:T(8,128)S(1)}, u32[]{:S(2)}, u32[]{:S(2)}) collective-permute-start(f32[4,2,32,512]{3,2,1,0:T(8,128)S(1)} %get-tuple-element.34.refs_3_), channel_id=1, source_target_pairs={{0,1},{4,5},{8,9},{12,13},{1,2},{5,6},{9,10},{13,14},{2,3},{6,7},{... | collective-permute-start | bytes 1572872 | tf_op jit(solution)/shard_map/ppermute | solution.py:22
  107.5 2.2 %collective-permute-start.18 = (f32[4,2,32,512]{3,2,1,0:T(8,128)S(1)}, f32[4,2,32,512]{3,2,1,0:T(8,128)S(1)}, u32[]{:S(2)}, u32[]{:S(2)}) collective-permute-start(f32[4,2,32,512]{3,2,1,0:T(8,128)S(1)} %get-tuple-element.33.refs_7_), channel_id=1, source_target_pairs={{0,3},{4,7},{8,11},{12,15},{1,0},{5,4},{9,8},{13,12},{2,1},{6,5},{... | collective-permute-start | bytes 1572872 | tf_op jit(solution)/shard_map/ppermute | solution.py:22
  109.7 3.9 %collective-permute-start.16 = (f32[4,2,32,512]{3,2,1,0:T(8,128)S(1)}, f32[4,2,32,512]{3,2,1,0:T(8,128)S(1)}, u32[]{:S(2)}, u32[]{:S(2)}) collective-permute-start(f32[4,2,32,512]{3,2,1,0:T(8,128)S(1)} %get-tuple-element.34.refs_3_), channel_id=1, source_target_pairs={{0,3},{4,7},{8,11},{12,15},{1,0},{5,4},{9,8},{13,12},{2,1},{6,5},{... | collective-permute-start | bytes 1572872 | tf_op jit(solution)/shard_map/ppermute | solution.py:22
  113.6 1.9 %collective-permute-start.17 = (f32[4,2,32,512]{3,2,1,0:T(8,128)S(1)}, f32[4,2,32,512]{3,2,1,0:T(8,128)S(1)}, u32[]{:S(2)}, u32[]{:S(2)}) collective-permute-start(f32[4,2,32,512]{3,2,1,0:T(8,128)S(1)} %get-tuple-element.33.refs_7_), channel_id=1, source_target_pairs={{0,1},{4,5},{8,9},{12,13},{1,2},{5,6},{9,10},{13,14},{2,3},{6,7},{... | collective-permute-start | bytes 1572872 | tf_op jit(solution)/shard_map/ppermute | solution.py:22
  115.5 1.3 collective-permute-start.11
  116.8 4.9 %collective-permute-start.15 = (f32[4,2,32,512]{3,2,1,0:T(8,128)S(1)}, f32[4,2,32,512]{3,2,1,0:T(8,128)S(1)}, u32[]{:S(2)}, u32[]{:S(2)}) collective-permute-start(f32[4,2,32,512]{3,2,1,0:T(8,128)S(1)} %collective-permute-done.14.refs_4_), channel_id=1, source_target_pairs={{0,1},{4,5},{8,9},{12,13},{1,2},{5,6},{9,10},{13,14},{2,3},{6,7},{... | collective-permute-start | bytes 1572872 | tf_op jit(solution)/shard_map/ppermute | solution.py:22
  121.7 1.9 %collective-permute-start.19 = (f32[4,2,32,512]{3,2,1,0:T(8,128)S(1)}, f32[4,2,32,512]{3,2,1,0:T(8,128)S(1)}, u32[]{:S(2)}, u32[]{:S(2)}) collective-permute-start(f32[4,2,32,512]{3,2,1,0:T(8,128)S(1)} %collective-permute-done.18.refs_10_), channel_id=1, source_target_pairs={{0,3},{4,7},{8,11},{12,15},{1,0},{5,4},{9,8},{13,12},{2,1},{6,5},{... | collective-permute-start | bytes 1572872 | tf_op jit(solution)/shard_map/ppermute | solution.py:22
  123.7 0.5 collective-permute-done.16.refs_6_
  124.2 0.7 collective-permute-done.17.refs_8_
  124.9 1.7 %collective-permute-done.11.refs_1_ = f32[4,2,32,512]{3,2,1,0:T(8,128)S(1)} collective-permute-done((f32[4,2,32,512]{3,2,1,0:T(8,128)S(1)}, f32[4,2,32,512]{3,2,1,0:T(8,128)S(1)}, u32[]{:S(2)}, u32[]{:S(2)}) %collective-permute-start.11) | collective-permute-done | bytes 524320 | tf_op jit(solution)/shard_map/ppermute | solution.py:22
  126.6 6.5 %collective-permute-done.15.refs_5_ = f32[4,2,32,512]{3,2,1,0:T(8,128)S(1)} collective-permute-done((f32[4,2,32,512]{3,2,1,0:T(8,128)S(1)}, f32[4,2,32,512]{3,2,1,0:T(8,128)S(1)}, u32[]{:S(2)}, u32[]{:S(2)}) %collective-permute-start.15) | collective-permute-done | bytes 524320 | tf_op jit(solution)/shard_map/ppermute | solution.py:22
  133.1 4.9 %second_level.1 = f32[4,2,32,512]{3,2,1,0:T(8,128)S(1)} custom-call(f32[4,2,32,512]{3,2,1,0:T(8,128)S(1)} %get-tuple-element.9.refs_0_, f32[4,2,32,512]{3,2,1,0:T(8,128)S(1)} %collective-permute-done.11.refs_1_, f32[4,2,32,512]{3,2,1,0:T(8,128)S(1)} %get-tuple-element.8.refs_2_, f32[4,2,32,512]{3,2,1,0:T(8,128)S(1)} %get-tuple-element.34.refs_3_, ...), custom_call_target="tpu_custom_call" | custom-call | tf_op jit(solution)/shard_map/second_level/pallas_call | solution.py:255
  138.0 4.3 %collective-permute-start.20 = (f32[2,32,512]{2,1,0:T(8,128)S(1)}, f32[2,32,512]{2,1,0:T(8,128)S(1)}, u32[]{:S(2)}, u32[]{:S(2)}) collective-permute-start(f32[2,32,512]{2,1,0:T(8,128)S(1)} %get-tuple-element.32), channel_id=1, source_target_pairs={{0,12},{4,0},{8,20},{12,24},{1,9},{5,13},{9,17},{13,21},{2,6},{6,1... | collective-permute-start | bytes 393224 | tf_op jit(solution)/shard_map/ppermute | solution.py:22
  142.3 0.7 collective-permute-start.21
  143.0 1.9 %collective-permute-start.22 = (f32[2,32,512]{2,1,0:T(8,128)S(1)}, f32[2,32,512]{2,1,0:T(8,128)S(1)}, u32[]{:S(2)}, u32[]{:S(2)}) collective-permute-start(f32[2,32,512]{2,1,0:T(8,128)S(1)} %get-tuple-element.30), channel_id=1, source_target_pairs={{0,4},{4,8},{8,28},{12,16},{1,1},{5,5},{9,25},{13,29},{2,14},{6,2}... | collective-permute-start | bytes 393224 | tf_op jit(solution)/shard_map/ppermute | solution.py:22
  144.9 1.9 %collective-permute-start.23 = (f32[2,32,512]{2,1,0:T(8,128)S(1)}, f32[2,32,512]{2,1,0:T(8,128)S(1)}, u32[]{:S(2)}, u32[]{:S(2)}) collective-permute-start(f32[2,32,512]{2,1,0:T(8,128)S(1)} %get-tuple-element.29), channel_id=1, source_target_pairs={{0,0},{4,4},{8,24},{12,28},{1,13},{5,1},{9,21},{13,25},{2,10},{6,1... | collective-permute-start | bytes 393224 | tf_op jit(solution)/shard_map/ppermute | solution.py:22
  146.9 2.9 %collective-permute-done.22 = f32[2,32,512]{2,1,0:T(8,128)S(1)} collective-permute-done((f32[2,32,512]{2,1,0:T(8,128)S(1)}, f32[2,32,512]{2,1,0:T(8,128)S(1)}, u32[]{:S(2)}, u32[]{:S(2)}) %collective-permute-start.22) | collective-permute-done | bytes 131104 | tf_op jit(solution)/shard_map/ppermute | solution.py:22
  149.9 4.5 %collective-permute-done.23 = f32[2,32,512]{2,1,0:T(8,128)S(1)} collective-permute-done((f32[2,32,512]{2,1,0:T(8,128)S(1)}, f32[2,32,512]{2,1,0:T(8,128)S(1)}, u32[]{:S(2)}, u32[]{:S(2)}) %collective-permute-start.23) | collective-permute-done | bytes 131104 | tf_op jit(solution)/shard_map/ppermute | solution.py:22
  154.4 0.8 select_bitcast_fusion
  (28 shorter events, 0.4 us)
Async XLA Ops:
  0.8 1.3 copy-start
  0.8 1.4 copy-start.1
  2.4 11.5 %collective-permute-start = (f32[2,32,512]{2,1,0:T(8,128)S(1)}, f32[2,32,512]{2,1,0:T(8,128)S(1)}, u32[]{:S(2)}, u32[]{:S(2)}) collective-permute-start(f32[2,32,512]{2,1,0:T(8,128)S(1)} %get-tuple-element.43), channel_id=1, source_target_pairs={{0,496},{4,500},{8,504},{12,508},{1,497},{5,501},{9,505},{13,509},... | collective-permute-start | bytes 393224 | tf_op jit(solution)/shard_map/ppermute | solution.py:22
  11.3 2.6 %copy-start.3 = (f32[5,2,32,512]{3,2,1,0:T(8,128)}, f32[5,2,32,512]{3,2,1,0:T(8,128)S(1)}, u32[]{:S(2)}) copy-start(f32[5,2,32,512]{3,2,1,0:T(8,128)S(1)} %get-tuple-element.39) | copy-start | bytes 1966084
  13.9 13.4 %collective-permute-start.2 = (f32[4,2,32,512]{3,2,1,0:T(8,128)S(1)}, f32[4,2,32,512]{3,2,1,0:T(8,128)S(1)}, u32[]{:S(2)}, u32[]{:S(2)}) collective-permute-start(f32[4,2,32,512]{3,2,1,0:T(8,128)S(1)} %pad_maximum_fusion.1), channel_id=1, source_target_pairs={{0,8},{4,12},{8,0},{12,4},{1,9},{5,13},{9,1},{13,5},{2,10},{6,14},... | collective-permute-start | bytes 1572872 | tf_op jit(solution)/shard_map/ppermute | solution.py:22
  19.0 2.8 %copy-start.4 = (f32[5,2,32,512]{3,2,1,0:T(8,128)S(1)}, f32[5,2,32,512]{3,2,1,0:T(8,128)}, u32[]{:S(2)}) copy-start(f32[5,2,32,512]{3,2,1,0:T(8,128)} %copy-done.3) | copy-start | bytes 1966084
  19.1 13.0 %collective-permute-start.1 = (f32[4,2,32,512]{3,2,1,0:T(8,128)S(1)}, f32[4,2,32,512]{3,2,1,0:T(8,128)S(1)}, u32[]{:S(2)}, u32[]{:S(2)}) collective-permute-start(f32[4,2,32,512]{3,2,1,0:T(8,128)S(1)} %pad_maximum_fusion), channel_id=1, source_target_pairs={{0,4},{4,8},{8,12},{12,0},{1,5},{5,9},{9,13},{13,1},{2,6},{6,10},{... | collective-permute-start | bytes 1572872 | tf_op jit(solution)/shard_map/ppermute | solution.py:22
  21.8 1.0 copy-start.2
  22.8 16.9 %collective-permute-start.3 = (f32[5,2,32,512]{3,2,1,0:T(8,128)S(1)}, f32[5,2,32,512]{3,2,1,0:T(8,128)S(1)}, u32[]{:S(2)}, u32[]{:S(2)}) collective-permute-start(f32[5,2,32,512]{3,2,1,0:T(8,128)S(1)} %get-tuple-element.44), channel_id=1, source_target_pairs={{0,12},{4,0},{8,4},{12,8},{1,13},{5,1},{9,5},{13,9},{2,14},{6,2},{... | collective-permute-start | bytes 1966088 | tf_op jit(solution)/shard_map/ppermute | solution.py:22
  39.8 11.8 %collective-permute-start.8 = (f32[4,2,32,512]{3,2,1,0:T(8,128)S(1)}, f32[4,2,32,512]{3,2,1,0:T(8,128)S(1)}, u32[]{:S(2)}, u32[]{:S(2)}) collective-permute-start(f32[4,2,32,512]{3,2,1,0:T(8,128)S(1)} %pad_maximum_fusion.3), channel_id=1, source_target_pairs={{0,3},{4,7},{8,11},{12,15},{1,0},{5,4},{9,8},{13,12},{2,1},{6,5},{... | collective-permute-start | bytes 1572872 | tf_op jit(solution)/shard_map/ppermute | solution.py:22
  42.2 11.7 %collective-permute-start.4 = (f32[4,2,32,512]{3,2,1,0:T(8,128)S(1)}, f32[4,2,32,512]{3,2,1,0:T(8,128)S(1)}, u32[]{:S(2)}, u32[]{:S(2)}) collective-permute-start(f32[4,2,32,512]{3,2,1,0:T(8,128)S(1)} %pad_maximum_fusion.2), channel_id=1, source_target_pairs={{0,1},{4,5},{8,9},{12,13},{1,2},{5,6},{9,10},{13,14},{2,3},{6,7},{... | collective-permute-start | bytes 1572872 | tf_op jit(solution)/shard_map/ppermute | solution.py:22
  45.7 13.2 %collective-permute-start.7 = (f32[4,2,32,512]{3,2,1,0:T(8,128)S(1)}, f32[4,2,32,512]{3,2,1,0:T(8,128)S(1)}, u32[]{:S(2)}, u32[]{:S(2)}) collective-permute-start(f32[4,2,32,512]{3,2,1,0:T(8,128)S(1)} %pad_maximum_fusion.3), channel_id=1, source_target_pairs={{0,1},{4,5},{8,9},{12,13},{1,2},{5,6},{9,10},{13,14},{2,3},{6,7},{... | collective-permute-start | bytes 1572872 | tf_op jit(solution)/shard_map/ppermute | solution.py:22
  48.3 11.1 %collective-permute-start.6 = (f32[4,2,32,512]{3,2,1,0:T(8,128)S(1)}, f32[4,2,32,512]{3,2,1,0:T(8,128)S(1)}, u32[]{:S(2)}, u32[]{:S(2)}) collective-permute-start(f32[4,2,32,512]{3,2,1,0:T(8,128)S(1)} %pad_maximum_fusion.2), channel_id=1, source_target_pairs={{0,3},{4,7},{8,11},{12,15},{1,0},{5,4},{9,8},{13,12},{2,1},{6,5},{... | collective-permute-start | bytes 1572872 | tf_op jit(solution)/shard_map/ppermute | solution.py:22
  51.6 13.4 %collective-permute-start.9 = (f32[4,2,32,512]{3,2,1,0:T(8,128)S(1)}, f32[4,2,32,512]{3,2,1,0:T(8,128)S(1)}, u32[]{:S(2)}, u32[]{:S(2)}) collective-permute-start(f32[4,2,32,512]{3,2,1,0:T(8,128)S(1)} %collective-permute-done.8.refs_9_), channel_id=1, source_target_pairs={{0,3},{4,7},{8,11},{12,15},{1,0},{5,4},{9,8},{13,12},{2,1},{6,5},{... | collective-permute-start | bytes 1572872 | tf_op jit(solution)/shard_map/ppermute | solution.py:22
  54.0 11.1 %collective-permute-start.5 = (f32[4,2,32,512]{3,2,1,0:T(8,128)S(1)}, f32[4,2,32,512]{3,2,1,0:T(8,128)S(1)}, u32[]{:S(2)}, u32[]{:S(2)}) collective-permute-start(f32[4,2,32,512]{3,2,1,0:T(8,128)S(1)} %collective-permute-done.4.refs_4_), channel_id=1, source_target_pairs={{0,1},{4,5},{8,9},{12,13},{1,2},{5,6},{9,10},{13,14},{2,3},{6,7},{... | collective-permute-start | bytes 1572872 | tf_op jit(solution)/shard_map/ppermute | solution.py:22
  69.2 11.0 %collective-permute-start.10 = (f32[4,2,32,512]{3,2,1,0:T(8,128)S(1)}, f32[4,2,32,512]{3,2,1,0:T(8,128)S(1)}, u32[]{:S(2)}, u32[]{:S(2)}) collective-permute-start(f32[4,2,32,512]{3,2,1,0:T(8,128)S(1)} %get-tuple-element.8.refs_2_), channel_id=1, source_target_pairs={{4,12},{12,4},{5,13},{13,5},{6,14},{14,6},{7,15},{15,7},{17,19},{1... | collective-permute-start | bytes 1572872 | tf_op jit(solution)/shard_map/ppermute | solution.py:22
  69.9 24.3 %collective-permute-start.12 = (f32[4,2,32,512]{3,2,1,0:T(8,128)S(1)}, f32[4,2,32,512]{3,2,1,0:T(8,128)S(1)}, u32[]{:S(2)}, u32[]{:S(2)}) collective-permute-start(f32[4,2,32,512]{3,2,1,0:T(8,128)S(1)} %get-tuple-element.10), channel_id=1, source_target_pairs={{0,12},{4,8},{8,4},{12,0},{1,13},{5,9},{9,5},{13,1},{2,14},{6,10},... | collective-permute-start | bytes 1572872 | tf_op jit(solution)/shard_map/ppermute | solution.py:22
  78.8 17.9 %collective-permute-start.13 = (f32[4,2,32,512]{3,2,1,0:T(8,128)S(1)}, f32[4,2,32,512]{3,2,1,0:T(8,128)S(1)}, u32[]{:S(2)}, u32[]{:S(2)}) collective-permute-start(f32[4,2,32,512]{3,2,1,0:T(8,128)S(1)} %get-tuple-element.8.refs_2_), channel_id=1, source_target_pairs={{4,0},{12,8},{5,1},{13,9},{6,2},{14,10},{7,3},{15,11},{17,16},{19,... | collective-permute-start | bytes 1572872 | tf_op jit(solution)/shard_map/ppermute | solution.py:22
  97.0 19.8 %collective-permute-start.14 = (f32[4,2,32,512]{3,2,1,0:T(8,128)S(1)}, f32[4,2,32,512]{3,2,1,0:T(8,128)S(1)}, u32[]{:S(2)}, u32[]{:S(2)}) collective-permute-start(f32[4,2,32,512]{3,2,1,0:T(8,128)S(1)} %get-tuple-element.34.refs_3_), channel_id=1, source_target_pairs={{0,1},{4,5},{8,9},{12,13},{1,2},{5,6},{9,10},{13,14},{2,3},{6,7},{... | collective-permute-start | bytes 1572872 | tf_op jit(solution)/shard_map/ppermute | solution.py:22
  107.5 14.2 %collective-permute-start.18 = (f32[4,2,32,512]{3,2,1,0:T(8,128)S(1)}, f32[4,2,32,512]{3,2,1,0:T(8,128)S(1)}, u32[]{:S(2)}, u32[]{:S(2)}) collective-permute-start(f32[4,2,32,512]{3,2,1,0:T(8,128)S(1)} %get-tuple-element.33.refs_7_), channel_id=1, source_target_pairs={{0,3},{4,7},{8,11},{12,15},{1,0},{5,4},{9,8},{13,12},{2,1},{6,5},{... | collective-permute-start | bytes 1572872 | tf_op jit(solution)/shard_map/ppermute | solution.py:22
  109.7 14.5 %collective-permute-start.16 = (f32[4,2,32,512]{3,2,1,0:T(8,128)S(1)}, f32[4,2,32,512]{3,2,1,0:T(8,128)S(1)}, u32[]{:S(2)}, u32[]{:S(2)}) collective-permute-start(f32[4,2,32,512]{3,2,1,0:T(8,128)S(1)} %get-tuple-element.34.refs_3_), channel_id=1, source_target_pairs={{0,3},{4,7},{8,11},{12,15},{1,0},{5,4},{9,8},{13,12},{2,1},{6,5},{... | collective-permute-start | bytes 1572872 | tf_op jit(solution)/shard_map/ppermute | solution.py:22
  113.6 11.3 %collective-permute-start.17 = (f32[4,2,32,512]{3,2,1,0:T(8,128)S(1)}, f32[4,2,32,512]{3,2,1,0:T(8,128)S(1)}, u32[]{:S(2)}, u32[]{:S(2)}) collective-permute-start(f32[4,2,32,512]{3,2,1,0:T(8,128)S(1)} %get-tuple-element.33.refs_7_), channel_id=1, source_target_pairs={{0,1},{4,5},{8,9},{12,13},{1,2},{5,6},{9,10},{13,14},{2,3},{6,7},{... | collective-permute-start | bytes 1572872 | tf_op jit(solution)/shard_map/ppermute | solution.py:22
  115.5 11.1 %collective-permute-start.11 = (f32[4,2,32,512]{3,2,1,0:T(8,128)S(1)}, f32[4,2,32,512]{3,2,1,0:T(8,128)S(1)}, u32[]{:S(2)}, u32[]{:S(2)}) collective-permute-start(f32[4,2,32,512]{3,2,1,0:T(8,128)S(1)} %get-tuple-element.9.refs_0_), channel_id=1, source_target_pairs={{4,0},{12,8},{5,1},{13,9},{6,2},{14,10},{7,3},{15,11},{17,16},{19,... | collective-permute-start | bytes 1572872 | tf_op jit(solution)/shard_map/ppermute | solution.py:22
  116.8 16.3 %collective-permute-start.15 = (f32[4,2,32,512]{3,2,1,0:T(8,128)S(1)}, f32[4,2,32,512]{3,2,1,0:T(8,128)S(1)}, u32[]{:S(2)}, u32[]{:S(2)}) collective-permute-start(f32[4,2,32,512]{3,2,1,0:T(8,128)S(1)} %collective-permute-done.14.refs_4_), channel_id=1, source_target_pairs={{0,1},{4,5},{8,9},{12,13},{1,2},{5,6},{9,10},{13,14},{2,3},{6,7},{... | collective-permute-start | bytes 1572872 | tf_op jit(solution)/shard_map/ppermute | solution.py:22
  121.7 11.4 %collective-permute-start.19 = (f32[4,2,32,512]{3,2,1,0:T(8,128)S(1)}, f32[4,2,32,512]{3,2,1,0:T(8,128)S(1)}, u32[]{:S(2)}, u32[]{:S(2)}) collective-permute-start(f32[4,2,32,512]{3,2,1,0:T(8,128)S(1)} %collective-permute-done.18.refs_10_), channel_id=1, source_target_pairs={{0,3},{4,7},{8,11},{12,15},{1,0},{5,4},{9,8},{13,12},{2,1},{6,5},{... | collective-permute-start | bytes 1572872 | tf_op jit(solution)/shard_map/ppermute | solution.py:22
  138.0 8.9 %collective-permute-start.20 = (f32[2,32,512]{2,1,0:T(8,128)S(1)}, f32[2,32,512]{2,1,0:T(8,128)S(1)}, u32[]{:S(2)}, u32[]{:S(2)}) collective-permute-start(f32[2,32,512]{2,1,0:T(8,128)S(1)} %get-tuple-element.32), channel_id=1, source_target_pairs={{0,12},{4,0},{8,20},{12,24},{1,9},{5,13},{9,17},{13,21},{2,6},{6,1... | collective-permute-start | bytes 393224 | tf_op jit(solution)/shard_map/ppermute | solution.py:22
  142.3 4.6 %collective-permute-start.21 = (f32[2,32,512]{2,1,0:T(8,128)S(1)}, f32[2,32,512]{2,1,0:T(8,128)S(1)}, u32[]{:S(2)}, u32[]{:S(2)}) collective-permute-start(f32[2,32,512]{2,1,0:T(8,128)S(1)} %get-tuple-element.31), channel_id=1, source_target_pairs={{0,8},{4,12},{8,16},{12,20},{1,5},{5,9},{9,29},{13,17},{2,2},{6,6}... | collective-permute-start | bytes 393224 | tf_op jit(solution)/shard_map/ppermute | solution.py:22
  143.0 6.9 %collective-permute-start.22 = (f32[2,32,512]{2,1,0:T(8,128)S(1)}, f32[2,32,512]{2,1,0:T(8,128)S(1)}, u32[]{:S(2)}, u32[]{:S(2)}) collective-permute-start(f32[2,32,512]{2,1,0:T(8,128)S(1)} %get-tuple-element.30), channel_id=1, source_target_pairs={{0,4},{4,8},{8,28},{12,16},{1,1},{5,5},{9,25},{13,29},{2,14},{6,2}... | collective-permute-start | bytes 393224 | tf_op jit(solution)/shard_map/ppermute | solution.py:22
  144.9 9.5 %collective-permute-start.23 = (f32[2,32,512]{2,1,0:T(8,128)S(1)}, f32[2,32,512]{2,1,0:T(8,128)S(1)}, u32[]{:S(2)}, u32[]{:S(2)}) collective-permute-start(f32[2,32,512]{2,1,0:T(8,128)S(1)} %get-tuple-element.29), channel_id=1, source_target_pairs={{0,0},{4,4},{8,24},{12,28},{1,13},{5,1},{9,21},{13,25},{2,10},{6,1... | collective-permute-start | bytes 393224 | tf_op jit(solution)/shard_map/ppermute | solution.py:22

commit v5 on v4

--- a/solution.py
+++ b/solution.py
@@ -47,13 +47,17 @@
     return (slab, orb(slab, line, spot + 2)) if spot % 2 else None
 
 
-def slab_below(slab, line, spot):
-    return slab - 1, orb(slab, line, spot)
-
-
 def to_owner(step):
     def target(slab, line, spot):
         return slab + spot // 2, orb(slab, line, step + spot - line)
+
+    return target
+
+
+def from_owner(step):
+    def target(slab, line, spot):
+        code = (line + spot - step) % 4
+        return (slab, orb(slab, line, code)) if code < 2 else (slab - 1, orb(slab - 1, spot, code))
 
     return target
 
@@ -103,10 +107,11 @@
 
 def first_kernel(*refs):
     messages = refs[0:4]
-    greens = refs[4:7]
-    parts = refs[7:10]
-    front_ref, term_ref, cross_ref = refs[10:13]
-    green_high, green_low, part_high, part_low, left = refs[13:]
+    aboves = refs[4:8]
+    greens = refs[8:11]
+    parts = refs[11:14]
+    front_ref, term_ref, cross_ref = refs[14:17]
+    green_high, green_low, part_high, part_low, left = refs[17:]
     core, line, spot = place()
     rows = messages[0].shape[2]
     for step in range(4):
@@ -118,9 +123,10 @@
             store_block(part_high, part_low, row, rows, factor[0], factor[1])
     for step in range(4):
         own = pl.multiple_of(lax.rem(spot - step + 4, 4) * rows, rows)
+        there = pl.multiple_of(lax.rem(step + spot - line + 4, 4) * rows, rows)
         for part in range(2):
             left[part, pl.ds(own, rows), :] = messages[step][2, part]
-            left[part, pl.ds(4 * rows + own, rows), :] = messages[step][3, part]
+            left[part, pl.ds(4 * rows + there, rows), :] = aboves[step][part]
     middle_re, middle_im = product(left[0], left[1], green_high[...], green_low[...])
     out_re, out_im = product(middle_re, middle_im, part_high[...], part_low[...])
     count = 4 * rows
@@ -137,7 +143,7 @@
             term_ref[block, part] = other[piece]
         for step in (0, 3):
             block = lax.rem(spot - step + 4, 4)
-            term_ref[block, part] += jnp.where(outer, 0.0, messages[step][4, part])
+            term_ref[block, part] += jnp.where(outer, 0.0, messages[step][3, part])
         for block in range(4):
             cross_ref[block, part] = jnp.where(outer, front_ref[block, part], term_ref[block, part])
 
@@ -206,8 +212,6 @@
     width = lower.shape[3]
     slabs = lax.axis_size("slab")
     core, line, spot = place()
-    next_lower = permuted(lower[0], slabs, slab_below)
-
     def message(step):
         there = lax.rem(spot + step, 4)
         odd = lax.div(there, 2)
@@ -216,8 +220,7 @@
         up = lax.dynamic_index_in_dim(upper, 2 * odd + 1, 0, False)
         below = lax.dynamic_index_in_dim(upper, 2 * odd, 0, False)
         with_lower = (there == 0) | (there == 3)
-        above = jnp.where(odd == 0, lower[2], next_lower)
-        blocks = [green, jnp.where(with_lower, down, up), below, above]
+        blocks = [green, jnp.where(with_lower, down, up), below]
         return jnp.stack(blocks + [diag_even[1]] if step in (0, 3) else blocks)
 
     def ringed(first, second):
@@ -230,18 +233,25 @@
         return [first_one, first_two, first_three], [second_one, second_two, second_three]
 
     messages = [message(0)] + [permuted(message(step), slabs, along_spot(step)) for step in range(1, 4)]
-    greens, parts = ringed(*(jnp.stack([piece[side] for piece in messages]) for side in range(2)))
+    first, second = (jnp.stack([piece[side] for piece in messages]) for side in range(2))
+    greens, parts = ringed(first, second)
+    own_row, next_row, _ = lax.optimization_barrier((lower[2], lower[0], greens[0]))
+
+    def above(step):
+        return jnp.where(lax.rem(line + spot - step + 4, 4) < 2, own_row, next_row)
+
+    aboves = [permuted(above(step), slabs, from_owner(step)) for step in range(4)]
     four = jax.ShapeDtypeStruct((4, 2, rows, width), jnp.float32)
     wide = pltpu.VMEM((width, 2 * width), jnp.bfloat16)
     front, term, cross = pl.pallas_call(
         first_kernel,
         out_shape=[four] * 3,
-        in_specs=vmem(10),
+        in_specs=vmem(14),
         out_specs=vmem(3),
         scratch_shapes=[wide] * 4 + [pltpu.VMEM((2, 8 * rows, width), jnp.float32)],
         compiler_params=pltpu.CompilerParams(vmem_limit_bytes=VMEM_LIMIT),
         name="first_level",
-    )(*messages, *greens, *parts)
+    )(*messages, *aboves, *greens, *parts)
 
     outer = lax.rem(spot, 2) == 0
     term_there = permuted(term, slabs, inner)

time: 156 us -> 153 us (0.981)
  the two profiles are of different devices: /device:TPU:4 before, /device:TPU:16 now
where the time goes in v5:
time: 153 us; the launch traced here: 152 us
  starting transfers between devices  91 us (59%)
  waiting for transfers between devices  40 us (26%)
  Pallas kernels  11.1 us (7%)
  local copies, waits for them, and re-layouts  4.43 us (3%)
  other arithmetic  4.23 us (3%)
    ppermute x27, starting transfers between devices, permuted(): return lax.ppermute(value, ('slab', 'orb'), pairs)  91 us
    ppermute x27, waiting for transfers between devices, permuted(): return lax.ppermute(value, ('slab', 'orb'), pairs)  40 us
    pallas_call x1, Pallas kernels, shards(): pl.pallas_call(first_kernel, out_shape=[four] * 3, in_specs=vmem(14), out...  6.24 us
    pallas_call x1, Pallas kernels, shards(): pl.pallas_call(second_kernel, out_shape=four, in_specs=vmem(11), out_spec...  4.87 us
    unnamed x16, local copies, waits for them, and re-layouts  3.09 us
  transfers between devices with their start and end apart: 27, of which 12 were waited for; matrix products, arithmetic and copies ran while one was open for 1% of the time, Pallas kernels for 0%

profile of v5, /device:TPU:16, one launch (start us, length us, event | category | flops | bytes accessed | tf_op | source)
XLA Modules:
  0.0 152.1 jit_solution(8498176626637531329)
XLA Ops:
  0.8 1.2 constant_dynamic-slice_fusion.1
  2.2 0.9 dynamic-slice_select_fusion
  3.1 3.2 %collective-permute-start = (f32[3,2,32,512]{3,2,1,0:T(8,128)S(1)}, f32[3,2,32,512]{3,2,1,0:T(8,128)S(1)}, u32[]{:S(2)}, u32[]{:S(2)}) collective-permute-start(f32[3,2,32,512]{3,2,1,0:T(8,128)S(1)} %pad_maximum_fusion.5), channel_id=1, source_target_pairs={{0,4},{4,8},{8,12},{12,0},{1,5},{5,9},{9,13},{13,1},{2,6},{6,10},{... | collective-permute-start | bytes 1179656 | tf_op jit(solution)/shard_map/ppermute | solution.py:22
  6.4 6.5 %collective-permute-start.1 = (f32[3,2,32,512]{3,2,1,0:T(8,128)S(1)}, f32[3,2,32,512]{3,2,1,0:T(8,128)S(1)}, u32[]{:S(2)}, u32[]{:S(2)}) collective-permute-start(f32[3,2,32,512]{3,2,1,0:T(8,128)S(1)} %pad_maximum_fusion.6), channel_id=1, source_target_pairs={{0,8},{4,12},{8,0},{12,4},{1,9},{5,13},{9,1},{13,5},{2,10},{6,14},... | collective-permute-start | bytes 1179656 | tf_op jit(solution)/shard_map/ppermute | solution.py:22
  12.9 4.5 %collective-permute-start.2 = (f32[4,2,32,512]{3,2,1,0:T(8,128)S(1)}, f32[4,2,32,512]{3,2,1,0:T(8,128)S(1)}, u32[]{:S(2)}, u32[]{:S(2)}) collective-permute-start(f32[4,2,32,512]{3,2,1,0:T(8,128)S(1)} %pad_maximum_fusion), channel_id=1, source_target_pairs={{0,12},{4,0},{8,4},{12,8},{1,13},{5,1},{9,5},{13,9},{2,14},{6,2},{... | collective-permute-start | bytes 1572872 | tf_op jit(solution)/shard_map/ppermute | solution.py:22
  17.5 3.2 %collective-permute-done.1.refs_2_ = f32[3,2,32,512]{3,2,1,0:T(8,128)S(1)} collective-permute-done((f32[3,2,32,512]{3,2,1,0:T(8,128)S(1)}, f32[3,2,32,512]{3,2,1,0:T(8,128)S(1)}, u32[]{:S(2)}, u32[]{:S(2)}) %collective-permute-start.1) | collective-permute-done | bytes 393248 | tf_op jit(solution)/shard_map/ppermute | solution.py:22
  20.7 4.6 %collective-permute-done.2.refs_3_ = f32[4,2,32,512]{3,2,1,0:T(8,128)S(1)} collective-permute-done((f32[4,2,32,512]{3,2,1,0:T(8,128)S(1)}, f32[4,2,32,512]{3,2,1,0:T(8,128)S(1)}, u32[]{:S(2)}, u32[]{:S(2)}) %collective-permute-start.2) | collective-permute-done | bytes 524320 | tf_op jit(solution)/shard_map/ppermute | solution.py:22
  25.4 1.2 pad_maximum_fusion.4
  26.6 1.9 %collective-permute-start.11 = (f32[4,2,32,512]{3,2,1,0:T(8,128)}, f32[4,2,32,512]{3,2,1,0:T(8,128)S(1)}, u32[]{:S(2)}, u32[]{:S(2)}) collective-permute-start(f32[4,2,32,512]{3,2,1,0:T(8,128)} %get-tuple-element.48), channel_id=1, source_target_pairs={{0,3},{4,7},{8,11},{12,15},{1,0},{5,4},{9,8},{13,12},{2,1},{6,5},{... | collective-permute-start | bytes 1572872 | tf_op jit(solution)/shard_map/ppermute | solution.py:22
  28.5 3.9 %collective-permute-start.3 = (f32[4,2,32,512]{3,2,1,0:T(8,128)}, f32[4,2,32,512]{3,2,1,0:T(8,128)S(1)}, u32[]{:S(2)}, u32[]{:S(2)}) collective-permute-start(f32[4,2,32,512]{3,2,1,0:T(8,128)} %get-tuple-element.50), channel_id=1, source_target_pairs={{0,1},{4,5},{8,9},{12,13},{1,2},{5,6},{9,10},{13,14},{2,3},{6,7},{... | collective-permute-start | bytes 1572872 | tf_op jit(solution)/shard_map/ppermute | solution.py:22
  32.5 1.9 %collective-permute-start.10 = (f32[4,2,32,512]{3,2,1,0:T(8,128)}, f32[4,2,32,512]{3,2,1,0:T(8,128)S(1)}, u32[]{:S(2)}, u32[]{:S(2)}) collective-permute-start(f32[4,2,32,512]{3,2,1,0:T(8,128)} %get-tuple-element.48), channel_id=1, source_target_pairs={{0,1},{4,5},{8,9},{12,13},{1,2},{5,6},{9,10},{13,14},{2,3},{6,7},{... | collective-permute-start | bytes 1572872 | tf_op jit(solution)/shard_map/ppermute | solution.py:22
  34.4 5.1 %collective-permute-start.9 = (f32[4,2,32,512]{3,2,1,0:T(8,128)}, f32[4,2,32,512]{3,2,1,0:T(8,128)}, u32[]{:S(2)}, u32[]{:S(2)}) collective-permute-start(f32[4,2,32,512]{3,2,1,0:T(8,128)} %get-tuple-element.50), channel_id=1, source_target_pairs={{0,3},{4,7},{8,11},{12,15},{1,0},{5,4},{9,8},{13,12},{2,1},{6,5},{... | collective-permute-start | bytes 1572872 | tf_op jit(solution)/shard_map/ppermute | solution.py:22
  39.5 1.9 %collective-permute-start.12 = (f32[4,2,32,512]{3,2,1,0:T(8,128)S(1)}, f32[4,2,32,512]{3,2,1,0:T(8,128)}, u32[]{:S(2)}, u32[]{:S(2)}) collective-permute-start(f32[4,2,32,512]{3,2,1,0:T(8,128)S(1)} %collective-permute-done.11.refs_13_), channel_id=1, source_target_pairs={{0,3},{4,7},{8,11},{12,15},{1,0},{5,4},{9,8},{13,12},{2,1},{6,5},{... | collective-permute-start | bytes 1572872 | tf_op jit(solution)/shard_map/ppermute | solution.py:22
  41.5 3.9 %collective-permute-start.8 = (f32[4,2,32,512]{3,2,1,0:T(8,128)S(1)}, f32[4,2,32,512]{3,2,1,0:T(8,128)}, u32[]{:S(2)}, u32[]{:S(2)}) collective-permute-start(f32[4,2,32,512]{3,2,1,0:T(8,128)S(1)} %collective-permute-done.3.refs_8_), channel_id=1, source_target_pairs={{0,1},{4,5},{8,9},{12,13},{1,2},{5,6},{9,10},{13,14},{2,3},{6,7},{... | collective-permute-start | bytes 1572872 | tf_op jit(solution)/shard_map/ppermute | solution.py:22
  45.5 1.0 broadcast_select_fusion.1
  46.4 7.3 %collective-permute-start.4 = (f32[2,32,512]{2,1,0:T(8,128)S(1)}, f32[2,32,512]{2,1,0:T(8,128)S(1)}, u32[]{:S(2)}, u32[]{:S(2)}) collective-permute-start(f32[2,32,512]{2,1,0:T(8,128)S(1)} %get-tuple-element.43), channel_id=1, source_target_pairs={{0,0},{4,4},{8,506},{12,511},{1,5},{5,502},{9,507},{13,1},{2,498},... | collective-permute-start | bytes 393224 | tf_op jit(solution)/shard_map/ppermute | solution.py:22
  53.7 0.8 copy-done.2
  54.5 1.9 %collective-permute-start.5 = (f32[2,32,512]{2,1,0:T(8,128)S(1)}, f32[2,32,512]{2,1,0:T(8,128)S(1)}, u32[]{:S(2)}, u32[]{:S(2)}) collective-permute-start(f32[2,32,512]{2,1,0:T(8,128)S(1)} %get-tuple-element.42), channel_id=1, source_target_pairs={{0,499},{4,0},{8,4},{12,510},{1,1},{5,5},{9,506},{13,511},{2,6},{6... | collective-permute-start | bytes 393224 | tf_op jit(solution)/shard_map/ppermute | solution.py:22
  56.5 9.4 %collective-permute-start.6 = (f32[2,32,512]{2,1,0:T(8,128)S(1)}, f32[2,32,512]{2,1,0:T(8,128)S(1)}, u32[]{:S(2)}, u32[]{:S(2)}) collective-permute-start(f32[2,32,512]{2,1,0:T(8,128)S(1)} %get-tuple-element.41), channel_id=1, source_target_pairs={{0,498},{4,503},{8,0},{12,4},{1,499},{5,1},{9,5},{13,510},{2,2},{6... | collective-permute-start | bytes 393224 | tf_op jit(solution)/shard_map/ppermute | solution.py:22
  65.9 2.4 %collective-permute-start.7 = (f32[2,32,512]{2,1,0:T(8,128)S(1)}, f32[2,32,512]{2,1,0:T(8,128)S(1)}, u32[]{:S(2)}, u32[]{:S(2)}) collective-permute-start(f32[2,32,512]{2,1,0:T(8,128)S(1)} %get-tuple-element.40), channel_id=1, source_target_pairs={{0,4},{4,502},{8,507},{12,0},{1,498},{5,503},{9,1},{13,5},{2,499},... | collective-permute-start | bytes 393224 | tf_op jit(solution)/shard_map/ppermute | solution.py:22
  68.4 3.8 %collective-permute-done.7.refs_7_ = f32[2,32,512]{2,1,0:T(8,128)S(1)} collective-permute-done((f32[2,32,512]{2,1,0:T(8,128)S(1)}, f32[2,32,512]{2,1,0:T(8,128)S(1)}, u32[]{:S(2)}, u32[]{:S(2)}) %collective-permute-start.7) | collective-permute-done | bytes 131104 | tf_op jit(solution)/shard_map/ppermute | solution.py:22
  72.2 1.0 copy-done.1
  73.3 1.0 copy-done.3
  74.3 6.2 %first_level.1 = (f32[4,2,32,512]{3,2,1,0:T(8,128)S(1)}, f32[4,2,32,512]{3,2,1,0:T(8,128)S(1)}, f32[4,2,32,512]{3,2,1,0:T(8,128)}) custom-call(f32[4,2,32,512]{3,2,1,0:T(8,128)S(1)} %get-tuple-element.49.refs_0_, f32[3,2,32,512]{3,2,1,0:T(8,128)S(1)} %collective-permute-done.refs_1_, f32[3,2,32,512]{3,2,1,0:T(8,128)S(1)} %collective-permute-done.1.refs_2_, ...), custom_call_target="tpu_custom_call" | custom-call | tf_op jit(solution)/shard_map/first_level/pallas_call | solution.py:246
  80.5 0.7 collective-permute-start.13
  81.2 3.9 %collective-permute-start.15 = (f32[4,2,32,512]{3,2,1,0:T(8,128)}, f32[4,2,32,512]{3,2,1,0:T(8,128)S(1)}, u32[]{:S(2)}, u32[]{:S(2)}) collective-permute-start(f32[4,2,32,512]{3,2,1,0:T(8,128)} %get-tuple-element.14), channel_id=1, source_target_pairs={{0,12},{4,8},{8,4},{12,0},{1,13},{5,9},{9,5},{13,1},{2,14},{6,10},... | collective-permute-start | bytes 1572872 | tf_op jit(solution)/shard_map/ppermute | solution.py:22
  85.1 1.3 collective-permute-start.16
  86.4 9.9 %collective-permute-done.15 = f32[4,2,32,512]{3,2,1,0:T(8,128)S(1)} collective-permute-done((f32[4,2,32,512]{3,2,1,0:T(8,128)}, f32[4,2,32,512]{3,2,1,0:T(8,128)S(1)}, u32[]{:S(2)}, u32[]{:S(2)}) %collective-permute-start.15) | collective-permute-done | bytes 524320 | tf_op jit(solution)/shard_map/ppermute | solution.py:22
  96.3 1.0 collective-permute-done.16
  97.6 2.9 %collective-permute-start.17 = (f32[4,2,32,512]{3,2,1,0:T(8,128)S(1)}, f32[4,2,32,512]{3,2,1,0:T(8,128)S(1)}, u32[]{:S(2)}, u32[]{:S(2)}) collective-permute-start(f32[4,2,32,512]{3,2,1,0:T(8,128)S(1)} %get-tuple-element.27.refs_3_), channel_id=1, source_target_pairs={{0,1},{4,5},{8,9},{12,13},{1,2},{5,6},{9,10},{13,14},{2,3},{6,7},{... | collective-permute-start | bytes 1572872 | tf_op jit(solution)/shard_map/ppermute | solution.py:22
  100.5 4.2 %collective-permute-start.21 = (f32[4,2,32,512]{3,2,1,0:T(8,128)S(1)}, f32[4,2,32,512]{3,2,1,0:T(8,128)S(1)}, u32[]{:S(2)}, u32[]{:S(2)}) collective-permute-start(f32[4,2,32,512]{3,2,1,0:T(8,128)S(1)} %get-tuple-element.26.refs_7_), channel_id=1, source_target_pairs={{0,3},{4,7},{8,11},{12,15},{1,0},{5,4},{9,8},{13,12},{2,1},{6,5},{... | collective-permute-start | bytes 1572872 | tf_op jit(solution)/shard_map/ppermute | solution.py:22
  104.7 1.9 %collective-permute-start.19 = (f32[4,2,32,512]{3,2,1,0:T(8,128)S(1)}, f32[4,2,32,512]{3,2,1,0:T(8,128)S(1)}, u32[]{:S(2)}, u32[]{:S(2)}) collective-permute-start(f32[4,2,32,512]{3,2,1,0:T(8,128)S(1)} %get-tuple-element.27.refs_3_), channel_id=1, source_target_pairs={{0,3},{4,7},{8,11},{12,15},{1,0},{5,4},{9,8},{13,12},{2,1},{6,5},{... | collective-permute-start | bytes 1572872 | tf_op jit(solution)/shard_map/ppermute | solution.py:22
  106.6 3.9 %collective-permute-start.20 = (f32[4,2,32,512]{3,2,1,0:T(8,128)S(1)}, f32[4,2,32,512]{3,2,1,0:T(8,128)S(1)}, u32[]{:S(2)}, u32[]{:S(2)}) collective-permute-start(f32[4,2,32,512]{3,2,1,0:T(8,128)S(1)} %get-tuple-element.26.refs_7_), channel_id=1, source_target_pairs={{0,1},{4,5},{8,9},{12,13},{1,2},{5,6},{9,10},{13,14},{2,3},{6,7},{... | collective-permute-start | bytes 1572872 | tf_op jit(solution)/shard_map/ppermute | solution.py:22
  110.5 1.3 collective-permute-start.14
  111.8 1.9 %collective-permute-start.18 = (f32[4,2,32,512]{3,2,1,0:T(8,128)S(1)}, f32[4,2,32,512]{3,2,1,0:T(8,128)S(1)}, u32[]{:S(2)}, u32[]{:S(2)}) collective-permute-start(f32[4,2,32,512]{3,2,1,0:T(8,128)S(1)} %collective-permute-done.17.refs_4_), channel_id=1, source_target_pairs={{0,1},{4,5},{8,9},{12,13},{1,2},{5,6},{9,10},{13,14},{2,3},{6,7},{... | collective-permute-start | bytes 1572872 | tf_op jit(solution)/shard_map/ppermute | solution.py:22
  113.8 5.1 %collective-permute-start.22 = (f32[4,2,32,512]{3,2,1,0:T(8,128)S(1)}, f32[4,2,32,512]{3,2,1,0:T(8,128)S(1)}, u32[]{:S(2)}, u32[]{:S(2)}) collective-permute-start(f32[4,2,32,512]{3,2,1,0:T(8,128)S(1)} %collective-permute-done.21.refs_10_), channel_id=1, source_target_pairs={{0,3},{4,7},{8,11},{12,15},{1,0},{5,4},{9,8},{13,12},{2,1},{6,5},{... | collective-permute-start | bytes 1572872 | tf_op jit(solution)/shard_map/ppermute | solution.py:22
  118.9 3.9 %collective-permute-done.19.refs_6_ = f32[4,2,32,512]{3,2,1,0:T(8,128)S(1)} collective-permute-done((f32[4,2,32,512]{3,2,1,0:T(8,128)S(1)}, f32[4,2,32,512]{3,2,1,0:T(8,128)S(1)}, u32[]{:S(2)}, u32[]{:S(2)}) %collective-permute-start.19) | collective-permute-done | bytes 524320 | tf_op jit(solution)/shard_map/ppermute | solution.py:22
  122.8 3.2 %collective-permute-done.14.refs_1_ = f32[4,2,32,512]{3,2,1,0:T(8,128)S(1)} collective-permute-done((f32[4,2,32,512]{3,2,1,0:T(8,128)S(1)}, f32[4,2,32,512]{3,2,1,0:T(8,128)S(1)}, u32[]{:S(2)}, u32[]{:S(2)}) %collective-permute-start.14) | collective-permute-done | bytes 524320 | tf_op jit(solution)/shard_map/ppermute | solution.py:22
  126.0 2.4 %collective-permute-done.22.refs_9_ = f32[4,2,32,512]{3,2,1,0:T(8,128)S(1)} collective-permute-done((f32[4,2,32,512]{3,2,1,0:T(8,128)S(1)}, f32[4,2,32,512]{3,2,1,0:T(8,128)S(1)}, u32[]{:S(2)}, u32[]{:S(2)}) %collective-permute-start.22) | collective-permute-done | bytes 524320 | tf_op jit(solution)/shard_map/ppermute | solution.py:22
  128.4 4.9 %second_level.1 = f32[4,2,32,512]{3,2,1,0:T(8,128)S(1)} custom-call(f32[4,2,32,512]{3,2,1,0:T(8,128)S(1)} %get-tuple-element.13.refs_0_, f32[4,2,32,512]{3,2,1,0:T(8,128)S(1)} %collective-permute-done.14.refs_1_, f32[4,2,32,512]{3,2,1,0:T(8,128)S(1)} %get-tuple-element.12.refs_2_, f32[4,2,32,512]{3,2,1,0:T(8,128)S(1)} %get-tuple-element.27.refs_3_, ...), custom_call_target="tpu_custom_call" | custom-call | tf_op jit(solution)/shard_map/second_level/pallas_call | solution.py:265
  133.3 2.1 %collective-permute-start.23 = (f32[2,32,512]{2,1,0:T(8,128)S(1)}, f32[2,32,512]{2,1,0:T(8,128)S(1)}, u32[]{:S(2)}, u32[]{:S(2)}) collective-permute-start(f32[2,32,512]{2,1,0:T(8,128)S(1)} %get-tuple-element.25), channel_id=1, source_target_pairs={{0,12},{4,0},{8,20},{12,24},{1,9},{5,13},{9,17},{13,21},{2,6},{6,1... | collective-permute-start | bytes 393224 | tf_op jit(solution)/shard_map/ppermute | solution.py:22
  135.4 3.6 %collective-permute-start.24 = (f32[2,32,512]{2,1,0:T(8,128)S(1)}, f32[2,32,512]{2,1,0:T(8,128)S(1)}, u32[]{:S(2)}, u32[]{:S(2)}) collective-permute-start(f32[2,32,512]{2,1,0:T(8,128)S(1)} %get-tuple-element.24), channel_id=1, source_target_pairs={{0,8},{4,12},{8,16},{12,20},{1,5},{5,9},{9,29},{13,17},{2,2},{6,6}... | collective-permute-start | bytes 393224 | tf_op jit(solution)/shard_map/ppermute | solution.py:22
  139.0 2.4 %collective-permute-start.25 = (f32[2,32,512]{2,1,0:T(8,128)S(1)}, f32[2,32,512]{2,1,0:T(8,128)S(1)}, u32[]{:S(2)}, u32[]{:S(2)}) collective-permute-start(f32[2,32,512]{2,1,0:T(8,128)S(1)} %get-tuple-element.23), channel_id=1, source_target_pairs={{0,4},{4,8},{8,28},{12,16},{1,1},{5,5},{9,25},{13,29},{2,14},{6,2}... | collective-permute-start | bytes 393224 | tf_op jit(solution)/shard_map/ppermute | solution.py:22
  141.4 1.9 %collective-permute-start.26 = (f32[2,32,512]{2,1,0:T(8,128)S(1)}, f32[2,32,512]{2,1,0:T(8,128)S(1)}, u32[]{:S(2)}, u32[]{:S(2)}) collective-permute-start(f32[2,32,512]{2,1,0:T(8,128)S(1)} %get-tuple-element.22), channel_id=1, source_target_pairs={{0,0},{4,4},{8,24},{12,28},{1,13},{5,1},{9,21},{13,25},{2,10},{6,1... | collective-permute-start | bytes 393224 | tf_op jit(solution)/shard_map/ppermute | solution.py:22
  143.4 0.7 collective-permute-done.24
  144.1 1.8 %collective-permute-done.25 = f32[2,32,512]{2,1,0:T(8,128)S(1)} collective-permute-done((f32[2,32,512]{2,1,0:T(8,128)S(1)}, f32[2,32,512]{2,1,0:T(8,128)S(1)}, u32[]{:S(2)}, u32[]{:S(2)}) %collective-permute-start.25) | collective-permute-done | bytes 131104 | tf_op jit(solution)/shard_map/ppermute | solution.py:22
  145.9 5.4 %collective-permute-done.26 = f32[2,32,512]{2,1,0:T(8,128)S(1)} collective-permute-done((f32[2,32,512]{2,1,0:T(8,128)S(1)}, f32[2,32,512]{2,1,0:T(8,128)S(1)}, u32[]{:S(2)}, u32[]{:S(2)}) %collective-permute-start.26) | collective-permute-done | bytes 131104 | tf_op jit(solution)/shard_map/ppermute | solution.py:22
  151.3 0.8 select_bitcast_fusion
  (38 shorter events, 0.9 us)
Async XLA Ops:
  0.8 1.3 copy-start.4
  0.8 1.4 copy-start.5
  3.1 14.3 %collective-permute-start = (f32[3,2,32,512]{3,2,1,0:T(8,128)S(1)}, f32[3,2,32,512]{3,2,1,0:T(8,128)S(1)}, u32[]{:S(2)}, u32[]{:S(2)}) collective-permute-start(f32[3,2,32,512]{3,2,1,0:T(8,128)S(1)} %pad_maximum_fusion.5), channel_id=1, source_target_pairs={{0,4},{4,8},{8,12},{12,0},{1,5},{5,9},{9,13},{13,1},{2,6},{6,10},{... | collective-permute-start | bytes 1179656 | tf_op jit(solution)/shard_map/ppermute | solution.py:22
  6.3 6.5 %copy-start.6 = (f32[2,2,32,512]{3,2,1,0:T(8,128)S(1)}, f32[2,2,32,512]{3,2,1,0:T(8,128)}, u32[]{:S(2)}) copy-start(f32[2,2,32,512]{3,2,1,0:T(8,128)} %param.4) | copy-start | bytes 786436
  6.4 14.3 %collective-permute-start.1 = (f32[3,2,32,512]{3,2,1,0:T(8,128)S(1)}, f32[3,2,32,512]{3,2,1,0:T(8,128)S(1)}, u32[]{:S(2)}, u32[]{:S(2)}) collective-permute-start(f32[3,2,32,512]{3,2,1,0:T(8,128)S(1)} %pad_maximum_fusion.6), channel_id=1, source_target_pairs={{0,8},{4,12},{8,0},{12,4},{1,9},{5,13},{9,1},{13,5},{2,10},{6,14},... | collective-permute-start | bytes 1179656 | tf_op jit(solution)/shard_map/ppermute | solution.py:22
  12.9 12.4 %collective-permute-start.2 = (f32[4,2,32,512]{3,2,1,0:T(8,128)S(1)}, f32[4,2,32,512]{3,2,1,0:T(8,128)S(1)}, u32[]{:S(2)}, u32[]{:S(2)}) collective-permute-start(f32[4,2,32,512]{3,2,1,0:T(8,128)S(1)} %pad_maximum_fusion), channel_id=1, source_target_pairs={{0,12},{4,0},{8,4},{12,8},{1,13},{5,1},{9,5},{13,9},{2,14},{6,2},{... | collective-permute-start | bytes 1572872 | tf_op jit(solution)/shard_map/ppermute | solution.py:22
  26.6 12.9 %collective-permute-start.11 = (f32[4,2,32,512]{3,2,1,0:T(8,128)}, f32[4,2,32,512]{3,2,1,0:T(8,128)S(1)}, u32[]{:S(2)}, u32[]{:S(2)}) collective-permute-start(f32[4,2,32,512]{3,2,1,0:T(8,128)} %get-tuple-element.48), channel_id=1, source_target_pairs={{0,3},{4,7},{8,11},{12,15},{1,0},{5,4},{9,8},{13,12},{2,1},{6,5},{... | collective-permute-start | bytes 1572872 | tf_op jit(solution)/shard_map/ppermute | solution.py:22
  28.5 12.9 %collective-permute-start.3 = (f32[4,2,32,512]{3,2,1,0:T(8,128)}, f32[4,2,32,512]{3,2,1,0:T(8,128)S(1)}, u32[]{:S(2)}, u32[]{:S(2)}) collective-permute-start(f32[4,2,32,512]{3,2,1,0:T(8,128)} %get-tuple-element.50), channel_id=1, source_target_pairs={{0,1},{4,5},{8,9},{12,13},{1,2},{5,6},{9,10},{13,14},{2,3},{6,7},{... | collective-permute-start | bytes 1572872 | tf_op jit(solution)/shard_map/ppermute | solution.py:22
  32.5 21.3 %collective-permute-start.10 = (f32[4,2,32,512]{3,2,1,0:T(8,128)}, f32[4,2,32,512]{3,2,1,0:T(8,128)S(1)}, u32[]{:S(2)}, u32[]{:S(2)}) collective-permute-start(f32[4,2,32,512]{3,2,1,0:T(8,128)} %get-tuple-element.48), channel_id=1, source_target_pairs={{0,1},{4,5},{8,9},{12,13},{1,2},{5,6},{9,10},{13,14},{2,3},{6,7},{... | collective-permute-start | bytes 1572872 | tf_op jit(solution)/shard_map/ppermute | solution.py:22
  34.4 22.1 %collective-permute-start.9 = (f32[4,2,32,512]{3,2,1,0:T(8,128)}, f32[4,2,32,512]{3,2,1,0:T(8,128)}, u32[]{:S(2)}, u32[]{:S(2)}) collective-permute-start(f32[4,2,32,512]{3,2,1,0:T(8,128)} %get-tuple-element.50), channel_id=1, source_target_pairs={{0,3},{4,7},{8,11},{12,15},{1,0},{5,4},{9,8},{13,12},{2,1},{6,5},{... | collective-permute-start | bytes 1572872 | tf_op jit(solution)/shard_map/ppermute | solution.py:22
  39.5 32.7 %collective-permute-start.12 = (f32[4,2,32,512]{3,2,1,0:T(8,128)S(1)}, f32[4,2,32,512]{3,2,1,0:T(8,128)}, u32[]{:S(2)}, u32[]{:S(2)}) collective-permute-start(f32[4,2,32,512]{3,2,1,0:T(8,128)S(1)} %collective-permute-done.11.refs_13_), channel_id=1, source_target_pairs={{0,3},{4,7},{8,11},{12,15},{1,0},{5,4},{9,8},{13,12},{2,1},{6,5},{... | collective-permute-start | bytes 1572872 | tf_op jit(solution)/shard_map/ppermute | solution.py:22
  41.5 30.7 %copy-start = (f32[4,2,32,512]{3,2,1,0:T(8,128)}, f32[4,2,32,512]{3,2,1,0:T(8,128)S(1)}, u32[]{:S(2)}) copy-start(f32[4,2,32,512]{3,2,1,0:T(8,128)S(1)} %collective-permute-done.3.refs_8_) | copy-start | bytes 1572868
  41.5 30.7 %collective-permute-start.8 = (f32[4,2,32,512]{3,2,1,0:T(8,128)S(1)}, f32[4,2,32,512]{3,2,1,0:T(8,128)}, u32[]{:S(2)}, u32[]{:S(2)}) collective-permute-start(f32[4,2,32,512]{3,2,1,0:T(8,128)S(1)} %collective-permute-done.3.refs_8_), channel_id=1, source_target_pairs={{0,1},{4,5},{8,9},{12,13},{1,2},{5,6},{9,10},{13,14},{2,3},{6,7},{... | collective-permute-start | bytes 1572872 | tf_op jit(solution)/shard_map/ppermute | solution.py:22
  46.4 19.5 %collective-permute-start.4 = (f32[2,32,512]{2,1,0:T(8,128)S(1)}, f32[2,32,512]{2,1,0:T(8,128)S(1)}, u32[]{:S(2)}, u32[]{:S(2)}) collective-permute-start(f32[2,32,512]{2,1,0:T(8,128)S(1)} %get-tuple-element.43), channel_id=1, source_target_pairs={{0,0},{4,4},{8,506},{12,511},{1,5},{5,502},{9,507},{13,1},{2,498},... | collective-permute-start | bytes 393224 | tf_op jit(solution)/shard_map/ppermute | solution.py:22
  53.7 0.8 copy-start.2
  54.5 13.8 %collective-permute-start.5 = (f32[2,32,512]{2,1,0:T(8,128)S(1)}, f32[2,32,512]{2,1,0:T(8,128)S(1)}, u32[]{:S(2)}, u32[]{:S(2)}) collective-permute-start(f32[2,32,512]{2,1,0:T(8,128)S(1)} %get-tuple-element.42), channel_id=1, source_target_pairs={{0,499},{4,0},{8,4},{12,510},{1,1},{5,5},{9,506},{13,511},{2,6},{6... | collective-permute-start | bytes 393224 | tf_op jit(solution)/shard_map/ppermute | solution.py:22
  56.5 11.9 %collective-permute-start.6 = (f32[2,32,512]{2,1,0:T(8,128)S(1)}, f32[2,32,512]{2,1,0:T(8,128)S(1)}, u32[]{:S(2)}, u32[]{:S(2)}) collective-permute-start(f32[2,32,512]{2,1,0:T(8,128)S(1)} %get-tuple-element.41), channel_id=1, source_target_pairs={{0,498},{4,503},{8,0},{12,4},{1,499},{5,1},{9,5},{13,510},{2,2},{6... | collective-permute-start | bytes 393224 | tf_op jit(solution)/shard_map/ppermute | solution.py:22
  65.9 6.3 %collective-permute-start.7 = (f32[2,32,512]{2,1,0:T(8,128)S(1)}, f32[2,32,512]{2,1,0:T(8,128)S(1)}, u32[]{:S(2)}, u32[]{:S(2)}) collective-permute-start(f32[2,32,512]{2,1,0:T(8,128)S(1)} %get-tuple-element.40), channel_id=1, source_target_pairs={{0,4},{4,502},{8,507},{12,0},{1,498},{5,503},{9,1},{13,5},{2,499},... | collective-permute-start | bytes 393224 | tf_op jit(solution)/shard_map/ppermute | solution.py:22
  72.2 1.0 copy-start.1
  73.3 1.0 copy-start.3
  80.5 5.9 %collective-permute-start.13 = (f32[4,2,32,512]{3,2,1,0:T(8,128)S(1)}, f32[4,2,32,512]{3,2,1,0:T(8,128)S(1)}, u32[]{:S(2)}, u32[]{:S(2)}) collective-permute-start(f32[4,2,32,512]{3,2,1,0:T(8,128)S(1)} %get-tuple-element.12.refs_2_), channel_id=1, source_target_pairs={{4,12},{12,4},{5,13},{13,5},{6,14},{14,6},{7,15},{15,7},{17,19},{1... | collective-permute-start | bytes 1572872 | tf_op jit(solution)/shard_map/ppermute | solution.py:22
  81.2 15.1 %collective-permute-start.15 = (f32[4,2,32,512]{3,2,1,0:T(8,128)}, f32[4,2,32,512]{3,2,1,0:T(8,128)S(1)}, u32[]{:S(2)}, u32[]{:S(2)}) collective-permute-start(f32[4,2,32,512]{3,2,1,0:T(8,128)} %get-tuple-element.14), channel_id=1, source_target_pairs={{0,12},{4,8},{8,4},{12,0},{1,13},{5,9},{9,5},{13,1},{2,14},{6,10},... | collective-permute-start | bytes 1572872 | tf_op jit(solution)/shard_map/ppermute | solution.py:22
  85.1 12.2 %collective-permute-start.16 = (f32[4,2,32,512]{3,2,1,0:T(8,128)S(1)}, f32[4,2,32,512]{3,2,1,0:T(8,128)S(1)}, u32[]{:S(2)}, u32[]{:S(2)}) collective-permute-start(f32[4,2,32,512]{3,2,1,0:T(8,128)S(1)} %get-tuple-element.12.refs_2_), channel_id=1, source_target_pairs={{4,0},{12,8},{5,1},{13,9},{6,2},{14,10},{7,3},{15,11},{17,16},{19,... | collective-permute-start | bytes 1572872 | tf_op jit(solution)/shard_map/ppermute | solution.py:22
  97.6 14.2 %collective-permute-start.17 = (f32[4,2,32,512]{3,2,1,0:T(8,128)S(1)}, f32[4,2,32,512]{3,2,1,0:T(8,128)S(1)}, u32[]{:S(2)}, u32[]{:S(2)}) collective-permute-start(f32[4,2,32,512]{3,2,1,0:T(8,128)S(1)} %get-tuple-element.27.refs_3_), channel_id=1, source_target_pairs={{0,1},{4,5},{8,9},{12,13},{1,2},{5,6},{9,10},{13,14},{2,3},{6,7},{... | collective-permute-start | bytes 1572872 | tf_op jit(solution)/shard_map/ppermute | solution.py:22
  100.5 13.3 %collective-permute-start.21 = (f32[4,2,32,512]{3,2,1,0:T(8,128)S(1)}, f32[4,2,32,512]{3,2,1,0:T(8,128)S(1)}, u32[]{:S(2)}, u32[]{:S(2)}) collective-permute-start(f32[4,2,32,512]{3,2,1,0:T(8,128)S(1)} %get-tuple-element.26.refs_7_), channel_id=1, source_target_pairs={{0,3},{4,7},{8,11},{12,15},{1,0},{5,4},{9,8},{13,12},{2,1},{6,5},{... | collective-permute-start | bytes 1572872 | tf_op jit(solution)/shard_map/ppermute | solution.py:22
  104.7 18.1 %collective-permute-start.19 = (f32[4,2,32,512]{3,2,1,0:T(8,128)S(1)}, f32[4,2,32,512]{3,2,1,0:T(8,128)S(1)}, u32[]{:S(2)}, u32[]{:S(2)}) collective-permute-start(f32[4,2,32,512]{3,2,1,0:T(8,128)S(1)} %get-tuple-element.27.refs_3_), channel_id=1, source_target_pairs={{0,3},{4,7},{8,11},{12,15},{1,0},{5,4},{9,8},{13,12},{2,1},{6,5},{... | collective-permute-start | bytes 1572872 | tf_op jit(solution)/shard_map/ppermute | solution.py:22
  106.6 16.2 %collective-permute-start.20 = (f32[4,2,32,512]{3,2,1,0:T(8,128)S(1)}, f32[4,2,32,512]{3,2,1,0:T(8,128)S(1)}, u32[]{:S(2)}, u32[]{:S(2)}) collective-permute-start(f32[4,2,32,512]{3,2,1,0:T(8,128)S(1)} %get-tuple-element.26.refs_7_), channel_id=1, source_target_pairs={{0,1},{4,5},{8,9},{12,13},{1,2},{5,6},{9,10},{13,14},{2,3},{6,7},{... | collective-permute-start | bytes 1572872 | tf_op jit(solution)/shard_map/ppermute | solution.py:22
  110.5 15.5 %collective-permute-start.14 = (f32[4,2,32,512]{3,2,1,0:T(8,128)S(1)}, f32[4,2,32,512]{3,2,1,0:T(8,128)S(1)}, u32[]{:S(2)}, u32[]{:S(2)}) collective-permute-start(f32[4,2,32,512]{3,2,1,0:T(8,128)S(1)} %get-tuple-element.13.refs_0_), channel_id=1, source_target_pairs={{4,0},{12,8},{5,1},{13,9},{6,2},{14,10},{7,3},{15,11},{17,16},{19,... | collective-permute-start | bytes 1572872 | tf_op jit(solution)/shard_map/ppermute | solution.py:22
  111.8 14.2 %collective-permute-start.18 = (f32[4,2,32,512]{3,2,1,0:T(8,128)S(1)}, f32[4,2,32,512]{3,2,1,0:T(8,128)S(1)}, u32[]{:S(2)}, u32[]{:S(2)}) collective-permute-start(f32[4,2,32,512]{3,2,1,0:T(8,128)S(1)} %collective-permute-done.17.refs_4_), channel_id=1, source_target_pairs={{0,1},{4,5},{8,9},{12,13},{1,2},{5,6},{9,10},{13,14},{2,3},{6,7},{... | collective-permute-start | bytes 1572872 | tf_op jit(solution)/shard_map/ppermute | solution.py:22
  113.8 14.6 %collective-permute-start.22 = (f32[4,2,32,512]{3,2,1,0:T(8,128)S(1)}, f32[4,2,32,512]{3,2,1,0:T(8,128)S(1)}, u32[]{:S(2)}, u32[]{:S(2)}) collective-permute-start(f32[4,2,32,512]{3,2,1,0:T(8,128)S(1)} %collective-permute-done.21.refs_10_), channel_id=1, source_target_pairs={{0,3},{4,7},{8,11},{12,15},{1,0},{5,4},{9,8},{13,12},{2,1},{6,5},{... | collective-permute-start | bytes 1572872 | tf_op jit(solution)/shard_map/ppermute | solution.py:22
  133.3 18.1 %copy-start.7 = (f32[2,2,32,512]{3,2,1,0:T(8,128)S(1)}, f32[2,2,32,512]{3,2,1,0:T(8,128)}, u32[]{:S(2)}) copy-start(f32[2,2,32,512]{3,2,1,0:T(8,128)} %param.4) | copy-start | bytes 786436
  133.3 10.0 %collective-permute-start.23 = (f32[2,32,512]{2,1,0:T(8,128)S(1)}, f32[2,32,512]{2,1,0:T(8,128)S(1)}, u32[]{:S(2)}, u32[]{:S(2)}) collective-permute-start(f32[2,32,512]{2,1,0:T(8,128)S(1)} %get-tuple-element.25), channel_id=1, source_target_pairs={{0,12},{4,0},{8,20},{12,24},{1,9},{5,13},{9,17},{13,21},{2,6},{6,1... | collective-permute-start | bytes 393224 | tf_op jit(solution)/shard_map/ppermute | solution.py:22
  135.4 8.7 %collective-permute-start.24 = (f32[2,32,512]{2,1,0:T(8,128)S(1)}, f32[2,32,512]{2,1,0:T(8,128)S(1)}, u32[]{:S(2)}, u32[]{:S(2)}) collective-permute-start(f32[2,32,512]{2,1,0:T(8,128)S(1)} %get-tuple-element.24), channel_id=1, source_target_pairs={{0,8},{4,12},{8,16},{12,20},{1,5},{5,9},{9,29},{13,17},{2,2},{6,6}... | collective-permute-start | bytes 393224 | tf_op jit(solution)/shard_map/ppermute | solution.py:22
  139.0 6.9 %collective-permute-start.25 = (f32[2,32,512]{2,1,0:T(8,128)S(1)}, f32[2,32,512]{2,1,0:T(8,128)S(1)}, u32[]{:S(2)}, u32[]{:S(2)}) collective-permute-start(f32[2,32,512]{2,1,0:T(8,128)S(1)} %get-tuple-element.23), channel_id=1, source_target_pairs={{0,4},{4,8},{8,28},{12,16},{1,1},{5,5},{9,25},{13,29},{2,14},{6,2}... | collective-permute-start | bytes 393224 | tf_op jit(solution)/shard_map/ppermute | solution.py:22
  141.4 9.9 %collective-permute-start.26 = (f32[2,32,512]{2,1,0:T(8,128)S(1)}, f32[2,32,512]{2,1,0:T(8,128)S(1)}, u32[]{:S(2)}, u32[]{:S(2)}) collective-permute-start(f32[2,32,512]{2,1,0:T(8,128)S(1)} %get-tuple-element.22), channel_id=1, source_target_pairs={{0,0},{4,4},{8,24},{12,28},{1,13},{5,1},{9,21},{13,25},{2,10},{6,1... | collective-permute-start | bytes 393224 | tf_op jit(solution)/shard_map/ppermute | solution.py:22

commit v6 on v4

--- a/solution.py
+++ b/solution.py
@@ -1,3 +1,5 @@
+import functools
+
 import jax
 import jax.numpy as jnp
 from jax import lax
@@ -6,7 +8,7 @@
 from jax.sharding import PartitionSpec as P
 
 SIDE = 4
-VMEM_LIMIT = 20 * 1024 * 1024
+VMEM_LIMIT = 16 * 1024 * 1024
 
 
 def permuted(value, slabs, target):
@@ -47,15 +49,15 @@
     return (slab, orb(slab, line, spot + 2)) if spot % 2 else None
 
 
-def slab_below(slab, line, spot):
-    return slab - 1, orb(slab, line, spot)
-
-
 def to_owner(step):
     def target(slab, line, spot):
         return slab + spot // 2, orb(slab, line, step + spot - line)
 
     return target
+
+
+def slab_below(slab, line, spot):
+    return slab - 1, orb(slab, line, spot)
 
 
 def place():
@@ -101,12 +103,13 @@
         low_ref[pl.ds(row, rows), columns] = low
 
 
-def first_kernel(*refs):
+def first_kernel(with_diag, *refs):
     messages = refs[0:4]
     greens = refs[4:7]
     parts = refs[7:10]
-    front_ref, term_ref, cross_ref = refs[10:13]
-    green_high, green_low, part_high, part_low, left = refs[13:]
+    lefts = refs[10:-6]
+    out_ref = refs[-6]
+    green_high, green_low, part_high, part_low, left = refs[-5:]
     core, line, spot = place()
     rows = messages[0].shape[2]
     for step in range(4):
@@ -119,38 +122,28 @@
     for step in range(4):
         own = pl.multiple_of(lax.rem(spot - step + 4, 4) * rows, rows)
         for part in range(2):
-            left[part, pl.ds(own, rows), :] = messages[step][2, part]
-            left[part, pl.ds(4 * rows + own, rows), :] = messages[step][3, part]
+            left[part, pl.ds(own, rows), :] = messages[step][2, part] if with_diag else lefts[step][part]
     middle_re, middle_im = product(left[0], left[1], green_high[...], green_low[...])
-    out_re, out_im = product(middle_re, middle_im, part_high[...], part_low[...])
-    count = 4 * rows
-    with_lower = (spot == 0) | (spot == 3)
-    outer = lax.rem(spot, 2) == 0
-    for part, value in enumerate((out_re, out_im)):
-        below = -value[:count]
-        above = -value[count:]
-        panel = jnp.where(with_lower, above, below)
-        other = jnp.where(with_lower, below, above)
-        for block in range(4):
-            piece = slice(block * rows, (block + 1) * rows)
-            front_ref[block, part] = panel[piece]
-            term_ref[block, part] = other[piece]
-        for step in (0, 3):
-            block = lax.rem(spot - step + 4, 4)
-            term_ref[block, part] += jnp.where(outer, 0.0, messages[step][4, part])
-        for block in range(4):
-            cross_ref[block, part] = jnp.where(outer, front_ref[block, part], term_ref[block, part])
+    outs = product(middle_re, middle_im, part_high[...], part_low[...])
+    for part, value in enumerate(outs):
+        for block in range(4):
+            out_ref[block, part] = -value[block * rows : (block + 1) * rows]
+        if with_diag:
+            for step in (0, 3):
+                block = lax.rem(spot - step + 4, 4)
+                diag = messages[step][3, part]
+                out_ref[block, part] += jnp.where(lax.rem(spot, 2) == 0, 0.0, diag)
 
 
 def second_kernel(*refs):
-    front_ref, front_there_ref, keep_ref = refs[0:3]
-    pivots = refs[3:7]
-    panels = refs[7:11]
-    out_ref = refs[11]
-    pivot_high, pivot_low, panel_high, panel_low = refs[12:]
+    side_ref, side_there_ref = refs[0:2]
+    pivots = refs[2:6]
+    panels = refs[6:10]
+    out_ref = refs[10]
+    pivot_high, pivot_low, panel_high, panel_low = refs[11:]
     core, line, spot = place()
-    rows = front_ref.shape[2]
-    width = front_ref.shape[3]
+    rows = side_ref.shape[2]
+    width = side_ref.shape[3]
     outer = lax.rem(spot, 2) == 0
     column_iota = lax.broadcasted_iota(jnp.int32, (rows, width), 1)
     row_iota = lax.broadcasted_iota(jnp.int32, (rows, width), 0)
@@ -182,7 +175,7 @@
         return 2.0 * re - take_re, 2.0 * im - take_im
 
     left_re, left_im = (
-        jnp.concatenate([jnp.where(outer, front_there_ref[block, part], front_ref[block, part]) for block in range(4)], 0)
+        jnp.concatenate([jnp.where(outer, side_there_ref[block, part], side_ref[block, part]) for block in range(4)], 0)
         for part in range(2)
     )
     guess_re, guess_im = times_first(left_re, left_im)
@@ -192,7 +185,7 @@
     outs = product(solved_re, solved_im, panel_high[...], panel_low[...])
     for part, value in enumerate(outs):
         for block in range(4):
-            kept = jnp.where(outer, keep_ref[block, part], 0.0)
+            kept = jnp.where(outer, side_ref[block, part], 0.0)
             slot = lax.rem(block + line - spot + 4, 4)
             out_ref[slot, part] = kept - value[block * rows : (block + 1) * rows]
 
@@ -206,18 +199,14 @@
     width = lower.shape[3]
     slabs = lax.axis_size("slab")
     core, line, spot = place()
-    next_lower = permuted(lower[0], slabs, slab_below)
-
     def message(step):
         there = lax.rem(spot + step, 4)
         odd = lax.div(there, 2)
         green = lax.dynamic_index_in_dim(odd_green, odd, 0, False)
         down = lax.dynamic_index_in_dim(lower, 2 * odd + 1, 0, False)
         up = lax.dynamic_index_in_dim(upper, 2 * odd + 1, 0, False)
-        below = lax.dynamic_index_in_dim(upper, 2 * odd, 0, False)
         with_lower = (there == 0) | (there == 3)
-        above = jnp.where(odd == 0, lower[2], next_lower)
-        blocks = [green, jnp.where(with_lower, down, up), below, above]
+        blocks = [green, jnp.where(with_lower, down, up), jnp.where(odd == 0, lower[2], upper[2])]
         return jnp.stack(blocks + [diag_even[1]] if step in (0, 3) else blocks)
 
     def ringed(first, second):
@@ -230,37 +219,54 @@
         return [first_one, first_two, first_three], [second_one, second_two, second_three]
 
     messages = [message(0)] + [permuted(message(step), slabs, along_spot(step)) for step in range(1, 4)]
-    greens, parts = ringed(*(jnp.stack([piece[side] for piece in messages]) for side in range(2)))
+    first, second = (jnp.stack([piece[side] for piece in messages]) for side in range(2))
+    greens, parts = ringed(first, second)
+    own_row, next_row, _ = lax.optimization_barrier((upper[0], lower[0], greens[0]))
+    next_row = permuted(next_row, slabs, slab_below)
     four = jax.ShapeDtypeStruct((4, 2, rows, width), jnp.float32)
     wide = pltpu.VMEM((width, 2 * width), jnp.bfloat16)
-    front, term, cross = pl.pallas_call(
-        first_kernel,
-        out_shape=[four] * 3,
-        in_specs=vmem(10),
-        out_specs=vmem(3),
-        scratch_shapes=[wide] * 4 + [pltpu.VMEM((2, 8 * rows, width), jnp.float32)],
-        compiler_params=pltpu.CompilerParams(vmem_limit_bytes=VMEM_LIMIT),
-        name="first_level",
-    )(*messages, *greens, *parts)
+
+    def rows_through(with_diag, message, lefts):
+        flops = 3 * 2 * 2 * (8 * rows) * width * (2 * width)
+        return pl.pallas_call(
+            functools.partial(first_kernel, with_diag),
+            out_shape=four,
+            in_specs=vmem(10 + len(lefts)),
+            out_specs=vmem(1)[0],
+            scratch_shapes=[wide] * 4 + [pltpu.VMEM((2, 4 * rows, width), jnp.float32)],
+            compiler_params=pltpu.CompilerParams(vmem_limit_bytes=VMEM_LIMIT),
+            cost_estimate=pl.CostEstimate(flops=flops, bytes_accessed=12 * width * width, transcendentals=0),
+            name="first_level" if with_diag else "first_level_side",
+        )(message, *messages[1:], *greens, *parts, *lefts)
+
+    ready, next_row = lax.optimization_barrier((messages[0], next_row))
+    main = rows_through(True, ready, [])
+
+    def late(step):
+        return jnp.where(lax.rem(spot + step, 4) < 2, own_row, next_row)
+
+    lates = [late(0)] + [permuted(late(step), slabs, along_spot(step)) for step in range(1, 4)]
 
     outer = lax.rem(spot, 2) == 0
-    term_there = permuted(term, slabs, inner)
-    term_out = permuted(term, slabs, outwards)
-    cross_there = permuted(cross, slabs, crossed)
-    panel = jnp.where(outer, front, cross_there)
-    pivot = jnp.where(outer, cross_there + term_out, term + term_there)
+    cross_there = permuted(main, slabs, crossed)
+    term_out = permuted(main, slabs, outwards)
+    term_there = permuted(main, slabs, inner)
+    panel = jnp.where(outer, main, cross_there)
+    pivot = jnp.where(outer, cross_there + term_out, main + term_there)
+    pivot, *lates = lax.optimization_barrier((pivot, *lates))
     pivots, panels = ringed(pivot, panel)
-    after, _ = lax.optimization_barrier((front, term_there))
-    front_there = permuted(after, slabs, outwards)
+    *lates, _ = lax.optimization_barrier((*lates, pivots[0]))
+    side = rows_through(False, messages[0], lates)
+    side_there = permuted(side, slabs, outwards)
     out = pl.pallas_call(
         second_kernel,
         out_shape=four,
-        in_specs=vmem(11),
+        in_specs=vmem(10),
         out_specs=vmem(1)[0],
         scratch_shapes=[wide] * 4,
         compiler_params=pltpu.CompilerParams(vmem_limit_bytes=VMEM_LIMIT),
         name="second_level",
-    )(front, front_there, term, pivot, *pivots, panel, *panels)
+    )(side, side_there, pivot, *pivots, panel, *panels)
     ends = [permuted(out[step], slabs, to_owner(step)) for step in range(4)]
 
     def ended(code):

time: 156 us -> 139 us (0.89)
  the two profiles are of different devices: /device:TPU:4 before, /device:TPU:112 now
where the time goes in v6:
time: 139 us
  starting transfers between devices  84.5 us (61%)
  waiting for transfers between devices  33.6 us (24%)
  Pallas kernels  10.7 us (8%)
  other arithmetic  5.47 us (4%)
  local copies, waits for them, and re-layouts  2.92 us (2%)
  between operations  1.4 us (1%)
    ppermute x27, starting transfers between devices, permuted(): return lax.ppermute(value, ('slab', 'orb'), pairs)  84.5 us
    ppermute x27, waiting for transfers between devices, permuted(): return lax.ppermute(value, ('slab', 'orb'), pairs)  33.6 us
    pallas_call x2, Pallas kernels, rows_through(): pl.pallas_call(functools.partial(first_kernel, with_diag), out_shape=four...  5.87 us
    pallas_call x1, Pallas kernels, shards(): pl.pallas_call(second_kernel, out_shape=four, in_specs=vmem(10), out_spec...  4.87 us
  transfers between devices with their start and end apart: 27, of which 10 were waited for; matrix products, arithmetic and copies ran while one was open for 3% of the time, Pallas kernels for 2%

profile of v6, /device:TPU:112, one launch (start us, length us, event | category | flops | bytes accessed | tf_op | source)
XLA Modules:
  0.0 138.6 jit_solution(12694788954916163566)
XLA Ops:
  0.8 1.9 %constant_dynamic-slice_fusion = (f32[1,2,32,512]{3,2,1,0:T(8,128)S(1)}, f32[1,2,32,512]{3,2,1,0:T(8,128)S(1)}, f32[1,2,32,512]{3,2,1,0:T(8,128)}, f32[1,2,32,512]{3,2,1,0:T(8,128)S(1)}) fusion(f32[2,2,32,512]{3,2,1,0:T(8,128)} %param.5, s32[]{:T(128)S(6)} %select_n.224, s32[]{:T(128)S(6)} %select_n.212, s32[]{:T(128)S(6)} %select_n.206, s32[]{:T(128)S(6)} %select_n.218), kind=kLoop, calls=%fused_computation.35 | loop fusion | bytes 1048592 | tf_op jit(solution)/shard_map/jit(dynamic_index_in_dim)/dynamic_slice | solution.py:205
  2.7 0.1 dynamic-slice_select_fusion
  2.9 0.8 pad_maximum_fusion.6
  3.6 2.2 %collective-permute-start.1 = (f32[3,2,32,512]{3,2,1,0:T(8,128)}, f32[3,2,32,512]{3,2,1,0:T(8,128)S(1)}, u32[]{:S(2)}, u32[]{:S(2)}) collective-permute-start(f32[3,2,32,512]{3,2,1,0:T(8,128)} %pad_maximum_fusion.6), channel_id=1, source_target_pairs={{0,8},{4,12},{8,0},{12,4},{1,9},{5,13},{9,1},{13,5},{2,10},{6,14},... | collective-permute-start | bytes 1179656 | tf_op jit(solution)/shard_map/ppermute | solution.py:24
  5.9 4.3 %collective-permute-start.2 = (f32[4,2,32,512]{3,2,1,0:T(8,128)S(1)}, f32[4,2,32,512]{3,2,1,0:T(8,128)S(1)}, u32[]{:S(2)}, u32[]{:S(2)}) collective-permute-start(f32[4,2,32,512]{3,2,1,0:T(8,128)S(1)} %pad_maximum_fusion), channel_id=1, source_target_pairs={{0,12},{4,0},{8,4},{12,8},{1,13},{5,1},{9,5},{13,9},{2,14},{6,2},{... | collective-permute-start | bytes 1572872 | tf_op jit(solution)/shard_map/ppermute | solution.py:24
  10.3 0.8 pad_maximum_fusion.5
  11.0 1.9 %collective-permute-start = (f32[3,2,32,512]{3,2,1,0:T(8,128)}, f32[3,2,32,512]{3,2,1,0:T(8,128)S(1)}, u32[]{:S(2)}, u32[]{:S(2)}) collective-permute-start(f32[3,2,32,512]{3,2,1,0:T(8,128)} %pad_maximum_fusion.5), channel_id=1, source_target_pairs={{0,4},{4,8},{8,12},{12,0},{1,5},{5,9},{9,13},{13,1},{2,6},{6,10},{... | collective-permute-start | bytes 1179656 | tf_op jit(solution)/shard_map/ppermute | solution.py:24
  13.0 2.0 %collective-permute-done.1.refs_2_ = f32[3,2,32,512]{3,2,1,0:T(8,128)S(1)} collective-permute-done((f32[3,2,32,512]{3,2,1,0:T(8,128)}, f32[3,2,32,512]{3,2,1,0:T(8,128)S(1)}, u32[]{:S(2)}, u32[]{:S(2)}) %collective-permute-start.1) | collective-permute-done | bytes 393248 | tf_op jit(solution)/shard_map/ppermute | solution.py:24
  15.0 5.9 %collective-permute-done.refs_1_ = f32[3,2,32,512]{3,2,1,0:T(8,128)S(1)} collective-permute-done((f32[3,2,32,512]{3,2,1,0:T(8,128)}, f32[3,2,32,512]{3,2,1,0:T(8,128)S(1)}, u32[]{:S(2)}, u32[]{:S(2)}) %collective-permute-start) | collective-permute-done | bytes 393248 | tf_op jit(solution)/shard_map/ppermute | solution.py:24
  21.0 0.9 copy-done.8
  21.8 0.2 pad_maximum_fusion.4
  22.0 3.4 %collective-permute-start.3 = (f32[4,2,32,512]{3,2,1,0:T(8,128)S(1)}, f32[4,2,32,512]{3,2,1,0:T(8,128)S(1)}, u32[]{:S(2)}, u32[]{:S(2)}) collective-permute-start(f32[4,2,32,512]{3,2,1,0:T(8,128)S(1)} %get-tuple-element.64), channel_id=1, source_target_pairs={{0,1},{4,5},{8,9},{12,13},{1,2},{5,6},{9,10},{13,14},{2,3},{6,7},{... | collective-permute-start | bytes 1572872 | tf_op jit(solution)/shard_map/ppermute | solution.py:24
  25.4 3.7 %collective-permute-start.7 = (f32[4,2,32,512]{3,2,1,0:T(8,128)S(1)}, f32[4,2,32,512]{3,2,1,0:T(8,128)S(1)}, u32[]{:S(2)}, u32[]{:S(2)}) collective-permute-start(f32[4,2,32,512]{3,2,1,0:T(8,128)S(1)} %get-tuple-element.62), channel_id=1, source_target_pairs={{0,3},{4,7},{8,11},{12,15},{1,0},{5,4},{9,8},{13,12},{2,1},{6,5},{... | collective-permute-start | bytes 1572872 | tf_op jit(solution)/shard_map/ppermute | solution.py:24
  29.1 3.5 %collective-permute-start.5 = (f32[4,2,32,512]{3,2,1,0:T(8,128)S(1)}, f32[4,2,32,512]{3,2,1,0:T(8,128)S(1)}, u32[]{:S(2)}, u32[]{:S(2)}) collective-permute-start(f32[4,2,32,512]{3,2,1,0:T(8,128)S(1)} %get-tuple-element.64), channel_id=1, source_target_pairs={{0,3},{4,7},{8,11},{12,15},{1,0},{5,4},{9,8},{13,12},{2,1},{6,5},{... | collective-permute-start | bytes 1572872 | tf_op jit(solution)/shard_map/ppermute | solution.py:24
  32.6 2.4 %collective-permute-start.6 = (f32[4,2,32,512]{3,2,1,0:T(8,128)S(1)}, f32[4,2,32,512]{3,2,1,0:T(8,128)S(1)}, u32[]{:S(2)}, u32[]{:S(2)}) collective-permute-start(f32[4,2,32,512]{3,2,1,0:T(8,128)S(1)} %get-tuple-element.62), channel_id=1, source_target_pairs={{0,1},{4,5},{8,9},{12,13},{1,2},{5,6},{9,10},{13,14},{2,3},{6,7},{... | collective-permute-start | bytes 1572872 | tf_op jit(solution)/shard_map/ppermute | solution.py:24
  35.0 2.2 %collective-permute-start.4 = (f32[4,2,32,512]{3,2,1,0:T(8,128)S(1)}, f32[4,2,32,512]{3,2,1,0:T(8,128)S(1)}, u32[]{:S(2)}, u32[]{:S(2)}) collective-permute-start(f32[4,2,32,512]{3,2,1,0:T(8,128)S(1)} %collective-permute-done.3.refs_4_), channel_id=1, source_target_pairs={{0,1},{4,5},{8,9},{12,13},{1,2},{5,6},{9,10},{13,14},{2,3},{6,7},{... | collective-permute-start | bytes 1572872 | tf_op jit(solution)/shard_map/ppermute | solution.py:24
  37.2 4.9 %collective-permute-start.8 = (f32[4,2,32,512]{3,2,1,0:T(8,128)S(1)}, f32[4,2,32,512]{3,2,1,0:T(8,128)S(1)}, u32[]{:S(2)}, u32[]{:S(2)}) collective-permute-start(f32[4,2,32,512]{3,2,1,0:T(8,128)S(1)} %collective-permute-done.7.refs_9_), channel_id=1, source_target_pairs={{0,3},{4,7},{8,11},{12,15},{1,0},{5,4},{9,8},{13,12},{2,1},{6,5},{... | collective-permute-start | bytes 1572872 | tf_op jit(solution)/shard_map/ppermute | solution.py:24
  42.1 2.5 %collective-permute-done.9 = f32[2,32,512]{2,1,0:T(8,128)S(1)} collective-permute-done((f32[2,32,512]{2,1,0:T(8,128)S(1)}, f32[2,32,512]{2,1,0:T(8,128)S(1)}, u32[]{:S(2)}, u32[]{:S(2)}) %collective-permute-start.9) | collective-permute-done | bytes 131104 | tf_op jit(solution)/shard_map/ppermute | solution.py:24
  44.6 0.3 collective-permute-done.6.refs_7_
  44.9 5.6 %collective-permute-done.4.refs_5_ = f32[4,2,32,512]{3,2,1,0:T(8,128)S(1)} collective-permute-done((f32[4,2,32,512]{3,2,1,0:T(8,128)S(1)}, f32[4,2,32,512]{3,2,1,0:T(8,128)S(1)}, u32[]{:S(2)}, u32[]{:S(2)}) %collective-permute-start.4) | collective-permute-done | bytes 524320 | tf_op jit(solution)/shard_map/ppermute | solution.py:24
  50.5 3.4 %first_level.1 = f32[4,2,32,512]{3,2,1,0:T(8,128)} custom-call(f32[4,2,32,512]{3,2,1,0:T(8,128)S(1)} %get-tuple-element.17.refs_0_, f32[3,2,32,512]{3,2,1,0:T(8,128)S(1)} %collective-permute-done.refs_1_, f32[3,2,32,512]{3,2,1,0:T(8,128)S(1)} %collective-permute-done.1.refs_2_, f32[4,2,32,512]{3,2,1,0:T(8,128)S(1)} %collective-permute-done.2.refs_3_, ...), custom_call_target="tpu_custom_call" | custom-call | flops 1610612736 | bytes 3145728 | tf_op jit(solution)/shard_map/first_level/pallas_call | solution.py:231
  53.9 3.3 %collective-permute-start.10 = (f32[4,2,32,512]{3,2,1,0:T(8,128)}, f32[4,2,32,512]{3,2,1,0:T(8,128)}, u32[]{:S(2)}, u32[]{:S(2)}) collective-permute-start(f32[4,2,32,512]{3,2,1,0:T(8,128)} %first_level.1), channel_id=1, source_target_pairs={{0,12},{4,8},{8,4},{12,0},{1,13},{5,9},{9,5},{13,1},{2,14},{6,10},... | collective-permute-start | bytes 1572872 | tf_op jit(solution)/shard_map/ppermute | solution.py:24
  57.1 1.5 %collective-permute-start.12 = (f32[4,2,32,512]{3,2,1,0:T(8,128)}, f32[4,2,32,512]{3,2,1,0:T(8,128)}, u32[]{:S(2)}, u32[]{:S(2)}) collective-permute-start(f32[4,2,32,512]{3,2,1,0:T(8,128)} %first_level.1), channel_id=1, source_target_pairs={{4,12},{12,4},{5,13},{13,5},{6,14},{14,6},{7,15},{15,7},{17,19},{1... | collective-permute-start | bytes 1572872 | tf_op jit(solution)/shard_map/ppermute | solution.py:24
  58.6 1.3 collective-permute-start.11
  59.9 1.0 broadcast_select_fusion.1
  60.9 6.0 %collective-permute-start.13 = (f32[2,32,512]{2,1,0:T(8,128)S(1)}, f32[2,32,512]{2,1,0:T(8,128)S(1)}, u32[]{:S(2)}, u32[]{:S(2)}) collective-permute-start(f32[2,32,512]{2,1,0:T(8,128)S(1)} %get-tuple-element.56), channel_id=1, source_target_pairs={{0,4},{4,8},{8,12},{12,0},{1,5},{5,9},{9,13},{13,1},{2,6},{6,10},{... | collective-permute-start | bytes 393224 | tf_op jit(solution)/shard_map/ppermute | solution.py:24
  66.9 4.8 %collective-permute-start.14 = (f32[2,32,512]{2,1,0:T(8,128)S(1)}, f32[2,32,512]{2,1,0:T(8,128)S(1)}, u32[]{:S(2)}, u32[]{:S(2)}) collective-permute-start(f32[2,32,512]{2,1,0:T(8,128)S(1)} %get-tuple-element.55), channel_id=1, source_target_pairs={{0,8},{4,12},{8,0},{12,4},{1,9},{5,13},{9,1},{13,5},{2,10},{6,14},... | collective-permute-start | bytes 393224 | tf_op jit(solution)/shard_map/ppermute | solution.py:24
  71.8 2.5 %collective-permute-start.15 = (f32[2,32,512]{2,1,0:T(8,128)S(1)}, f32[2,32,512]{2,1,0:T(8,128)S(1)}, u32[]{:S(2)}, u32[]{:S(2)}) collective-permute-start(f32[2,32,512]{2,1,0:T(8,128)S(1)} %get-tuple-element.54), channel_id=1, source_target_pairs={{0,12},{4,0},{8,4},{12,8},{1,13},{5,1},{9,5},{13,9},{2,14},{6,2},{... | collective-permute-start | bytes 393224 | tf_op jit(solution)/shard_map/ppermute | solution.py:24
  74.3 0.8 collective-permute-done.11
  75.1 1.8 %broadcast_select_fusion = (f32[4,2,32,512]{3,2,1,0:T(8,128)S(1)}, f32[4,2,32,512]{3,2,1,0:T(8,128)S(1)}) fusion(f32[4,2,32,512]{3,2,1,0:T(8,128)} %first_level.1, f32[4,2,32,512]{3,2,1,0:T(8,128)} %collective-permute-done.10, pred[]{:T(512)S(6)} %eq.93, f32[4,2,32,512]{3,2,1,0:T(8,128)} %collective-permute-done.12, f32[4,2,32,512]{3,2,1,0:T(8,128)} %collective-permute-done.11), kind=kLoop, calls=%fused_computation.11 | loop fusion | flops 524288 | bytes 3145729 | tf_op jit(solution)/shard_map/jit(_where)/select_n | solution.py:254
  76.8 1.9 %collective-permute-done.15.refs_13_ = f32[2,32,512]{2,1,0:T(8,128)S(1)} collective-permute-done((f32[2,32,512]{2,1,0:T(8,128)S(1)}, f32[2,32,512]{2,1,0:T(8,128)S(1)}, u32[]{:S(2)}, u32[]{:S(2)}) %collective-permute-start.15) | collective-permute-done | bytes 131104 | tf_op jit(solution)/shard_map/ppermute | solution.py:24
  78.8 1.9 %collective-permute-start.16 = (f32[4,2,32,512]{3,2,1,0:T(8,128)S(1)}, f32[4,2,32,512]{3,2,1,0:T(8,128)S(1)}, u32[]{:S(2)}, u32[]{:S(2)}) collective-permute-start(f32[4,2,32,512]{3,2,1,0:T(8,128)S(1)} %get-tuple-element.24.refs_2_), channel_id=1, source_target_pairs={{0,1},{4,5},{8,9},{12,13},{1,2},{5,6},{9,10},{13,14},{2,3},{6,7},{... | collective-permute-start | bytes 1572872 | tf_op jit(solution)/shard_map/ppermute | solution.py:24
  80.7 5.1 %collective-permute-start.21 = (f32[4,2,32,512]{3,2,1,0:T(8,128)S(1)}, f32[4,2,32,512]{3,2,1,0:T(8,128)S(1)}, u32[]{:S(2)}, u32[]{:S(2)}) collective-permute-start(f32[4,2,32,512]{3,2,1,0:T(8,128)S(1)} %get-tuple-element.29.refs_6_), channel_id=1, source_target_pairs={{0,3},{4,7},{8,11},{12,15},{1,0},{5,4},{9,8},{13,12},{2,1},{6,5},{... | collective-permute-start | bytes 1572872 | tf_op jit(solution)/shard_map/ppermute | solution.py:24
  85.8 2.6 %collective-permute-start.19 = (f32[4,2,32,512]{3,2,1,0:T(8,128)S(1)}, f32[4,2,32,512]{3,2,1,0:T(8,128)S(1)}, u32[]{:S(2)}, u32[]{:S(2)}) collective-permute-start(f32[4,2,32,512]{3,2,1,0:T(8,128)S(1)} %get-tuple-element.24.refs_2_), channel_id=1, source_target_pairs={{0,3},{4,7},{8,11},{12,15},{1,0},{5,4},{9,8},{13,12},{2,1},{6,5},{... | collective-permute-start | bytes 1572872 | tf_op jit(solution)/shard_map/ppermute | solution.py:24
  88.5 3.2 %collective-permute-start.20 = (f32[4,2,32,512]{3,2,1,0:T(8,128)S(1)}, f32[4,2,32,512]{3,2,1,0:T(8,128)S(1)}, u32[]{:S(2)}, u32[]{:S(2)}) collective-permute-start(f32[4,2,32,512]{3,2,1,0:T(8,128)S(1)} %get-tuple-element.29.refs_6_), channel_id=1, source_target_pairs={{0,1},{4,5},{8,9},{12,13},{1,2},{5,6},{9,10},{13,14},{2,3},{6,7},{... | collective-permute-start | bytes 1572872 | tf_op jit(solution)/shard_map/ppermute | solution.py:24
  91.7 2.5 %first_level_side.1.refs_0_ = f32[4,2,32,512]{3,2,1,0:T(8,128)S(1)} custom-call(f32[4,2,32,512]{3,2,1,0:T(8,128)S(1)} %get-tuple-element.17.refs_0_, f32[3,2,32,512]{3,2,1,0:T(8,128)S(1)} %collective-permute-done.refs_1_, f32[3,2,32,512]{3,2,1,0:T(8,128)S(1)} %collective-permute-done.1.refs_2_, f32[4,2,32,512]{3,2,1,0:T(8,128)S(1)} %collective-permute-done.2.refs_3_, ...), custom_call_target="tpu_custom_call" | custom-call | flops 1610612736 | bytes 3145728 | tf_op jit(solution)/shard_map/first_level_side/pallas_call | solution.py:231
  94.3 1.3 collective-permute-start.17
  95.6 1.9 %collective-permute-start.18 = (f32[4,2,32,512]{3,2,1,0:T(8,128)S(1)}, f32[4,2,32,512]{3,2,1,0:T(8,128)S(1)}, u32[]{:S(2)}, u32[]{:S(2)}) collective-permute-start(f32[4,2,32,512]{3,2,1,0:T(8,128)S(1)} %collective-permute-done.16.refs_3_), channel_id=1, source_target_pairs={{0,1},{4,5},{8,9},{12,13},{1,2},{5,6},{9,10},{13,14},{2,3},{6,7},{... | collective-permute-start | bytes 1572872 | tf_op jit(solution)/shard_map/ppermute | solution.py:24
  97.5 5.1 %collective-permute-start.22 = (f32[4,2,32,512]{3,2,1,0:T(8,128)S(1)}, f32[4,2,32,512]{3,2,1,0:T(8,128)S(1)}, u32[]{:S(2)}, u32[]{:S(2)}) collective-permute-start(f32[4,2,32,512]{3,2,1,0:T(8,128)S(1)} %collective-permute-done.21.refs_9_), channel_id=1, source_target_pairs={{0,3},{4,7},{8,11},{12,15},{1,0},{5,4},{9,8},{13,12},{2,1},{6,5},{... | collective-permute-start | bytes 1572872 | tf_op jit(solution)/shard_map/ppermute | solution.py:24
  102.7 7.9 %collective-permute-done.17.refs_1_ = f32[4,2,32,512]{3,2,1,0:T(8,128)S(1)} collective-permute-done((f32[4,2,32,512]{3,2,1,0:T(8,128)S(1)}, f32[4,2,32,512]{3,2,1,0:T(8,128)S(1)}, u32[]{:S(2)}, u32[]{:S(2)}) %collective-permute-start.17) | collective-permute-done | bytes 524320 | tf_op jit(solution)/shard_map/ppermute | solution.py:24
  110.5 4.9 %second_level.1 = f32[4,2,32,512]{3,2,1,0:T(8,128)S(1)} custom-call(f32[4,2,32,512]{3,2,1,0:T(8,128)S(1)} %first_level_side.1.refs_0_, f32[4,2,32,512]{3,2,1,0:T(8,128)S(1)} %collective-permute-done.17.refs_1_, f32[4,2,32,512]{3,2,1,0:T(8,128)S(1)} %get-tuple-element.24.refs_2_, f32[4,2,32,512]{3,2,1,0:T(8,128)S(1)} %collective-permute-done.16.refs_3_, ...), custom_call_target="tpu_custom_call" | custom-call | tf_op jit(solution)/shard_map/second_level/pallas_call | solution.py:261
  115.5 2.1 %collective-permute-start.23 = (f32[2,32,512]{2,1,0:T(8,128)S(1)}, f32[2,32,512]{2,1,0:T(8,128)S(1)}, u32[]{:S(2)}, u32[]{:S(2)}) collective-permute-start(f32[2,32,512]{2,1,0:T(8,128)S(1)} %get-tuple-element.44), channel_id=1, source_target_pairs={{0,12},{4,0},{8,20},{12,24},{1,9},{5,13},{9,17},{13,21},{2,6},{6,1... | collective-permute-start | bytes 393224 | tf_op jit(solution)/shard_map/ppermute | solution.py:24
  117.5 4.9 %collective-permute-start.24 = (f32[2,32,512]{2,1,0:T(8,128)S(1)}, f32[2,32,512]{2,1,0:T(8,128)S(1)}, u32[]{:S(2)}, u32[]{:S(2)}) collective-permute-start(f32[2,32,512]{2,1,0:T(8,128)S(1)} %get-tuple-element.43), channel_id=1, source_target_pairs={{0,8},{4,12},{8,16},{12,20},{1,5},{5,9},{9,29},{13,17},{2,2},{6,6}... | collective-permute-start | bytes 393224 | tf_op jit(solution)/shard_map/ppermute | solution.py:24
  122.4 6.7 %collective-permute-start.25 = (f32[2,32,512]{2,1,0:T(8,128)S(1)}, f32[2,32,512]{2,1,0:T(8,128)S(1)}, u32[]{:S(2)}, u32[]{:S(2)}) collective-permute-start(f32[2,32,512]{2,1,0:T(8,128)S(1)} %get-tuple-element.42), channel_id=1, source_target_pairs={{0,4},{4,8},{8,28},{12,16},{1,1},{5,5},{9,25},{13,29},{2,14},{6,2}... | collective-permute-start | bytes 393224 | tf_op jit(solution)/shard_map/ppermute | solution.py:24
  129.1 1.9 %collective-permute-start.26 = (f32[2,32,512]{2,1,0:T(8,128)S(1)}, f32[2,32,512]{2,1,0:T(8,128)S(1)}, u32[]{:S(2)}, u32[]{:S(2)}) collective-permute-start(f32[2,32,512]{2,1,0:T(8,128)S(1)} %get-tuple-element.41), channel_id=1, source_target_pairs={{0,0},{4,4},{8,24},{12,28},{1,13},{5,1},{9,21},{13,25},{2,10},{6,1... | collective-permute-start | bytes 393224 | tf_op jit(solution)/shard_map/ppermute | solution.py:24
  131.1 0.5 collective-permute-done.25
  131.6 6.2 %collective-permute-done.26 = f32[2,32,512]{2,1,0:T(8,128)S(1)} collective-permute-done((f32[2,32,512]{2,1,0:T(8,128)S(1)}, f32[2,32,512]{2,1,0:T(8,128)S(1)}, u32[]{:S(2)}, u32[]{:S(2)}) %collective-permute-start.26) | collective-permute-done | bytes 131104 | tf_op jit(solution)/shard_map/ppermute | solution.py:24
  137.7 0.8 select_bitcast_fusion
  (48 shorter events, 0.3 us)
Async XLA Ops:
  0.8 1.9 %copy-start.6 = (f32[4,2,32,512]{3,2,1,0:T(8,128)S(1)}, f32[4,2,32,512]{3,2,1,0:T(8,128)}, u32[]{:S(2)}) copy-start(f32[4,2,32,512]{3,2,1,0:T(8,128)} %param.7) | copy-start | bytes 1572868
  0.8 1.9 %copy-start.7 = (f32[4,2,32,512]{3,2,1,0:T(8,128)S(1)}, f32[4,2,32,512]{3,2,1,0:T(8,128)}, u32[]{:S(2)}) copy-start(f32[4,2,32,512]{3,2,1,0:T(8,128)} %param.6) | copy-start | bytes 1572868
  2.8 3.0 %copy-start.9 = (f32[2,2,32,512]{3,2,1,0:T(8,128)S(1)}, f32[2,2,32,512]{3,2,1,0:T(8,128)}, u32[]{:S(2)}) copy-start(f32[2,2,32,512]{3,2,1,0:T(8,128)} %param.4) | copy-start | bytes 786436
  3.6 11.4 %collective-permute-start.1 = (f32[3,2,32,512]{3,2,1,0:T(8,128)}, f32[3,2,32,512]{3,2,1,0:T(8,128)S(1)}, u32[]{:S(2)}, u32[]{:S(2)}) collective-permute-start(f32[3,2,32,512]{3,2,1,0:T(8,128)} %pad_maximum_fusion.6), channel_id=1, source_target_pairs={{0,8},{4,12},{8,0},{12,4},{1,9},{5,13},{9,1},{13,5},{2,10},{6,14},... | collective-permute-start | bytes 1179656 | tf_op jit(solution)/shard_map/ppermute | solution.py:24
  5.9 15.0 %collective-permute-start.2 = (f32[4,2,32,512]{3,2,1,0:T(8,128)S(1)}, f32[4,2,32,512]{3,2,1,0:T(8,128)S(1)}, u32[]{:S(2)}, u32[]{:S(2)}) collective-permute-start(f32[4,2,32,512]{3,2,1,0:T(8,128)S(1)} %pad_maximum_fusion), channel_id=1, source_target_pairs={{0,12},{4,0},{8,4},{12,8},{1,13},{5,1},{9,5},{13,9},{2,14},{6,2},{... | collective-permute-start | bytes 1572872 | tf_op jit(solution)/shard_map/ppermute | solution.py:24
  11.0 9.9 %collective-permute-start = (f32[3,2,32,512]{3,2,1,0:T(8,128)}, f32[3,2,32,512]{3,2,1,0:T(8,128)S(1)}, u32[]{:S(2)}, u32[]{:S(2)}) collective-permute-start(f32[3,2,32,512]{3,2,1,0:T(8,128)} %pad_maximum_fusion.5), channel_id=1, source_target_pairs={{0,4},{4,8},{8,12},{12,0},{1,5},{5,9},{9,13},{13,1},{2,6},{6,10},{... | collective-permute-start | bytes 1179656 | tf_op jit(solution)/shard_map/ppermute | solution.py:24
  20.9 0.9 copy-start.8
  22.0 12.9 %collective-permute-start.3 = (f32[4,2,32,512]{3,2,1,0:T(8,128)S(1)}, f32[4,2,32,512]{3,2,1,0:T(8,128)S(1)}, u32[]{:S(2)}, u32[]{:S(2)}) collective-permute-start(f32[4,2,32,512]{3,2,1,0:T(8,128)S(1)} %get-tuple-element.64), channel_id=1, source_target_pairs={{0,1},{4,5},{8,9},{12,13},{1,2},{5,6},{9,10},{13,14},{2,3},{6,7},{... | collective-permute-start | bytes 1572872 | tf_op jit(solution)/shard_map/ppermute | solution.py:24
  25.4 11.7 %collective-permute-start.7 = (f32[4,2,32,512]{3,2,1,0:T(8,128)S(1)}, f32[4,2,32,512]{3,2,1,0:T(8,128)S(1)}, u32[]{:S(2)}, u32[]{:S(2)}) collective-permute-start(f32[4,2,32,512]{3,2,1,0:T(8,128)S(1)} %get-tuple-element.62), channel_id=1, source_target_pairs={{0,3},{4,7},{8,11},{12,15},{1,0},{5,4},{9,8},{13,12},{2,1},{6,5},{... | collective-permute-start | bytes 1572872 | tf_op jit(solution)/shard_map/ppermute | solution.py:24
  29.1 15.5 %collective-permute-start.5 = (f32[4,2,32,512]{3,2,1,0:T(8,128)S(1)}, f32[4,2,32,512]{3,2,1,0:T(8,128)S(1)}, u32[]{:S(2)}, u32[]{:S(2)}) collective-permute-start(f32[4,2,32,512]{3,2,1,0:T(8,128)S(1)} %get-tuple-element.64), channel_id=1, source_target_pairs={{0,3},{4,7},{8,11},{12,15},{1,0},{5,4},{9,8},{13,12},{2,1},{6,5},{... | collective-permute-start | bytes 1572872 | tf_op jit(solution)/shard_map/ppermute | solution.py:24
  32.6 12.3 %collective-permute-start.6 = (f32[4,2,32,512]{3,2,1,0:T(8,128)S(1)}, f32[4,2,32,512]{3,2,1,0:T(8,128)S(1)}, u32[]{:S(2)}, u32[]{:S(2)}) collective-permute-start(f32[4,2,32,512]{3,2,1,0:T(8,128)S(1)} %get-tuple-element.62), channel_id=1, source_target_pairs={{0,1},{4,5},{8,9},{12,13},{1,2},{5,6},{9,10},{13,14},{2,3},{6,7},{... | collective-permute-start | bytes 1572872 | tf_op jit(solution)/shard_map/ppermute | solution.py:24
  35.0 15.5 %collective-permute-start.4 = (f32[4,2,32,512]{3,2,1,0:T(8,128)S(1)}, f32[4,2,32,512]{3,2,1,0:T(8,128)S(1)}, u32[]{:S(2)}, u32[]{:S(2)}) collective-permute-start(f32[4,2,32,512]{3,2,1,0:T(8,128)S(1)} %collective-permute-done.3.refs_4_), channel_id=1, source_target_pairs={{0,1},{4,5},{8,9},{12,13},{1,2},{5,6},{9,10},{13,14},{2,3},{6,7},{... | collective-permute-start | bytes 1572872 | tf_op jit(solution)/shard_map/ppermute | solution.py:24
  37.2 13.3 %collective-permute-start.8 = (f32[4,2,32,512]{3,2,1,0:T(8,128)S(1)}, f32[4,2,32,512]{3,2,1,0:T(8,128)S(1)}, u32[]{:S(2)}, u32[]{:S(2)}) collective-permute-start(f32[4,2,32,512]{3,2,1,0:T(8,128)S(1)} %collective-permute-done.7.refs_9_), channel_id=1, source_target_pairs={{0,3},{4,7},{8,11},{12,15},{1,0},{5,4},{9,8},{13,12},{2,1},{6,5},{... | collective-permute-start | bytes 1572872 | tf_op jit(solution)/shard_map/ppermute | solution.py:24
  42.1 2.5 %collective-permute-start.9 = (f32[2,32,512]{2,1,0:T(8,128)S(1)}, f32[2,32,512]{2,1,0:T(8,128)S(1)}, u32[]{:S(2)}, u32[]{:S(2)}) collective-permute-start(f32[2,32,512]{2,1,0:T(8,128)S(1)} %get-tuple-element.16), channel_id=1, source_target_pairs={{0,496},{4,500},{8,504},{12,508},{1,497},{5,501},{9,505},{13,509},... | collective-permute-start | bytes 393224 | tf_op jit(solution)/shard_map/ppermute | solution.py:24
  44.6 5.9 %copy-start.11 = (f32[2,32,512]{2,1,0:T(8,128)}, f32[2,32,512]{2,1,0:T(8,128)S(1)}, u32[]{:S(2)}) copy-start(f32[2,32,512]{2,1,0:T(8,128)S(1)} %collective-permute-done.9) | copy-start | bytes 393220
  44.9 9.0 %copy-start = (f32[4,2,32,512]{3,2,1,0:T(8,128)}, f32[4,2,32,512]{3,2,1,0:T(8,128)S(1)}, u32[]{:S(2)}) copy-start(f32[4,2,32,512]{3,2,1,0:T(8,128)S(1)} %collective-permute-done.6.refs_7_) | copy-start | bytes 1572868
  50.5 3.4 %copy-start.2 = (f32[4,2,32,512]{3,2,1,0:T(8,128)}, f32[4,2,32,512]{3,2,1,0:T(8,128)S(1)}, u32[]{:S(2)}) copy-start(f32[4,2,32,512]{3,2,1,0:T(8,128)S(1)} %collective-permute-done.4.refs_5_) | copy-start | bytes 1572868
  50.5 3.4 %copy-start.4 = (f32[4,2,32,512]{3,2,1,0:T(8,128)}, f32[4,2,32,512]{3,2,1,0:T(8,128)S(1)}, u32[]{:S(2)}) copy-start(f32[4,2,32,512]{3,2,1,0:T(8,128)S(1)} %collective-permute-done.8.refs_8_) | copy-start | bytes 1572868
  53.9 17.9 %collective-permute-start.10 = (f32[4,2,32,512]{3,2,1,0:T(8,128)}, f32[4,2,32,512]{3,2,1,0:T(8,128)}, u32[]{:S(2)}, u32[]{:S(2)}) collective-permute-start(f32[4,2,32,512]{3,2,1,0:T(8,128)} %first_level.1), channel_id=1, source_target_pairs={{0,12},{4,8},{8,4},{12,0},{1,13},{5,9},{9,5},{13,1},{2,14},{6,10},... | collective-permute-start | bytes 1572872 | tf_op jit(solution)/shard_map/ppermute | solution.py:24
  57.1 17.1 %collective-permute-start.12 = (f32[4,2,32,512]{3,2,1,0:T(8,128)}, f32[4,2,32,512]{3,2,1,0:T(8,128)}, u32[]{:S(2)}, u32[]{:S(2)}) collective-permute-start(f32[4,2,32,512]{3,2,1,0:T(8,128)} %first_level.1), channel_id=1, source_target_pairs={{4,12},{12,4},{5,13},{13,5},{6,14},{14,6},{7,15},{15,7},{17,19},{1... | collective-permute-start | bytes 1572872 | tf_op jit(solution)/shard_map/ppermute | solution.py:24
  58.6 16.4 %collective-permute-start.11 = (f32[4,2,32,512]{3,2,1,0:T(8,128)}, f32[4,2,32,512]{3,2,1,0:T(8,128)}, u32[]{:S(2)}, u32[]{:S(2)}) collective-permute-start(f32[4,2,32,512]{3,2,1,0:T(8,128)} %first_level.1), channel_id=1, source_target_pairs={{4,0},{12,8},{5,1},{13,9},{6,2},{14,10},{7,3},{15,11},{17,16},{19,... | collective-permute-start | bytes 1572872 | tf_op jit(solution)/shard_map/ppermute | solution.py:24
  60.9 15.9 %collective-permute-start.13 = (f32[2,32,512]{2,1,0:T(8,128)S(1)}, f32[2,32,512]{2,1,0:T(8,128)S(1)}, u32[]{:S(2)}, u32[]{:S(2)}) collective-permute-start(f32[2,32,512]{2,1,0:T(8,128)S(1)} %get-tuple-element.56), channel_id=1, source_target_pairs={{0,4},{4,8},{8,12},{12,0},{1,5},{5,9},{9,13},{13,1},{2,6},{6,10},{... | collective-permute-start | bytes 393224 | tf_op jit(solution)/shard_map/ppermute | solution.py:24
  66.9 9.9 %collective-permute-start.14 = (f32[2,32,512]{2,1,0:T(8,128)S(1)}, f32[2,32,512]{2,1,0:T(8,128)S(1)}, u32[]{:S(2)}, u32[]{:S(2)}) collective-permute-start(f32[2,32,512]{2,1,0:T(8,128)S(1)} %get-tuple-element.55), channel_id=1, source_target_pairs={{0,8},{4,12},{8,0},{12,4},{1,9},{5,13},{9,1},{13,5},{2,10},{6,14},... | collective-permute-start | bytes 393224 | tf_op jit(solution)/shard_map/ppermute | solution.py:24
  71.8 20.0 %copy-start.1 = (f32[4,2,32,512]{3,2,1,0:T(8,128)S(1)}, f32[4,2,32,512]{3,2,1,0:T(8,128)}, u32[]{:S(2)}) copy-start(f32[4,2,32,512]{3,2,1,0:T(8,128)} %copy-done) | copy-start | bytes 1572868
  71.8 20.0 %copy-start.3 = (f32[4,2,32,512]{3,2,1,0:T(8,128)S(1)}, f32[4,2,32,512]{3,2,1,0:T(8,128)}, u32[]{:S(2)}) copy-start(f32[4,2,32,512]{3,2,1,0:T(8,128)} %copy-done.2) | copy-start | bytes 1572868
  71.8 20.0 %copy-start.5 = (f32[4,2,32,512]{3,2,1,0:T(8,128)S(1)}, f32[4,2,32,512]{3,2,1,0:T(8,128)}, u32[]{:S(2)}) copy-start(f32[4,2,32,512]{3,2,1,0:T(8,128)} %copy-done.4) | copy-start | bytes 1572868
  71.8 7.0 %collective-permute-start.15 = (f32[2,32,512]{2,1,0:T(8,128)S(1)}, f32[2,32,512]{2,1,0:T(8,128)S(1)}, u32[]{:S(2)}, u32[]{:S(2)}) collective-permute-start(f32[2,32,512]{2,1,0:T(8,128)S(1)} %get-tuple-element.54), channel_id=1, source_target_pairs={{0,12},{4,0},{8,4},{12,8},{1,13},{5,1},{9,5},{13,9},{2,14},{6,2},{... | collective-permute-start | bytes 393224 | tf_op jit(solution)/shard_map/ppermute | solution.py:24
  78.8 12.9 %collective-permute-start.16 = (f32[4,2,32,512]{3,2,1,0:T(8,128)S(1)}, f32[4,2,32,512]{3,2,1,0:T(8,128)S(1)}, u32[]{:S(2)}, u32[]{:S(2)}) collective-permute-start(f32[4,2,32,512]{3,2,1,0:T(8,128)S(1)} %get-tuple-element.24.refs_2_), channel_id=1, source_target_pairs={{0,1},{4,5},{8,9},{12,13},{1,2},{5,6},{9,10},{13,14},{2,3},{6,7},{... | collective-permute-start | bytes 1572872 | tf_op jit(solution)/shard_map/ppermute | solution.py:24
  80.7 16.8 %collective-permute-start.21 = (f32[4,2,32,512]{3,2,1,0:T(8,128)S(1)}, f32[4,2,32,512]{3,2,1,0:T(8,128)S(1)}, u32[]{:S(2)}, u32[]{:S(2)}) collective-permute-start(f32[4,2,32,512]{3,2,1,0:T(8,128)S(1)} %get-tuple-element.29.refs_6_), channel_id=1, source_target_pairs={{0,3},{4,7},{8,11},{12,15},{1,0},{5,4},{9,8},{13,12},{2,1},{6,5},{... | collective-permute-start | bytes 1572872 | tf_op jit(solution)/shard_map/ppermute | solution.py:24
  85.8 16.8 %collective-permute-start.19 = (f32[4,2,32,512]{3,2,1,0:T(8,128)S(1)}, f32[4,2,32,512]{3,2,1,0:T(8,128)S(1)}, u32[]{:S(2)}, u32[]{:S(2)}) collective-permute-start(f32[4,2,32,512]{3,2,1,0:T(8,128)S(1)} %get-tuple-element.24.refs_2_), channel_id=1, source_target_pairs={{0,3},{4,7},{8,11},{12,15},{1,0},{5,4},{9,8},{13,12},{2,1},{6,5},{... | collective-permute-start | bytes 1572872 | tf_op jit(solution)/shard_map/ppermute | solution.py:24
  88.5 14.2 %collective-permute-start.20 = (f32[4,2,32,512]{3,2,1,0:T(8,128)S(1)}, f32[4,2,32,512]{3,2,1,0:T(8,128)S(1)}, u32[]{:S(2)}, u32[]{:S(2)}) collective-permute-start(f32[4,2,32,512]{3,2,1,0:T(8,128)S(1)} %get-tuple-element.29.refs_6_), channel_id=1, source_target_pairs={{0,1},{4,5},{8,9},{12,13},{1,2},{5,6},{9,10},{13,14},{2,3},{6,7},{... | collective-permute-start | bytes 1572872 | tf_op jit(solution)/shard_map/ppermute | solution.py:24
  94.3 16.3 %collective-permute-start.17 = (f32[4,2,32,512]{3,2,1,0:T(8,128)S(1)}, f32[4,2,32,512]{3,2,1,0:T(8,128)S(1)}, u32[]{:S(2)}, u32[]{:S(2)}) collective-permute-start(f32[4,2,32,512]{3,2,1,0:T(8,128)S(1)} %first_level_side.1.refs_0_), channel_id=1, source_target_pairs={{4,0},{12,8},{5,1},{13,9},{6,2},{14,10},{7,3},{15,11},{17,16},{19,... | collective-permute-start | bytes 1572872 | tf_op jit(solution)/shard_map/ppermute | solution.py:24
  95.6 15.0 %collective-permute-start.18 = (f32[4,2,32,512]{3,2,1,0:T(8,128)S(1)}, f32[4,2,32,512]{3,2,1,0:T(8,128)S(1)}, u32[]{:S(2)}, u32[]{:S(2)}) collective-permute-start(f32[4,2,32,512]{3,2,1,0:T(8,128)S(1)} %collective-permute-done.16.refs_3_), channel_id=1, source_target_pairs={{0,1},{4,5},{8,9},{12,13},{1,2},{5,6},{9,10},{13,14},{2,3},{6,7},{... | collective-permute-start | bytes 1572872 | tf_op jit(solution)/shard_map/ppermute | solution.py:24
  97.5 13.0 %collective-permute-start.22 = (f32[4,2,32,512]{3,2,1,0:T(8,128)S(1)}, f32[4,2,32,512]{3,2,1,0:T(8,128)S(1)}, u32[]{:S(2)}, u32[]{:S(2)}) collective-permute-start(f32[4,2,32,512]{3,2,1,0:T(8,128)S(1)} %collective-permute-done.21.refs_9_), channel_id=1, source_target_pairs={{0,3},{4,7},{8,11},{12,15},{1,0},{5,4},{9,8},{13,12},{2,1},{6,5},{... | collective-permute-start | bytes 1572872 | tf_op jit(solution)/shard_map/ppermute | solution.py:24
  115.4 22.4 %copy-start.10 = (f32[2,2,32,512]{3,2,1,0:T(8,128)S(1)}, f32[2,2,32,512]{3,2,1,0:T(8,128)}, u32[]{:S(2)}) copy-start(f32[2,2,32,512]{3,2,1,0:T(8,128)} %param.4) | copy-start | bytes 786436
  115.5 15.6 %collective-permute-start.23 = (f32[2,32,512]{2,1,0:T(8,128)S(1)}, f32[2,32,512]{2,1,0:T(8,128)S(1)}, u32[]{:S(2)}, u32[]{:S(2)}) collective-permute-start(f32[2,32,512]{2,1,0:T(8,128)S(1)} %get-tuple-element.44), channel_id=1, source_target_pairs={{0,12},{4,0},{8,20},{12,24},{1,9},{5,13},{9,17},{13,21},{2,6},{6,1... | collective-permute-start | bytes 393224 | tf_op jit(solution)/shard_map/ppermute | solution.py:24
  117.5 13.5 %collective-permute-start.24 = (f32[2,32,512]{2,1,0:T(8,128)S(1)}, f32[2,32,512]{2,1,0:T(8,128)S(1)}, u32[]{:S(2)}, u32[]{:S(2)}) collective-permute-start(f32[2,32,512]{2,1,0:T(8,128)S(1)} %get-tuple-element.43), channel_id=1, source_target_pairs={{0,8},{4,12},{8,16},{12,20},{1,5},{5,9},{9,29},{13,17},{2,2},{6,6}... | collective-permute-start | bytes 393224 | tf_op jit(solution)/shard_map/ppermute | solution.py:24
  122.4 9.2 %collective-permute-start.25 = (f32[2,32,512]{2,1,0:T(8,128)S(1)}, f32[2,32,512]{2,1,0:T(8,128)S(1)}, u32[]{:S(2)}, u32[]{:S(2)}) collective-permute-start(f32[2,32,512]{2,1,0:T(8,128)S(1)} %get-tuple-element.42), channel_id=1, source_target_pairs={{0,4},{4,8},{8,28},{12,16},{1,1},{5,5},{9,25},{13,29},{2,14},{6,2}... | collective-permute-start | bytes 393224 | tf_op jit(solution)/shard_map/ppermute | solution.py:24
  129.1 8.7 %collective-permute-start.26 = (f32[2,32,512]{2,1,0:T(8,128)S(1)}, f32[2,32,512]{2,1,0:T(8,128)S(1)}, u32[]{:S(2)}, u32[]{:S(2)}) collective-permute-start(f32[2,32,512]{2,1,0:T(8,128)S(1)} %get-tuple-element.41), channel_id=1, source_target_pairs={{0,0},{4,4},{8,24},{12,28},{1,13},{5,1},{9,21},{13,25},{2,10},{6,1... | collective-permute-start | bytes 393224 | tf_op jit(solution)/shard_map/ppermute | solution.py:24

commit v7 on v6

--- a/solution.py
+++ b/solution.py
@@ -105,9 +105,10 @@
 
 def first_kernel(with_diag, *refs):
     messages = refs[0:4]
-    greens = refs[4:7]
-    parts = refs[7:10]
-    lefts = refs[10:-6]
+    below, above, far_green, far_part = refs[4:8]
+    greens = (below.at[0], far_green, above.at[0])
+    parts = (below.at[1], far_part, above.at[1])
+    lefts = refs[8:-6]
     out_ref = refs[-6]
     green_high, green_low, part_high, part_low, left = refs[-5:]
     core, line, spot = place()
@@ -136,11 +137,11 @@
 
 
 def second_kernel(*refs):
-    side_ref, side_there_ref = refs[0:2]
-    pivots = refs[2:6]
-    panels = refs[6:10]
-    out_ref = refs[10]
-    pivot_high, pivot_low, panel_high, panel_low = refs[11:]
+    side_ref, side_there_ref, own, below, above, far_pivot, far_panel = refs[0:7]
+    pivots = (own.at[0], below.at[0], far_pivot, above.at[0])
+    panels = (own.at[1], below.at[1], far_panel, above.at[1])
+    out_ref = refs[7]
+    pivot_high, pivot_low, panel_high, panel_low = refs[8:]
     core, line, spot = place()
     rows = side_ref.shape[2]
     width = side_ref.shape[3]
@@ -209,20 +210,20 @@
         blocks = [green, jnp.where(with_lower, down, up), jnp.where(odd == 0, lower[2], upper[2])]
         return jnp.stack(blocks + [diag_even[1]] if step in (0, 3) else blocks)
 
-    def ringed(first, second):
-        first_one = permuted(first, slabs, along_line(1))
-        second_three = permuted(second, slabs, along_line(-1))
-        first_two = permuted(first_one, slabs, along_line(1))
-        second_two = permuted(second_three, slabs, along_line(-1))
-        second_one = permuted(second, slabs, along_line(1))
-        first_three = permuted(first, slabs, along_line(-1))
-        return [first_one, first_two, first_three], [second_one, second_two, second_three]
+    def ringed(pair, moved=None):
+        below = permuted(pair, slabs, along_line(1))
+        above = permuted(pair, slabs, along_line(-1))
+        first, second = below[0], above[1]
+        if moved is not None:
+            moved, _ = lax.optimization_barrier((moved, pair))
+            moved = permuted(moved, slabs, slab_below)
+            first, _ = lax.optimization_barrier((first, moved))
+            second, _ = lax.optimization_barrier((second, moved))
+        return moved, (below, above, permuted(first, slabs, along_line(1)), permuted(second, slabs, along_line(-1)))
 
     messages = [message(0)] + [permuted(message(step), slabs, along_spot(step)) for step in range(1, 4)]
-    first, second = (jnp.stack([piece[side] for piece in messages]) for side in range(2))
-    greens, parts = ringed(first, second)
-    own_row, next_row, _ = lax.optimization_barrier((upper[0], lower[0], greens[0]))
-    next_row = permuted(next_row, slabs, slab_below)
+    whole = jnp.stack([jnp.stack([piece[side] for piece in messages]) for side in range(2)])
+    next_row, ring = ringed(whole, lower[0])
     four = jax.ShapeDtypeStruct((4, 2, rows, width), jnp.float32)
     wide = pltpu.VMEM((width, 2 * width), jnp.bfloat16)
 
@@ -231,19 +232,18 @@
         return pl.pallas_call(
             functools.partial(first_kernel, with_diag),
             out_shape=four,
-            in_specs=vmem(10 + len(lefts)),
+            in_specs=vmem(8 + len(lefts)),
             out_specs=vmem(1)[0],
             scratch_shapes=[wide] * 4 + [pltpu.VMEM((2, 4 * rows, width), jnp.float32)],
             compiler_params=pltpu.CompilerParams(vmem_limit_bytes=VMEM_LIMIT),
             cost_estimate=pl.CostEstimate(flops=flops, bytes_accessed=12 * width * width, transcendentals=0),
             name="first_level" if with_diag else "first_level_side",
-        )(message, *messages[1:], *greens, *parts, *lefts)
-
-    ready, next_row = lax.optimization_barrier((messages[0], next_row))
-    main = rows_through(True, ready, [])
+        )(message, *messages[1:], *ring, *lefts)
+
+    main = rows_through(True, messages[0], [])
 
     def late(step):
-        return jnp.where(lax.rem(spot + step, 4) < 2, own_row, next_row)
+        return jnp.where(lax.rem(spot + step, 4) < 2, upper[0], next_row)
 
     lates = [late(0)] + [permuted(late(step), slabs, along_spot(step)) for step in range(1, 4)]
 
@@ -254,19 +254,20 @@
     panel = jnp.where(outer, main, cross_there)
     pivot = jnp.where(outer, cross_there + term_out, main + term_there)
     pivot, *lates = lax.optimization_barrier((pivot, *lates))
-    pivots, panels = ringed(pivot, panel)
-    *lates, _ = lax.optimization_barrier((*lates, pivots[0]))
+    pair_own = jnp.stack([pivot, panel])
+    _, pairs = ringed(pair_own)
+    *lates, _ = lax.optimization_barrier((*lates, pair_own))
     side = rows_through(False, messages[0], lates)
     side_there = permuted(side, slabs, outwards)
     out = pl.pallas_call(
         second_kernel,
         out_shape=four,
-        in_specs=vmem(10),
+        in_specs=vmem(7),
         out_specs=vmem(1)[0],
         scratch_shapes=[wide] * 4,
         compiler_params=pltpu.CompilerParams(vmem_limit_bytes=VMEM_LIMIT),
         name="second_level",
-    )(side, side_there, pivot, *pivots, panel, *panels)
+    )(side, side_there, pair_own, *pairs)
     ends = [permuted(out[step], slabs, to_owner(step)) for step in range(4)]
 
     def ended(code):

time: 139 us -> 146 us (1.050)
  the two profiles are of different devices: /device:TPU:112 before, /device:TPU:229 now
where the time goes in v7:
time: 146 us; the launch traced here: 145 us
  starting transfers between devices  82 us (56%)
  waiting for transfers between devices  42.6 us (29%)
  Pallas kernels  10.7 us (7%)
  other arithmetic  5.74 us (4%)
  local copies, waits for them, and re-layouts  2.45 us (2%)
    ppermute x23, starting transfers between devices, permuted(): return lax.ppermute(value, ('slab', 'orb'), pairs)  82 us
    ppermute x23, waiting for transfers between devices, permuted(): return lax.ppermute(value, ('slab', 'orb'), pairs)  42.6 us
    pallas_call x2, Pallas kernels, rows_through(): pl.pallas_call(functools.partial(first_kernel, with_diag), out_shape=four...  5.84 us
    pallas_call x1, Pallas kernels, shards(): pl.pallas_call(second_kernel, out_shape=four, in_specs=vmem(7), out_specs...  4.88 us
  transfers between devices with their start and end apart: 23, of which 13 were waited for; matrix products, arithmetic and copies ran while one was open for 3% of the time, Pallas kernels for 2%

profile of v7, /device:TPU:229, one launch (start us, length us, event | category | flops | bytes accessed | tf_op | source)
XLA Modules:
  0.0 144.9 jit_solution(4660050458987055826)
XLA Ops:
  0.8 1.2 constant_dynamic-slice_fusion
  2.1 0.2 copy-done.8
  2.4 0.8 pad_maximum_fusion.7
  3.2 2.1 %collective-permute-start.1 = (f32[3,2,32,512]{3,2,1,0:T(8,128)}, f32[3,2,32,512]{3,2,1,0:T(8,128)S(1)}, u32[]{:S(2)}, u32[]{:S(2)}) collective-permute-start(f32[3,2,32,512]{3,2,1,0:T(8,128)} %pad_maximum_fusion.7), channel_id=1, source_target_pairs={{0,8},{4,12},{8,0},{12,4},{1,9},{5,13},{9,1},{13,5},{2,10},{6,14},... | collective-permute-start | bytes 1179656 | tf_op jit(solution)/shard_map/ppermute | solution.py:24
  5.4 3.8 %collective-permute-start.2 = (f32[4,2,32,512]{3,2,1,0:T(8,128)S(1)}, f32[4,2,32,512]{3,2,1,0:T(8,128)S(1)}, u32[]{:S(2)}, u32[]{:S(2)}) collective-permute-start(f32[4,2,32,512]{3,2,1,0:T(8,128)S(1)} %pad_maximum_fusion.2), channel_id=1, source_target_pairs={{0,12},{4,0},{8,4},{12,8},{1,13},{5,1},{9,5},{13,9},{2,14},{6,2},{... | collective-permute-start | bytes 1572872 | tf_op jit(solution)/shard_map/ppermute | solution.py:24
  9.2 0.8 pad_maximum_fusion.6
  10.0 1.9 %collective-permute-start = (f32[3,2,32,512]{3,2,1,0:T(8,128)}, f32[3,2,32,512]{3,2,1,0:T(8,128)S(1)}, u32[]{:S(2)}, u32[]{:S(2)}) collective-permute-start(f32[3,2,32,512]{3,2,1,0:T(8,128)} %pad_maximum_fusion.6), channel_id=1, source_target_pairs={{0,4},{4,8},{8,12},{12,0},{1,5},{5,9},{9,13},{13,1},{2,6},{6,10},{... | collective-permute-start | bytes 1179656 | tf_op jit(solution)/shard_map/ppermute | solution.py:24
  11.9 1.8 %collective-permute-done.1.refs_2_ = f32[3,2,32,512]{3,2,1,0:T(8,128)S(1)} collective-permute-done((f32[3,2,32,512]{3,2,1,0:T(8,128)}, f32[3,2,32,512]{3,2,1,0:T(8,128)S(1)}, u32[]{:S(2)}, u32[]{:S(2)}) %collective-permute-start.1) | collective-permute-done | bytes 393248 | tf_op jit(solution)/shard_map/ppermute | solution.py:24
  13.7 5.3 %collective-permute-done.refs_1_ = f32[3,2,32,512]{3,2,1,0:T(8,128)S(1)} collective-permute-done((f32[3,2,32,512]{3,2,1,0:T(8,128)}, f32[3,2,32,512]{3,2,1,0:T(8,128)S(1)}, u32[]{:S(2)}, u32[]{:S(2)}) %collective-permute-start) | collective-permute-done | bytes 393248 | tf_op jit(solution)/shard_map/ppermute | solution.py:24
  19.0 0.7 copy-done
  19.7 0.2 fusion.3
  20.0 3.2 %collective-permute-start.3 = (f32[2,4,2,32,512]{4,3,2,1,0:T(8,128)S(1)}, f32[2,4,2,32,512]{4,3,2,1,0:T(8,128)S(1)}, u32[]{:S(2)}, u32[]{:S(2)}) collective-permute-start(f32[2,4,2,32,512]{4,3,2,1,0:T(8,128)S(1)} %pad_maximum_fusion), channel_id=1, source_target_pairs={{0,1},{4,5},{8,9},{12,13},{1,2},{5,6},{9,10},{13,14},{2,3},{6,7},{... | collective-permute-start | bytes 3145736 | tf_op jit(solution)/shard_map/ppermute | solution.py:24
  23.2 3.4 %collective-permute-start.4 = (f32[2,4,2,32,512]{4,3,2,1,0:T(8,128)S(1)}, f32[2,4,2,32,512]{4,3,2,1,0:T(8,128)S(1)}, u32[]{:S(2)}, u32[]{:S(2)}) collective-permute-start(f32[2,4,2,32,512]{4,3,2,1,0:T(8,128)S(1)} %pad_maximum_fusion), channel_id=1, source_target_pairs={{0,3},{4,7},{8,11},{12,15},{1,0},{5,4},{9,8},{13,12},{2,1},{6,5},{... | collective-permute-start | bytes 3145736 | tf_op jit(solution)/shard_map/ppermute | solution.py:24
  26.6 4.2 %collective-permute-start.5 = (f32[2,32,512]{2,1,0:T(8,128)S(1)}, f32[2,32,512]{2,1,0:T(8,128)S(1)}, u32[]{:S(2)}, u32[]{:S(2)}) collective-permute-start(f32[2,32,512]{2,1,0:T(8,128)S(1)} %get-tuple-element.15), channel_id=1, source_target_pairs={{0,496},{4,500},{8,504},{12,508},{1,497},{5,501},{9,505},{13,509},... | collective-permute-start | bytes 393224 | tf_op jit(solution)/shard_map/ppermute | solution.py:24
  30.8 6.1 %collective-permute-done.3.refs_4_ = f32[2,4,2,32,512]{4,3,2,1,0:T(8,128)S(1)} collective-permute-done((f32[2,4,2,32,512]{4,3,2,1,0:T(8,128)S(1)}, f32[2,4,2,32,512]{4,3,2,1,0:T(8,128)S(1)}, u32[]{:S(2)}, u32[]{:S(2)}) %collective-permute-start.3) | collective-permute-done | bytes 1048608 | tf_op jit(solution)/shard_map/ppermute | solution.py:24
  36.9 2.4 %collective-permute-start.6 = (f32[4,2,32,512]{3,2,1,0:T(8,128)S(1)}, f32[4,2,32,512]{3,2,1,0:T(8,128)S(1)}, u32[]{:S(2)}, u32[]{:S(2)}) collective-permute-start(f32[4,2,32,512]{3,2,1,0:T(8,128)S(1)} %slice_bitcast_fusion.3), channel_id=1, source_target_pairs={{0,1},{4,5},{8,9},{12,13},{1,2},{5,6},{9,10},{13,14},{2,3},{6,7},{... | collective-permute-start | bytes 1572872 | tf_op jit(solution)/shard_map/ppermute | solution.py:24
  39.4 4.3 %collective-permute-start.7 = (f32[4,2,32,512]{3,2,1,0:T(8,128)S(1)}, f32[4,2,32,512]{3,2,1,0:T(8,128)S(1)}, u32[]{:S(2)}, u32[]{:S(2)}) collective-permute-start(f32[4,2,32,512]{3,2,1,0:T(8,128)S(1)} %slice_bitcast_fusion.2), channel_id=1, source_target_pairs={{0,3},{4,7},{8,11},{12,15},{1,0},{5,4},{9,8},{13,12},{2,1},{6,5},{... | collective-permute-start | bytes 1572872 | tf_op jit(solution)/shard_map/ppermute | solution.py:24
  43.7 4.6 %collective-permute-done.6.refs_6_ = f32[4,2,32,512]{3,2,1,0:T(8,128)S(1)} collective-permute-done((f32[4,2,32,512]{3,2,1,0:T(8,128)S(1)}, f32[4,2,32,512]{3,2,1,0:T(8,128)S(1)}, u32[]{:S(2)}, u32[]{:S(2)}) %collective-permute-start.6) | collective-permute-done | bytes 524320 | tf_op jit(solution)/shard_map/ppermute | solution.py:24
  48.2 1.5 %collective-permute-done.7.refs_7_ = f32[4,2,32,512]{3,2,1,0:T(8,128)S(1)} collective-permute-done((f32[4,2,32,512]{3,2,1,0:T(8,128)S(1)}, f32[4,2,32,512]{3,2,1,0:T(8,128)S(1)}, u32[]{:S(2)}, u32[]{:S(2)}) %collective-permute-start.7) | collective-permute-done | bytes 524320 | tf_op jit(solution)/shard_map/ppermute | solution.py:24
  49.8 3.4 %first_level.1 = f32[4,2,32,512]{3,2,1,0:T(8,128)} custom-call(f32[4,2,32,512]{3,2,1,0:T(8,128)S(1)} %get-tuple-element.60.refs_0_, f32[3,2,32,512]{3,2,1,0:T(8,128)S(1)} %copy-done.1, f32[3,2,32,512]{3,2,1,0:T(8,128)S(1)} %collective-permute-done.1.refs_2_, f32[4,2,32,512]{3,2,1,0:T(8,128)S(1)} %collective-permute-done.2.refs_3_, ...), custom_call_target="tpu_custom_call" | custom-call | flops 1610612736 | bytes 3145728 | tf_op jit(solution)/shard_map/first_level/pallas_call | solution.py:232
  53.1 3.0 %collective-permute-start.8 = (f32[4,2,32,512]{3,2,1,0:T(8,128)}, f32[4,2,32,512]{3,2,1,0:T(8,128)}, u32[]{:S(2)}, u32[]{:S(2)}) collective-permute-start(f32[4,2,32,512]{3,2,1,0:T(8,128)} %first_level.1), channel_id=1, source_target_pairs={{0,12},{4,8},{8,4},{12,0},{1,13},{5,9},{9,5},{13,1},{2,14},{6,10},... | collective-permute-start | bytes 1572872 | tf_op jit(solution)/shard_map/ppermute | solution.py:24
  56.2 1.5 %collective-permute-start.10 = (f32[4,2,32,512]{3,2,1,0:T(8,128)}, f32[4,2,32,512]{3,2,1,0:T(8,128)}, u32[]{:S(2)}, u32[]{:S(2)}) collective-permute-start(f32[4,2,32,512]{3,2,1,0:T(8,128)} %first_level.1), channel_id=1, source_target_pairs={{4,12},{12,4},{5,13},{13,5},{6,14},{14,6},{7,15},{15,7},{17,19},{1... | collective-permute-start | bytes 1572872 | tf_op jit(solution)/shard_map/ppermute | solution.py:24
  57.7 1.3 collective-permute-start.9
  59.0 1.0 bitcast_select_fusion
  60.0 6.1 %collective-permute-start.11 = (f32[2,32,512]{2,1,0:T(8,128)S(1)}, f32[2,32,512]{2,1,0:T(8,128)S(1)}, u32[]{:S(2)}, u32[]{:S(2)}) collective-permute-start(f32[2,32,512]{2,1,0:T(8,128)S(1)} %get-tuple-element.38), channel_id=1, source_target_pairs={{0,4},{4,8},{8,12},{12,0},{1,5},{5,9},{9,13},{13,1},{2,6},{6,10},{... | collective-permute-start | bytes 393224 | tf_op jit(solution)/shard_map/ppermute | solution.py:24
  66.1 4.3 %collective-permute-start.12 = (f32[2,32,512]{2,1,0:T(8,128)S(1)}, f32[2,32,512]{2,1,0:T(8,128)S(1)}, u32[]{:S(2)}, u32[]{:S(2)}) collective-permute-start(f32[2,32,512]{2,1,0:T(8,128)S(1)} %get-tuple-element.37), channel_id=1, source_target_pairs={{0,8},{4,12},{8,0},{12,4},{1,9},{5,13},{9,1},{13,5},{2,10},{6,14},... | collective-permute-start | bytes 393224 | tf_op jit(solution)/shard_map/ppermute | solution.py:24
  70.4 2.0 %collective-permute-start.13 = (f32[2,32,512]{2,1,0:T(8,128)S(1)}, f32[2,32,512]{2,1,0:T(8,128)S(1)}, u32[]{:S(2)}, u32[]{:S(2)}) collective-permute-start(f32[2,32,512]{2,1,0:T(8,128)S(1)} %get-tuple-element.36), channel_id=1, source_target_pairs={{0,12},{4,0},{8,4},{12,8},{1,13},{5,1},{9,5},{13,9},{2,14},{6,2},{... | collective-permute-start | bytes 393224 | tf_op jit(solution)/shard_map/ppermute | solution.py:24
  72.3 1.4 collective-permute-done.9
  73.7 1.8 %select_bitcast_fusion = (f32[1,4,2,32,512]{4,3,2,1,0:T(8,128)S(1)}, f32[4,2,32,512]{3,2,1,0:T(8,128)S(1)}) fusion(f32[4,2,32,512]{3,2,1,0:T(8,128)} %first_level.1, f32[4,2,32,512]{3,2,1,0:T(8,128)} %collective-permute-done.8, pred[]{:T(512)S(6)} %eq.93, f32[4,2,32,512]{3,2,1,0:T(8,128)} %collective-permute-done.10, f32[4,2,32,512]{3,2,1,0:T(8,128)} %collective-permute-done.9), kind=kLoop, calls=%fused_computation.15 | loop fusion | flops 524288 | bytes 3145729 | tf_op jit(solution)/shard_map/stack | solution.py:257
  75.5 1.1 collective-permute-done.13.refs_11_
  76.7 2.3 %collective-permute-start.15 = (f32[2,4,2,32,512]{4,3,2,1,0:T(8,128)S(1)}, f32[2,4,2,32,512]{4,3,2,1,0:T(8,128)S(1)}, u32[]{:S(2)}, u32[]{:S(2)}) collective-permute-start(f32[2,4,2,32,512]{4,3,2,1,0:T(8,128)S(1)} %pad_maximum_fusion.1.refs_2_), channel_id=1, source_target_pairs={{0,1},{4,5},{8,9},{12,13},{1,2},{5,6},{9,10},{13,14},{2,3},{6,7},{... | collective-permute-start | bytes 3145736 | tf_op jit(solution)/shard_map/ppermute | solution.py:24
  79.0 4.4 %collective-permute-start.16 = (f32[2,4,2,32,512]{4,3,2,1,0:T(8,128)S(1)}, f32[2,4,2,32,512]{4,3,2,1,0:T(8,128)S(1)}, u32[]{:S(2)}, u32[]{:S(2)}) collective-permute-start(f32[2,4,2,32,512]{4,3,2,1,0:T(8,128)S(1)} %pad_maximum_fusion.1.refs_2_), channel_id=1, source_target_pairs={{0,3},{4,7},{8,11},{12,15},{1,0},{5,4},{9,8},{13,12},{2,1},{6,5},{... | collective-permute-start | bytes 3145736 | tf_op jit(solution)/shard_map/ppermute | solution.py:24
  83.5 2.5 %first_level_side.1.refs_0_ = f32[4,2,32,512]{3,2,1,0:T(8,128)S(1)} custom-call(f32[4,2,32,512]{3,2,1,0:T(8,128)S(1)} %get-tuple-element.60.refs_0_, f32[3,2,32,512]{3,2,1,0:T(8,128)S(1)} %copy-done.2, f32[3,2,32,512]{3,2,1,0:T(8,128)S(1)} %collective-permute-done.1.refs_2_, f32[4,2,32,512]{3,2,1,0:T(8,128)S(1)} %collective-permute-done.2.refs_3_, ...), custom_call_target="tpu_custom_call" | custom-call | flops 1610612736 | bytes 3145728 | tf_op jit(solution)/shard_map/first_level_side/pallas_call | solution.py:232
  86.0 1.3 collective-permute-start.14
  87.3 6.4 %collective-permute-done.15.refs_3_ = f32[2,4,2,32,512]{4,3,2,1,0:T(8,128)S(1)} collective-permute-done((f32[2,4,2,32,512]{4,3,2,1,0:T(8,128)S(1)}, f32[2,4,2,32,512]{4,3,2,1,0:T(8,128)S(1)}, u32[]{:S(2)}, u32[]{:S(2)}) %collective-permute-start.15) | collective-permute-done | bytes 1048608 | tf_op jit(solution)/shard_map/ppermute | solution.py:24
  93.7 1.9 %collective-permute-start.17 = (f32[4,2,32,512]{3,2,1,0:T(8,128)S(1)}, f32[4,2,32,512]{3,2,1,0:T(8,128)S(1)}, u32[]{:S(2)}, u32[]{:S(2)}) collective-permute-start(f32[4,2,32,512]{3,2,1,0:T(8,128)S(1)} %slice_bitcast_fusion.1), channel_id=1, source_target_pairs={{0,1},{4,5},{8,9},{12,13},{1,2},{5,6},{9,10},{13,14},{2,3},{6,7},{... | collective-permute-start | bytes 1572872 | tf_op jit(solution)/shard_map/ppermute | solution.py:24
  95.7 4.6 %collective-permute-start.18 = (f32[4,2,32,512]{3,2,1,0:T(8,128)S(1)}, f32[4,2,32,512]{3,2,1,0:T(8,128)S(1)}, u32[]{:S(2)}, u32[]{:S(2)}) collective-permute-start(f32[4,2,32,512]{3,2,1,0:T(8,128)S(1)} %slice_bitcast_fusion), channel_id=1, source_target_pairs={{0,3},{4,7},{8,11},{12,15},{1,0},{5,4},{9,8},{13,12},{2,1},{6,5},{... | collective-permute-start | bytes 1572872 | tf_op jit(solution)/shard_map/ppermute | solution.py:24
  100.3 0.4 collective-permute-done.14.refs_1_
  100.8 4.1 %collective-permute-done.17.refs_5_ = f32[4,2,32,512]{3,2,1,0:T(8,128)S(1)} collective-permute-done((f32[4,2,32,512]{3,2,1,0:T(8,128)S(1)}, f32[4,2,32,512]{3,2,1,0:T(8,128)S(1)}, u32[]{:S(2)}, u32[]{:S(2)}) %collective-permute-start.17) | collective-permute-done | bytes 524320 | tf_op jit(solution)/shard_map/ppermute | solution.py:24
  104.9 4.1 %collective-permute-done.18.refs_6_ = f32[4,2,32,512]{3,2,1,0:T(8,128)S(1)} collective-permute-done((f32[4,2,32,512]{3,2,1,0:T(8,128)S(1)}, f32[4,2,32,512]{3,2,1,0:T(8,128)S(1)}, u32[]{:S(2)}, u32[]{:S(2)}) %collective-permute-start.18) | collective-permute-done | bytes 524320 | tf_op jit(solution)/shard_map/ppermute | solution.py:24
  109.0 4.9 %second_level.1 = f32[4,2,32,512]{3,2,1,0:T(8,128)S(1)} custom-call(f32[4,2,32,512]{3,2,1,0:T(8,128)S(1)} %first_level_side.1.refs_0_, f32[4,2,32,512]{3,2,1,0:T(8,128)S(1)} %collective-permute-done.14.refs_1_, f32[2,4,2,32,512]{4,3,2,1,0:T(8,128)S(1)} %pad_maximum_fusion.1.refs_2_, f32[2,4,2,32,512]{4,3,2,1,0:T(8,128)S(1)} %collective-permute-done.15.refs_3_, ...), custom_call_target="tpu_custom_call" | custom-call | tf_op jit(solution)/shard_map/second_level/pallas_call | solution.py:262
  113.9 15.0 %collective-permute-start.19 = (f32[2,32,512]{2,1,0:T(8,128)S(1)}, f32[2,32,512]{2,1,0:T(8,128)S(1)}, u32[]{:S(2)}, u32[]{:S(2)}) collective-permute-start(f32[2,32,512]{2,1,0:T(8,128)S(1)} %get-tuple-element.46), channel_id=1, source_target_pairs={{0,12},{4,0},{8,20},{12,24},{1,9},{5,13},{9,17},{13,21},{2,6},{6,1... | collective-permute-start | bytes 393224 | tf_op jit(solution)/shard_map/ppermute | solution.py:24
  129.0 5.4 %collective-permute-start.20 = (f32[2,32,512]{2,1,0:T(8,128)S(1)}, f32[2,32,512]{2,1,0:T(8,128)S(1)}, u32[]{:S(2)}, u32[]{:S(2)}) collective-permute-start(f32[2,32,512]{2,1,0:T(8,128)S(1)} %get-tuple-element.45), channel_id=1, source_target_pairs={{0,8},{4,12},{8,16},{12,20},{1,5},{5,9},{9,29},{13,17},{2,2},{6,6}... | collective-permute-start | bytes 393224 | tf_op jit(solution)/shard_map/ppermute | solution.py:24
  134.4 1.9 %collective-permute-start.21 = (f32[2,32,512]{2,1,0:T(8,128)S(1)}, f32[2,32,512]{2,1,0:T(8,128)S(1)}, u32[]{:S(2)}, u32[]{:S(2)}) collective-permute-start(f32[2,32,512]{2,1,0:T(8,128)S(1)} %get-tuple-element.44), channel_id=1, source_target_pairs={{0,4},{4,8},{8,28},{12,16},{1,1},{5,5},{9,25},{13,29},{2,14},{6,2}... | collective-permute-start | bytes 393224 | tf_op jit(solution)/shard_map/ppermute | solution.py:24
  136.3 1.9 %collective-permute-start.22 = (f32[2,32,512]{2,1,0:T(8,128)S(1)}, f32[2,32,512]{2,1,0:T(8,128)S(1)}, u32[]{:S(2)}, u32[]{:S(2)}) collective-permute-start(f32[2,32,512]{2,1,0:T(8,128)S(1)} %get-tuple-element.43), channel_id=1, source_target_pairs={{0,0},{4,4},{8,24},{12,28},{1,13},{5,1},{9,21},{13,25},{2,10},{6,1... | collective-permute-start | bytes 393224 | tf_op jit(solution)/shard_map/ppermute | solution.py:24
  138.3 2.1 %collective-permute-done.21 = f32[2,32,512]{2,1,0:T(8,128)S(1)} collective-permute-done((f32[2,32,512]{2,1,0:T(8,128)S(1)}, f32[2,32,512]{2,1,0:T(8,128)S(1)}, u32[]{:S(2)}, u32[]{:S(2)}) %collective-permute-start.21) | collective-permute-done | bytes 131104 | tf_op jit(solution)/shard_map/ppermute | solution.py:24
  140.4 3.7 %collective-permute-done.22 = f32[2,32,512]{2,1,0:T(8,128)S(1)} collective-permute-done((f32[2,32,512]{2,1,0:T(8,128)S(1)}, f32[2,32,512]{2,1,0:T(8,128)S(1)}, u32[]{:S(2)}, u32[]{:S(2)}) %collective-permute-start.22) | collective-permute-done | bytes 131104 | tf_op jit(solution)/shard_map/ppermute | solution.py:24
  144.1 0.8 select_bitcast_fusion.1
  (46 shorter events, 0.8 us)
Async XLA Ops:
  0.8 1.3 copy-start.7
  0.8 1.4 copy-start.8
  2.4 2.9 %copy-start.9 = (f32[2,2,32,512]{3,2,1,0:T(8,128)S(1)}, f32[2,2,32,512]{3,2,1,0:T(8,128)}, u32[]{:S(2)}) copy-start(f32[2,2,32,512]{3,2,1,0:T(8,128)} %param.4) | copy-start | bytes 786436
  3.2 10.5 %collective-permute-start.1 = (f32[3,2,32,512]{3,2,1,0:T(8,128)}, f32[3,2,32,512]{3,2,1,0:T(8,128)S(1)}, u32[]{:S(2)}, u32[]{:S(2)}) collective-permute-start(f32[3,2,32,512]{3,2,1,0:T(8,128)} %pad_maximum_fusion.7), channel_id=1, source_target_pairs={{0,8},{4,12},{8,0},{12,4},{1,9},{5,13},{9,1},{13,5},{2,10},{6,14},... | collective-permute-start | bytes 1179656 | tf_op jit(solution)/shard_map/ppermute | solution.py:24
  5.4 13.6 %collective-permute-start.2 = (f32[4,2,32,512]{3,2,1,0:T(8,128)S(1)}, f32[4,2,32,512]{3,2,1,0:T(8,128)S(1)}, u32[]{:S(2)}, u32[]{:S(2)}) collective-permute-start(f32[4,2,32,512]{3,2,1,0:T(8,128)S(1)} %pad_maximum_fusion.2), channel_id=1, source_target_pairs={{0,12},{4,0},{8,4},{12,8},{1,13},{5,1},{9,5},{13,9},{2,14},{6,2},{... | collective-permute-start | bytes 1572872 | tf_op jit(solution)/shard_map/ppermute | solution.py:24
  10.0 9.0 %collective-permute-start = (f32[3,2,32,512]{3,2,1,0:T(8,128)}, f32[3,2,32,512]{3,2,1,0:T(8,128)S(1)}, u32[]{:S(2)}, u32[]{:S(2)}) collective-permute-start(f32[3,2,32,512]{3,2,1,0:T(8,128)} %pad_maximum_fusion.6), channel_id=1, source_target_pairs={{0,4},{4,8},{8,12},{12,0},{1,5},{5,9},{9,13},{13,1},{2,6},{6,10},{... | collective-permute-start | bytes 1179656 | tf_op jit(solution)/shard_map/ppermute | solution.py:24
  19.0 0.8 copy-start
  20.0 16.8 %collective-permute-start.3 = (f32[2,4,2,32,512]{4,3,2,1,0:T(8,128)S(1)}, f32[2,4,2,32,512]{4,3,2,1,0:T(8,128)S(1)}, u32[]{:S(2)}, u32[]{:S(2)}) collective-permute-start(f32[2,4,2,32,512]{4,3,2,1,0:T(8,128)S(1)} %pad_maximum_fusion), channel_id=1, source_target_pairs={{0,1},{4,5},{8,9},{12,13},{1,2},{5,6},{9,10},{13,14},{2,3},{6,7},{... | collective-permute-start | bytes 3145736 | tf_op jit(solution)/shard_map/ppermute | solution.py:24
  23.2 16.1 %collective-permute-start.4 = (f32[2,4,2,32,512]{4,3,2,1,0:T(8,128)S(1)}, f32[2,4,2,32,512]{4,3,2,1,0:T(8,128)S(1)}, u32[]{:S(2)}, u32[]{:S(2)}) collective-permute-start(f32[2,4,2,32,512]{4,3,2,1,0:T(8,128)S(1)} %pad_maximum_fusion), channel_id=1, source_target_pairs={{0,3},{4,7},{8,11},{12,15},{1,0},{5,4},{9,8},{13,12},{2,1},{6,5},{... | collective-permute-start | bytes 3145736 | tf_op jit(solution)/shard_map/ppermute | solution.py:24
  26.6 10.3 %collective-permute-start.5 = (f32[2,32,512]{2,1,0:T(8,128)S(1)}, f32[2,32,512]{2,1,0:T(8,128)S(1)}, u32[]{:S(2)}, u32[]{:S(2)}) collective-permute-start(f32[2,32,512]{2,1,0:T(8,128)S(1)} %get-tuple-element.15), channel_id=1, source_target_pairs={{0,496},{4,500},{8,504},{12,508},{1,497},{5,501},{9,505},{13,509},... | collective-permute-start | bytes 393224 | tf_op jit(solution)/shard_map/ppermute | solution.py:24
  36.9 12.9 %copy-start.1 = (f32[3,2,32,512]{3,2,1,0:T(8,128)S(1)}, f32[3,2,32,512]{3,2,1,0:T(8,128)}, u32[]{:S(2)}) copy-start(f32[3,2,32,512]{3,2,1,0:T(8,128)} %copy-done) | copy-start | bytes 1179652
  36.9 2.4 %copy-start.11 = (f32[2,32,512]{2,1,0:T(8,128)}, f32[2,32,512]{2,1,0:T(8,128)S(1)}, u32[]{:S(2)}) copy-start(f32[2,32,512]{2,1,0:T(8,128)S(1)} %collective-permute-done.5) | copy-start | bytes 393220
  36.9 11.3 %collective-permute-start.6 = (f32[4,2,32,512]{3,2,1,0:T(8,128)S(1)}, f32[4,2,32,512]{3,2,1,0:T(8,128)S(1)}, u32[]{:S(2)}, u32[]{:S(2)}) collective-permute-start(f32[4,2,32,512]{3,2,1,0:T(8,128)S(1)} %slice_bitcast_fusion.3), channel_id=1, source_target_pairs={{0,1},{4,5},{8,9},{12,13},{1,2},{5,6},{9,10},{13,14},{2,3},{6,7},{... | collective-permute-start | bytes 1572872 | tf_op jit(solution)/shard_map/ppermute | solution.py:24
  39.4 10.4 %collective-permute-start.7 = (f32[4,2,32,512]{3,2,1,0:T(8,128)S(1)}, f32[4,2,32,512]{3,2,1,0:T(8,128)S(1)}, u32[]{:S(2)}, u32[]{:S(2)}) collective-permute-start(f32[4,2,32,512]{3,2,1,0:T(8,128)S(1)} %slice_bitcast_fusion.2), channel_id=1, source_target_pairs={{0,3},{4,7},{8,11},{12,15},{1,0},{5,4},{9,8},{13,12},{2,1},{6,5},{... | collective-permute-start | bytes 1572872 | tf_op jit(solution)/shard_map/ppermute | solution.py:24
  48.2 4.9 %copy-start.3 = (f32[4,2,32,512]{3,2,1,0:T(8,128)}, f32[4,2,32,512]{3,2,1,0:T(8,128)S(1)}, u32[]{:S(2)}) copy-start(f32[4,2,32,512]{3,2,1,0:T(8,128)S(1)} %collective-permute-done.6.refs_6_) | copy-start | bytes 1572868
  49.8 3.4 %copy-start.5 = (f32[4,2,32,512]{3,2,1,0:T(8,128)}, f32[4,2,32,512]{3,2,1,0:T(8,128)S(1)}, u32[]{:S(2)}) copy-start(f32[4,2,32,512]{3,2,1,0:T(8,128)S(1)} %collective-permute-done.7.refs_7_) | copy-start | bytes 1572868
  53.1 17.2 %collective-permute-start.8 = (f32[4,2,32,512]{3,2,1,0:T(8,128)}, f32[4,2,32,512]{3,2,1,0:T(8,128)}, u32[]{:S(2)}, u32[]{:S(2)}) collective-permute-start(f32[4,2,32,512]{3,2,1,0:T(8,128)} %first_level.1), channel_id=1, source_target_pairs={{0,12},{4,8},{8,4},{12,0},{1,13},{5,9},{9,5},{13,1},{2,14},{6,10},... | collective-permute-start | bytes 1572872 | tf_op jit(solution)/shard_map/ppermute | solution.py:24
  56.2 16.1 %collective-permute-start.10 = (f32[4,2,32,512]{3,2,1,0:T(8,128)}, f32[4,2,32,512]{3,2,1,0:T(8,128)}, u32[]{:S(2)}, u32[]{:S(2)}) collective-permute-start(f32[4,2,32,512]{3,2,1,0:T(8,128)} %first_level.1), channel_id=1, source_target_pairs={{4,12},{12,4},{5,13},{13,5},{6,14},{14,6},{7,15},{15,7},{17,19},{1... | collective-permute-start | bytes 1572872 | tf_op jit(solution)/shard_map/ppermute | solution.py:24
  57.7 16.1 %collective-permute-start.9 = (f32[4,2,32,512]{3,2,1,0:T(8,128)}, f32[4,2,32,512]{3,2,1,0:T(8,128)}, u32[]{:S(2)}, u32[]{:S(2)}) collective-permute-start(f32[4,2,32,512]{3,2,1,0:T(8,128)} %first_level.1), channel_id=1, source_target_pairs={{4,0},{12,8},{5,1},{13,9},{6,2},{14,10},{7,3},{15,11},{17,16},{19,... | collective-permute-start | bytes 1572872 | tf_op jit(solution)/shard_map/ppermute | solution.py:24
  60.0 15.5 %collective-permute-start.11 = (f32[2,32,512]{2,1,0:T(8,128)S(1)}, f32[2,32,512]{2,1,0:T(8,128)S(1)}, u32[]{:S(2)}, u32[]{:S(2)}) collective-permute-start(f32[2,32,512]{2,1,0:T(8,128)S(1)} %get-tuple-element.38), channel_id=1, source_target_pairs={{0,4},{4,8},{8,12},{12,0},{1,5},{5,9},{9,13},{13,1},{2,6},{6,10},{... | collective-permute-start | bytes 393224 | tf_op jit(solution)/shard_map/ppermute | solution.py:24
  66.1 9.4 %collective-permute-start.12 = (f32[2,32,512]{2,1,0:T(8,128)S(1)}, f32[2,32,512]{2,1,0:T(8,128)S(1)}, u32[]{:S(2)}, u32[]{:S(2)}) collective-permute-start(f32[2,32,512]{2,1,0:T(8,128)S(1)} %get-tuple-element.37), channel_id=1, source_target_pairs={{0,8},{4,12},{8,0},{12,4},{1,9},{5,13},{9,1},{13,5},{2,10},{6,14},... | collective-permute-start | bytes 393224 | tf_op jit(solution)/shard_map/ppermute | solution.py:24
  70.4 6.3 %collective-permute-start.13 = (f32[2,32,512]{2,1,0:T(8,128)S(1)}, f32[2,32,512]{2,1,0:T(8,128)S(1)}, u32[]{:S(2)}, u32[]{:S(2)}) collective-permute-start(f32[2,32,512]{2,1,0:T(8,128)S(1)} %get-tuple-element.36), channel_id=1, source_target_pairs={{0,12},{4,0},{8,4},{12,8},{1,13},{5,1},{9,5},{13,9},{2,14},{6,2},{... | collective-permute-start | bytes 393224 | tf_op jit(solution)/shard_map/ppermute | solution.py:24
  76.6 6.8 %copy-start.2 = (f32[3,2,32,512]{3,2,1,0:T(8,128)S(1)}, f32[3,2,32,512]{3,2,1,0:T(8,128)}, u32[]{:S(2)}) copy-start(f32[3,2,32,512]{3,2,1,0:T(8,128)} %copy-done) | copy-start | bytes 1179652
  76.6 6.8 %copy-start.4 = (f32[4,2,32,512]{3,2,1,0:T(8,128)S(1)}, f32[4,2,32,512]{3,2,1,0:T(8,128)}, u32[]{:S(2)}) copy-start(f32[4,2,32,512]{3,2,1,0:T(8,128)} %copy-done.3) | copy-start | bytes 1572868
  76.6 6.8 %copy-start.6 = (f32[4,2,32,512]{3,2,1,0:T(8,128)S(1)}, f32[4,2,32,512]{3,2,1,0:T(8,128)}, u32[]{:S(2)}) copy-start(f32[4,2,32,512]{3,2,1,0:T(8,128)} %copy-done.5) | copy-start | bytes 1572868
  76.7 17.0 %collective-permute-start.15 = (f32[2,4,2,32,512]{4,3,2,1,0:T(8,128)S(1)}, f32[2,4,2,32,512]{4,3,2,1,0:T(8,128)S(1)}, u32[]{:S(2)}, u32[]{:S(2)}) collective-permute-start(f32[2,4,2,32,512]{4,3,2,1,0:T(8,128)S(1)} %pad_maximum_fusion.1.refs_2_), channel_id=1, source_target_pairs={{0,1},{4,5},{8,9},{12,13},{1,2},{5,6},{9,10},{13,14},{2,3},{6,7},{... | collective-permute-start | bytes 3145736 | tf_op jit(solution)/shard_map/ppermute | solution.py:24
  79.0 16.7 %collective-permute-start.16 = (f32[2,4,2,32,512]{4,3,2,1,0:T(8,128)S(1)}, f32[2,4,2,32,512]{4,3,2,1,0:T(8,128)S(1)}, u32[]{:S(2)}, u32[]{:S(2)}) collective-permute-start(f32[2,4,2,32,512]{4,3,2,1,0:T(8,128)S(1)} %pad_maximum_fusion.1.refs_2_), channel_id=1, source_target_pairs={{0,3},{4,7},{8,11},{12,15},{1,0},{5,4},{9,8},{13,12},{2,1},{6,5},{... | collective-permute-start | bytes 3145736 | tf_op jit(solution)/shard_map/ppermute | solution.py:24
  86.0 14.8 %collective-permute-start.14 = (f32[4,2,32,512]{3,2,1,0:T(8,128)S(1)}, f32[4,2,32,512]{3,2,1,0:T(8,128)S(1)}, u32[]{:S(2)}, u32[]{:S(2)}) collective-permute-start(f32[4,2,32,512]{3,2,1,0:T(8,128)S(1)} %first_level_side.1.refs_0_), channel_id=1, source_target_pairs={{4,0},{12,8},{5,1},{13,9},{6,2},{14,10},{7,3},{15,11},{17,16},{19,... | collective-permute-start | bytes 1572872 | tf_op jit(solution)/shard_map/ppermute | solution.py:24
  93.7 11.1 %collective-permute-start.17 = (f32[4,2,32,512]{3,2,1,0:T(8,128)S(1)}, f32[4,2,32,512]{3,2,1,0:T(8,128)S(1)}, u32[]{:S(2)}, u32[]{:S(2)}) collective-permute-start(f32[4,2,32,512]{3,2,1,0:T(8,128)S(1)} %slice_bitcast_fusion.1), channel_id=1, source_target_pairs={{0,1},{4,5},{8,9},{12,13},{1,2},{5,6},{9,10},{13,14},{2,3},{6,7},{... | collective-permute-start | bytes 1572872 | tf_op jit(solution)/shard_map/ppermute | solution.py:24
  95.7 13.3 %collective-permute-start.18 = (f32[4,2,32,512]{3,2,1,0:T(8,128)S(1)}, f32[4,2,32,512]{3,2,1,0:T(8,128)S(1)}, u32[]{:S(2)}, u32[]{:S(2)}) collective-permute-start(f32[4,2,32,512]{3,2,1,0:T(8,128)S(1)} %slice_bitcast_fusion), channel_id=1, source_target_pairs={{0,3},{4,7},{8,11},{12,15},{1,0},{5,4},{9,8},{13,12},{2,1},{6,5},{... | collective-permute-start | bytes 1572872 | tf_op jit(solution)/shard_map/ppermute | solution.py:24
  113.9 30.2 %copy-start.10 = (f32[2,2,32,512]{3,2,1,0:T(8,128)S(1)}, f32[2,2,32,512]{3,2,1,0:T(8,128)}, u32[]{:S(2)}) copy-start(f32[2,2,32,512]{3,2,1,0:T(8,128)} %param.4) | copy-start | bytes 786436
  113.9 24.4 %collective-permute-start.19 = (f32[2,32,512]{2,1,0:T(8,128)S(1)}, f32[2,32,512]{2,1,0:T(8,128)S(1)}, u32[]{:S(2)}, u32[]{:S(2)}) collective-permute-start(f32[2,32,512]{2,1,0:T(8,128)S(1)} %get-tuple-element.46), channel_id=1, source_target_pairs={{0,12},{4,0},{8,20},{12,24},{1,9},{5,13},{9,17},{13,21},{2,6},{6,1... | collective-permute-start | bytes 393224 | tf_op jit(solution)/shard_map/ppermute | solution.py:24
  129.0 9.3 %collective-permute-start.20 = (f32[2,32,512]{2,1,0:T(8,128)S(1)}, f32[2,32,512]{2,1,0:T(8,128)S(1)}, u32[]{:S(2)}, u32[]{:S(2)}) collective-permute-start(f32[2,32,512]{2,1,0:T(8,128)S(1)} %get-tuple-element.45), channel_id=1, source_target_pairs={{0,8},{4,12},{8,16},{12,20},{1,5},{5,9},{9,29},{13,17},{2,2},{6,6}... | collective-permute-start | bytes 393224 | tf_op jit(solution)/shard_map/ppermute | solution.py:24
  134.4 6.0 %collective-permute-start.21 = (f32[2,32,512]{2,1,0:T(8,128)S(1)}, f32[2,32,512]{2,1,0:T(8,128)S(1)}, u32[]{:S(2)}, u32[]{:S(2)}) collective-permute-start(f32[2,32,512]{2,1,0:T(8,128)S(1)} %get-tuple-element.44), channel_id=1, source_target_pairs={{0,4},{4,8},{8,28},{12,16},{1,1},{5,5},{9,25},{13,29},{2,14},{6,2}... | collective-permute-start | bytes 393224 | tf_op jit(solution)/shard_map/ppermute | solution.py:24
  136.3 7.8 %collective-permute-start.22 = (f32[2,32,512]{2,1,0:T(8,128)S(1)}, f32[2,32,512]{2,1,0:T(8,128)S(1)}, u32[]{:S(2)}, u32[]{:S(2)}) collective-permute-start(f32[2,32,512]{2,1,0:T(8,128)S(1)} %get-tuple-element.43), channel_id=1, source_target_pairs={{0,0},{4,4},{8,24},{12,28},{1,13},{5,1},{9,21},{13,25},{2,10},{6,1... | collective-permute-start | bytes 393224 | tf_op jit(solution)/shard_map/ppermute | solution.py:24
